TPU v7x, 128 devices: a whole 4x4x4 slice. The times are simulated.
128 devices in a mesh: dp: 8 (over z_lo, y), ctx: 16 (over z_hi, x, core).
Axes of the slice: x: 4, y: 4, z: 4 (z_hi: 2, z_lo: 2; z = z_hi * 2 + z_lo), core: 2. Of those that a mesh axis runs over, the one named last changes fastest.
Arguments:
- tokens: bfloat16 [16, 1024, 1536], P('dp', 'ctx'), may hold values from -6 to 6
- doc_start: int32 [16, 1024], P('dp'), may hold values from 0 to 1, as said below
- gain_attn: bfloat16 [1536], P(('dp', 'ctx')), may hold values from 0.5 to 1.5
- w_query: bfloat16 [1536, 1536], P(('dp', 'ctx')), may hold values from -0.15625 to 0.15625
- w_key: bfloat16 [1536, 1536], P(('dp', 'ctx')), may hold values from -0.15625 to 0.15625
- w_value: bfloat16 [1536, 1536], P(('dp', 'ctx')), may hold values from -0.15625 to 0.15625
- w_path: bfloat16 [1536, 1536], P(('dp', 'ctx')), may hold values from -0.15625 to 0.15625
- conv_path: bfloat16 [4, 1536], P(None, ('dp', 'ctx')), may hold values from -3 to 3
- w_beta: bfloat16 [1536, 12], P(('dp', 'ctx')), may hold values from -0.15625 to 0.15625
- w_out: bfloat16 [1536, 1536], P(('dp', 'ctx')), may hold values from -0.625 to 0.625
- gain_ffn: bfloat16 [1536], P(('dp', 'ctx')), may hold values from 0.5 to 1.5
- w_gate: bfloat16 [1536, 4096], P(('dp', 'ctx')), may hold values from -0.15625 to 0.15625
- w_up: bfloat16 [1536, 4096], P(('dp', 'ctx')), may hold values from -0.15625 to 0.15625
- w_down: bfloat16 [4096, 1536], P(('dp', 'ctx')), may hold values from -0.09375 to 0.09375
- grad_out: bfloat16 [16, 1024, 1536], P('dp', 'ctx'), may hold values from -6 to 6
Outputs:
- output: bfloat16 [16, 1024, 1536], P('dp', 'ctx')
- d_tokens: bfloat16 [16, 1024, 1536], P('dp', 'ctx')
- d_gain_attn: float32 [1536], P(('dp', 'ctx'))
- d_w_query: float32 [1536, 1536], P(('dp', 'ctx'))
- d_w_key: float32 [1536, 1536], P(('dp', 'ctx'))
- d_w_value: float32 [1536, 1536], P(('dp', 'ctx'))
- d_w_path: float32 [1536, 1536], P(('dp', 'ctx'))
- d_conv_path: float32 [4, 1536], P(None, ('dp', 'ctx'))
- d_w_beta: float32 [1536, 12], P(('dp', 'ctx'))
- d_w_out: float32 [1536, 1536], P(('dp', 'ctx'))
- d_gain_ffn: float32 [1536], P(('dp', 'ctx'))
- d_w_gate: float32 [1536, 4096], P(('dp', 'ctx'))
- d_w_up: float32 [1536, 4096], P(('dp', 'ctx'))
- d_w_down: float32 [4096, 1536], P(('dp', 'ctx'))
Inputs may be any that keep to these rules, and one draw needn't show every extreme that they name: `doc_start`: position 0 of every row is 1. Of the 2 rows held by each index of dp, one has a document that begins within the first 64 positions and ends within the last 64.
All inputs are finite; a program needn't handle non-finite values.
Results may differ from a plain program's by a relative error of at most 0.025.
Values may be sent and summed in bfloat16 or wider, within the bound.
A program may use at most 384 MiB of HBM per device.

v0:
```python
import jax
import jax.numpy as jnp
from jax import lax
from jax.sharding import PartitionSpec as P

PRECISE = lax.Precision.HIGHEST
EPS_NORM = 1e-05
EPS_UNIT = 1e-06


def shifted(block, axis, distance):
    devices = range(lax.axis_size(axis))
    route = [(i - distance, i) for i in devices if i - distance in devices]
    return lax.ppermute(block, axis, route)


def in_one_piece(arrays, axis, dim, along):
    widths = [a.shape[along] for a in arrays]
    both = jnp.concatenate(arrays, axis=along)
    whole = lax.all_gather(both, axis, axis=dim, tiled=True)
    return tuple(jnp.split(whole, [sum(widths[:k]) for k in range(1, len(widths))], axis=along))


def gather_turned(arrays, axis, dims):
    turned = [jnp.moveaxis(a, dim, 0) for a, dim in zip(arrays, dims)]
    widths = [t[0].size for t in turned]
    both = jnp.concatenate([t.reshape(-1, w) for t, w in zip(turned, widths)], axis=1)
    whole = lax.all_gather(both, axis, axis=0, tiled=True)
    parts = jnp.split(whole, [sum(widths[:k]) for k in range(1, len(widths))], axis=1)
    return tuple(
        (
            jnp.moveaxis(b.reshape(-1, *t.shape[1:]), 0, dim)
            for b, t, dim in zip(parts, turned, dims)
        )
    )


def in_one_piece_2(arrays, axis, dim, along):
    columns = [a.reshape(*a.shape[:along], -1) for a in arrays]
    both = jnp.concatenate(columns, axis=along)
    whole, at, outs = (lax.all_gather(both, axis, axis=dim, tiled=True), 0, [])
    for a, column in zip(arrays, columns):
        piece = whole[..., at : at + column.shape[along]]
        outs.append(piece.reshape(*piece.shape[:along], *a.shape[along:]))
        at += column.shape[along]
    return tuple(outs)


def rms_scale(values, gain_vec):
    return (
        values * lax.rsqrt(jnp.mean(values * values, axis=-1, keepdims=True) + EPS_NORM) * gain_vec
    )


def times_t(left_rows, right_rows):
    return lax.dot_general(
        left_rows, right_rows, (((1,), (1,)), ((), ())), preferred_element_type=jnp.float32
    )


def grad_of(left_rows, right_rows):
    return lax.dot_general(
        left_rows, right_rows, (((0,), (0,)), ((), ())), preferred_element_type=jnp.float32
    )


def to_heads(flat_rows, head_count):
    return flat_rows.reshape(flat_rows.shape[0], head_count, -1).transpose(1, 0, 2)


def from_heads(per_head):
    return per_head.transpose(1, 0, 2).reshape(per_head.shape[1], -1)


def half_products(query_b, key_b, vector_b):
    inner_ww = jnp.einsum("hsd,htd->hst", vector_b, vector_b, preferred_element_type=jnp.float32)
    inner_wk = jnp.einsum("hsd,hjd->hsj", vector_b, key_b, preferred_element_type=jnp.float32)
    inner_qw = jnp.einsum("hid,hsd->his", query_b, vector_b, preferred_element_type=jnp.float32)
    direct = jnp.einsum("hid,hjd->hij", query_b, key_b, preferred_element_type=jnp.float32)
    return (inner_ww, inner_wk, inner_qw, direct)


def products_back(grads, queries, key_rows, vectors):
    d_ww, d_wk, d_qw, d_direct = grads
    d_query = jnp.einsum("his,hsd->hid", d_qw, vectors, precision=PRECISE) + jnp.einsum(
        "hij,hjd->hid", d_direct, key_rows, precision=PRECISE
    )
    d_key = jnp.einsum("hsj,hsd->hjd", d_wk, vectors, precision=PRECISE) + jnp.einsum(
        "hij,hid->hjd", d_direct, queries, precision=PRECISE
    )
    d_vec = jnp.einsum("hst,htd->hsd", d_ww, vectors, precision=PRECISE) + jnp.einsum(
        "hst,hsd->htd", d_ww, vectors, precision=PRECISE
    )
    d_vec = (
        d_vec
        + jnp.einsum("hsj,hjd->hsd", d_wk, key_rows, precision=PRECISE)
        + jnp.einsum("his,hid->hsd", d_qw, queries, precision=PRECISE)
    )
    return (d_query, d_key, d_vec)


def own_block(queries, key_rows, vectors, beta_vals, inner_ww, inner_wk, inner_qw, direct):
    length = queries.shape[1]
    strict = jnp.tril(jnp.ones((length, length), bool), -1)
    closed = jnp.tril(jnp.ones((length, length), bool))
    system = jnp.eye(length, dtype=jnp.float32) + jnp.where(
        strict, inner_ww * beta_vals[:, None, :], 0.0
    )
    identity = jnp.broadcast_to(jnp.eye(length, dtype=jnp.float32), system.shape)
    inverse = jax.scipy.linalg.solve_triangular(system, identity, lower=True, unit_diagonal=True)
    masked_wk = jnp.where(strict, inner_wk, 0.0)
    coeffs = jnp.einsum("hst,htj->hsj", inverse, masked_wk, precision=PRECISE)
    masked_qw = jnp.where(closed, inner_qw, 0.0) * beta_vals[:, None, :]
    scores = direct - jnp.einsum("his,hsj->hij", masked_qw, coeffs, precision=PRECISE)
    mover_mat = jnp.einsum("his,hst->hit", masked_qw, inverse, precision=PRECISE)
    query_moved = queries - jnp.einsum("hit,htd->hid", mover_mat, vectors, precision=PRECISE)
    key_moved = key_rows - jnp.einsum(
        "hsj,hsd->hjd", coeffs, beta_vals[:, :, None] * vectors, precision=PRECISE
    )
    return (scores, query_moved, key_moved, inverse)


def transport(moving, vectors, beta_vals, inverse):
    inner_wm = jnp.einsum("hsd,hnd->hsn", vectors, moving, precision=PRECISE)
    solved = jnp.einsum("hst,htn->hsn", inverse, inner_wm, precision=PRECISE)
    return moving - jnp.einsum(
        "hsn,hsd->hnd", solved, beta_vals[:, :, None] * vectors, precision=PRECISE
    )


def path_vectors(current, rim_rows, conv_w, same_doc, head_count):
    rim_width = rim_rows.shape[0]
    length = current.shape[0]
    extended = jnp.concatenate([rim_rows, current], axis=0)
    conved = conv_w[0] * current
    for tap_index in range(1, rim_width + 1):
        earlier = extended[rim_width - tap_index : rim_width - tap_index + length]
        conved = conved + conv_w[tap_index] * jnp.where(same_doc[tap_index][:, None], earlier, 0.0)
    per_head = conved.reshape(length, head_count, -1)
    unit_rows = per_head * lax.rsqrt(
        jnp.sum(per_head * per_head, axis=-1, keepdims=True) + EPS_UNIT
    )
    return unit_rows.transpose(1, 0, 2)


def run_batch(inputs, upstream, doc_row, attn_full, ffn_full):
    gain_attn, w_query, w_key, w_value, w_path, conv_path, w_beta, w_out = attn_full
    gain_ffn, w_gate, w_up, w_down = ffn_full
    head_count = w_beta.shape[1]
    length = inputs.shape[0]
    rim_width = conv_path.shape[0] - 1
    position = lax.axis_index("ctx")
    cycle_len = lax.axis_size("ctx")
    score_scale = (w_query.shape[1] // head_count) ** (-0.5)
    doc_here = lax.dynamic_slice_in_dim(doc_row, position * length, length)
    padded_docs = jnp.concatenate([jnp.full((rim_width,), -1, jnp.int32), doc_row])
    ext_docs = lax.dynamic_slice_in_dim(padded_docs, position * length, length + rim_width)
    same_doc = jnp.stack(
        [
            ext_docs[rim_width - tap_index : rim_width - tap_index + length] == doc_here
            for tap_index in range(rim_width + 1)
        ]
    )
    inputs_f = inputs.astype(jnp.float32)
    gain_attn_f = gain_attn.astype(jnp.float32)
    normed = rms_scale(inputs_f, gain_attn_f).astype(jnp.bfloat16)
    queries = jnp.dot(normed, w_query, preferred_element_type=jnp.float32).astype(jnp.bfloat16)
    key_rows = jnp.dot(normed, w_key, preferred_element_type=jnp.float32).astype(jnp.bfloat16)
    value_rows = jnp.dot(normed, w_value, preferred_element_type=jnp.float32).astype(jnp.bfloat16)
    path_raw = jnp.dot(normed, w_path, preferred_element_type=jnp.float32).astype(jnp.bfloat16)
    beta_raw = jnp.dot(normed, w_beta, preferred_element_type=jnp.float32)
    rim_rows = shifted(path_raw[length - rim_width :], "ctx", 1)

    def make_vectors(current, rim_in, conv_w):
        return path_vectors(current, rim_in, conv_w, same_doc, head_count)

    vectors_f, vectors_pull = jax.vjp(
        make_vectors,
        path_raw.astype(jnp.float32),
        rim_rows.astype(jnp.float32),
        conv_path.astype(jnp.float32),
    )
    vector_b = vectors_f.astype(jnp.bfloat16)
    vectors = vector_b.astype(jnp.float32)
    beta_vals = (2.0 * jax.nn.sigmoid(beta_raw)).T
    query_b = to_heads(queries, head_count)
    key_b = to_heads(key_rows, head_count)
    value_b = to_heads(value_rows, head_count)
    query_h = query_b.astype(jnp.float32)
    key_h = key_b.astype(jnp.float32)
    value_h = value_b.astype(jnp.float32)
    inner_ww, inner_wk, inner_qw, direct = half_products(query_b, key_b, vector_b)
    (scores_d, query_moved, key_moved, inverse), block_pull = jax.vjp(
        own_block, query_h, key_h, vectors, beta_vals, inner_ww, inner_wk, inner_qw, direct
    )
    causal = jnp.tril(jnp.ones((length, length), bool)) & (doc_here[:, None] == doc_here[None, :])
    diag_scores = jnp.where(causal, scores_d * score_scale, -jnp.inf)
    row_max = diag_scores.max(-1)
    diag_probs = jnp.exp(diag_scores - row_max[..., None])
    denominator = diag_probs.sum(-1)
    weighted = jnp.einsum("hij,hjd->hid", diag_probs, value_h, precision=PRECISE)

    def remote_visible(cycle_step):
        source = position - cycle_step
        key_docs = lax.dynamic_slice_in_dim(doc_row, jnp.maximum(source, 0) * length, length)
        return (source >= 0) & (doc_here[:, None] == key_docs[None, :])

    def advance(cycle_state, cycle_step):
        outgoing, carried, old_max, old_denom, old_weighted = cycle_state
        got_keys, got_values = shifted((outgoing, carried), "ctx", 1)
        visible = remote_visible(cycle_step)
        scores = jnp.einsum("hid,hjd->hij", query_moved, got_keys, precision=PRECISE) * score_scale
        scores = jnp.where(visible, scores, -jnp.inf)
        new_max = jnp.maximum(old_max, scores.max(-1))
        attn_probs = jnp.exp(scores - new_max[..., None])
        shrink = jnp.exp(old_max - new_max)
        new_denom = old_denom * shrink + attn_probs.sum(-1)
        new_weighted = old_weighted * shrink[..., None] + jnp.einsum(
            "hij,hjd->hid", attn_probs, got_values, precision=PRECISE
        )
        outgoing = transport(got_keys, vectors, beta_vals, inverse)
        return ((outgoing, got_values, new_max, new_denom, new_weighted), (got_keys, got_values))

    steps_list = jnp.arange(1, cycle_len, dtype=jnp.int32)
    cycle_end, kept_blocks = lax.scan(
        advance, (key_moved, value_h, row_max, denominator, weighted), steps_list
    )
    row_max, denominator, weighted = (cycle_end[2], cycle_end[3], cycle_end[4])
    attn_heads = weighted / denominator[..., None]
    log_sum = row_max + jnp.log(denominator)
    attended = from_heads(attn_heads).astype(jnp.bfloat16)
    hidden = inputs_f + jnp.dot(attended, w_out, preferred_element_type=jnp.float32)
    gain_ffn_f = gain_ffn.astype(jnp.float32)
    normed_ffn = rms_scale(hidden, gain_ffn_f).astype(jnp.bfloat16)
    gate_pre = jnp.dot(normed_ffn, w_gate, preferred_element_type=jnp.float32)
    up_pre = jnp.dot(normed_ffn, w_up, preferred_element_type=jnp.float32)

    def gate_up(gate_in, up_in):
        return jax.nn.silu(gate_in) * up_in

    activation_f, gate_pull = jax.vjp(gate_up, gate_pre, up_pre)
    activation = activation_f.astype(jnp.bfloat16)
    output_rows = (hidden + jnp.dot(activation, w_down, preferred_element_type=jnp.float32)).astype(
        jnp.bfloat16
    )
    d_activation = times_t(upstream, w_down)
    d_gate, d_up = gate_pull(d_activation)
    d_gate = d_gate.astype(jnp.bfloat16)
    d_up = d_up.astype(jnp.bfloat16)
    d_normed_ffn = times_t(d_gate, w_gate) + times_t(d_up, w_up)
    _, ffn_norm_pull = jax.vjp(rms_scale, hidden, gain_ffn_f)
    d_hidden, d_gain_ffn = ffn_norm_pull(d_normed_ffn)
    d_hidden = d_hidden + upstream.astype(jnp.float32)
    d_branch = d_hidden.astype(jnp.bfloat16)
    d_attn = to_heads(times_t(d_branch, w_out), head_count)
    row_dot = jnp.sum(d_attn * attn_heads, axis=-1)

    def retreat(cycle_state, step_inputs):
        carry_keys, carry_values, d_query, d_vectors, d_betas, d_inverse = cycle_state
        cycle_step, got_keys, got_values = step_inputs
        _, move_pull = jax.vjp(transport, got_keys, vectors, beta_vals, inverse)
        d_keys, d_vec_part, d_beta_part, d_inv_part = move_pull(carry_keys)
        visible = remote_visible(cycle_step)
        scores = jnp.einsum("hid,hjd->hij", query_moved, got_keys, precision=PRECISE) * score_scale
        attn_probs = jnp.where(visible, jnp.exp(scores - log_sum[..., None]), 0.0)
        d_probs = jnp.einsum("hid,hjd->hij", d_attn, got_values, precision=PRECISE)
        d_scores = attn_probs * (d_probs - row_dot[..., None]) * score_scale
        d_query = d_query + jnp.einsum("hij,hjd->hid", d_scores, got_keys, precision=PRECISE)
        d_keys = d_keys + jnp.einsum("hij,hid->hjd", d_scores, query_moved, precision=PRECISE)
        d_values = carry_values + jnp.einsum("hij,hid->hjd", attn_probs, d_attn, precision=PRECISE)
        back_keys, back_values = shifted((d_keys, d_values), "ctx", -1)
        return (
            (
                back_keys,
                back_values,
                d_query,
                d_vectors + d_vec_part,
                d_betas + d_beta_part,
                d_inverse + d_inv_part,
            ),
            None,
        )

    zeros_heads = jnp.zeros_like(query_moved)
    back_start = (
        zeros_heads,
        zeros_heads,
        zeros_heads,
        jnp.zeros_like(vectors),
        jnp.zeros_like(beta_vals),
        jnp.zeros_like(inverse),
    )
    cycle_back, _ = lax.scan(
        retreat, back_start, (steps_list, kept_blocks[0], kept_blocks[1]), reverse=True
    )
    back_keys, back_values, d_query, d_vectors, d_betas, d_inverse = cycle_back
    diag_probs = jnp.where(causal, jnp.exp(scores_d * score_scale - log_sum[..., None]), 0.0)
    d_probs = jnp.einsum("hid,hjd->hij", d_attn, value_h, precision=PRECISE)
    d_diag = diag_probs * (d_probs - row_dot[..., None]) * score_scale
    d_value_h = back_values + jnp.einsum("hij,hid->hjd", diag_probs, d_attn, precision=PRECISE)
    block_grads = block_pull((d_diag, d_query, back_keys, d_inverse))
    d_query_h, d_key_h, d_vec_own, d_beta_own = (
        block_grads[0],
        block_grads[1],
        block_grads[2],
        block_grads[3],
    )
    d_query_more, d_key_more, d_vec_more = products_back(block_grads[4:], query_h, key_h, vectors)
    d_query_h = d_query_h + d_query_more
    d_key_h = d_key_h + d_key_more
    d_vectors = d_vectors + d_vec_own + d_vec_more
    d_betas = d_betas + d_beta_own
    d_current, d_rim, d_conv = vectors_pull(d_vectors)
    rim_grads = shifted(d_rim, "ctx", -1)
    d_path = d_current.at[length - rim_width :].add(rim_grads).astype(jnp.bfloat16)
    d_beta_raw = (d_betas * beta_vals * (1.0 - 0.5 * beta_vals)).T.astype(jnp.bfloat16)
    d_query_flat = from_heads(d_query_h).astype(jnp.bfloat16)
    d_key_flat = from_heads(d_key_h).astype(jnp.bfloat16)
    d_value_flat = from_heads(d_value_h).astype(jnp.bfloat16)
    d_normed = (
        times_t(d_query_flat, w_query) + times_t(d_key_flat, w_key) + times_t(d_value_flat, w_value)
    )
    d_normed = d_normed + times_t(d_path, w_path) + times_t(d_beta_raw, w_beta)
    _, norm_pull = jax.vjp(rms_scale, inputs_f, gain_attn_f)
    d_inputs_f, d_gain_attn = norm_pull(d_normed)
    d_inputs = (d_inputs_f + d_hidden).astype(jnp.bfloat16)
    grad_pairs = (
        (normed, d_query_flat),
        (normed, d_key_flat),
        (normed, d_value_flat),
        (normed, d_path),
        (normed, d_beta_raw),
        (attended, d_branch),
        (normed_ffn, d_gate),
        (normed_ffn, d_up),
        (activation, upstream),
    )
    small_grads = (d_gain_attn, d_conv, d_gain_ffn)
    return (output_rows, d_inputs, grad_pairs, small_grads)


def split_features(rows, dp_count, cycle_count):
    return rows.reshape(
        rows.shape[0], dp_count, cycle_count, rows.shape[1] // (dp_count * cycle_count)
    )


def weight_grads(pair_lists, small_lists):
    dp_count = lax.axis_size("dp")
    cycle_count = lax.axis_size("ctx")
    lefts = [
        jnp.concatenate([grad_pairs[slot_index][0] for grad_pairs in pair_lists], axis=0)
        for slot_index in (0, 5, 6, 8)
    ]
    rights = [
        jnp.concatenate([grad_pairs[slot_index][1] for grad_pairs in pair_lists], axis=0)
        for slot_index in range(9)
    ]
    moved = (
        lax.all_to_all(
            split_features(lefts[0], dp_count, cycle_count),
            "ctx",
            split_axis=2,
            concat_axis=0,
            tiled=True,
        ),
        lax.all_to_all(
            split_features(lefts[1], dp_count, cycle_count),
            "ctx",
            split_axis=2,
            concat_axis=0,
            tiled=True,
        ),
        lax.all_to_all(
            split_features(lefts[2], dp_count, cycle_count),
            "ctx",
            split_axis=2,
            concat_axis=0,
            tiled=True,
        ),
        lax.all_to_all(
            split_features(lefts[3], dp_count, cycle_count),
            "ctx",
            split_axis=2,
            concat_axis=0,
            tiled=True,
        ),
    )
    owned = [piece.reshape(piece.shape[0], -1) for piece in moved]
    gathered = in_one_piece(
        (
            rights[0],
            rights[1],
            rights[2],
            rights[3],
            rights[4],
            rights[5],
            rights[6],
            rights[7],
            rights[8],
        ),
        "ctx",
        0,
        1,
    )
    left_of = (
        owned[0],
        owned[0],
        owned[0],
        owned[0],
        owned[0],
        owned[1],
        owned[2],
        owned[2],
        owned[3],
    )
    products = [grad_of(left_of[slot_index], gathered[slot_index]) for slot_index in range(9)]
    shares = (
        lax.psum_scatter(
            products[0].astype(jnp.bfloat16), "dp", scatter_dimension=0, tiled=True
        ).astype(jnp.float32),
        lax.psum_scatter(
            products[1].astype(jnp.bfloat16), "dp", scatter_dimension=0, tiled=True
        ).astype(jnp.float32),
        lax.psum_scatter(
            products[2].astype(jnp.bfloat16), "dp", scatter_dimension=0, tiled=True
        ).astype(jnp.float32),
        lax.psum_scatter(
            products[3].astype(jnp.bfloat16), "dp", scatter_dimension=0, tiled=True
        ).astype(jnp.float32),
        lax.psum_scatter(
            products[4].astype(jnp.bfloat16), "dp", scatter_dimension=0, tiled=True
        ).astype(jnp.float32),
        lax.psum_scatter(
            products[5].astype(jnp.bfloat16), "dp", scatter_dimension=0, tiled=True
        ).astype(jnp.float32),
        lax.psum_scatter(
            products[6].astype(jnp.bfloat16), "dp", scatter_dimension=0, tiled=True
        ).astype(jnp.float32),
        lax.psum_scatter(
            products[7].astype(jnp.bfloat16), "dp", scatter_dimension=0, tiled=True
        ).astype(jnp.float32),
        lax.psum_scatter(
            products[8].astype(jnp.bfloat16), "dp", scatter_dimension=0, tiled=True
        ).astype(jnp.float32),
    )
    summed = [
        jnp.stack([small_grads[slot_index] for small_grads in small_lists]).sum(0)
        for slot_index in range(3)
    ]
    small_shares = (
        lax.psum_scatter(summed[0], ("dp", "ctx"), scatter_dimension=0, tiled=True),
        lax.psum_scatter(summed[1], ("dp", "ctx"), scatter_dimension=1, tiled=True),
        lax.psum_scatter(summed[2], ("dp", "ctx"), scatter_dimension=0, tiled=True),
    )
    return (
        small_shares[0],
        shares[0],
        shares[1],
        shares[2],
        shares[3],
        small_shares[1],
        shares[4],
        shares[5],
        small_shares[2],
        shares[6],
        shares[7],
        shares[8],
    )


def per_device(
    tokens,
    doc_start,
    gain_attn,
    w_query,
    w_key,
    w_value,
    w_path,
    conv_path,
    w_beta,
    w_out,
    gain_ffn,
    w_gate,
    w_up,
    w_down,
    grad_out,
):
    micro_count = tokens.shape[0]
    doc_rows = jnp.cumsum(doc_start, axis=1)
    output_list = []
    d_list = []
    attn_full = gather_turned(
        (gain_attn, w_query, w_key, w_value, w_path, conv_path, w_beta, w_out),
        ("dp", "ctx"),
        (0, 0, 0, 0, 0, 1, 0, 0),
    )
    ffn_full = (
        *in_one_piece_2((gain_ffn, w_gate, w_up), ("dp", "ctx"), 0, 1),
        lax.all_gather(w_down, ("dp", "ctx"), axis=0, tiled=True),
    )
    attn_full, ffn_full = (attn_full, ffn_full)
    pair_lists = []
    small_lists = []
    for micro_index in range(micro_count):
        output_rows, d_inputs, grad_pairs, small_grads = run_batch(
            tokens[micro_index], grad_out[micro_index], doc_rows[micro_index], attn_full, ffn_full
        )
        output_list.append(output_rows)
        d_list.append(d_inputs)
        pair_lists.append(grad_pairs)
        small_lists.append(small_grads)
    totals = weight_grads(pair_lists, small_lists)
    return (jnp.stack(output_list), jnp.stack(d_list)) + totals


def solution(mesh):
    placed = (
        P("dp", "ctx", None),
        P("dp", None),
        P(("dp", "ctx")),
        P(("dp", "ctx"), None),
        P(("dp", "ctx"), None),
        P(("dp", "ctx"), None),
        P(("dp", "ctx"), None),
        P(None, ("dp", "ctx")),
        P(("dp", "ctx"), None),
        P(("dp", "ctx"), None),
        P(("dp", "ctx")),
        P(("dp", "ctx"), None),
        P(("dp", "ctx"), None),
        P(("dp", "ctx"), None),
        P("dp", "ctx", None),
    )
    return jax.shard_map(
        per_device,
        mesh=mesh,
        in_specs=placed,
        out_specs=(
            P("dp", "ctx", None),
            P("dp", "ctx", None),
            P(("dp", "ctx")),
            P(("dp", "ctx"), None),
            P(("dp", "ctx"), None),
            P(("dp", "ctx"), None),
            P(("dp", "ctx"), None),
            P(None, ("dp", "ctx")),
            P(("dp", "ctx"), None),
            P(("dp", "ctx"), None),
            P(("dp", "ctx")),
            P(("dp", "ctx"), None),
            P(("dp", "ctx"), None),
            P(("dp", "ctx"), None),
        ),
        check_vma=False,
    )
```

profile of v0, /device:TPU:1, one launch (start us, length us, event | category | flops | bytes accessed | tf_op | source)
XLA Modules:
  0.0 3233.0 jit_solution(550362187327187519)
XLA Ops:
  27.1 194.5 %all-gather.7.cloned.1.call-done = bf16[4096,1536]{1,0:T(8,128)(2,1)} async-done(((bf16[32,1536]{1,0:T(8,128)(2,1)}), bf16[4096,1536]{1,0:T(8,128)(2,1)}) %all-gather.7.cloned.1.call-update) | async-done | bytes 12582928 | tf_op jit(solution)/shard_map/all_gather | solution.py:500
  221.6 9.7 fusion.514
  236.2 222.1 %all-gather.11.cloned.1.call-done = bf16[128,12,7697]{2,1,0:T(8,128)(2,1)} async-done(((bf16[1,12,7697]{2,1,0:T(8,128)(2,1)}), bf16[128,12,7697]{2,1,0:T(8,128)(2,1)}) %all-gather.11.cloned.1.call-update) | async-done | bytes 23645200 | tf_op jit(solution)/shard_map/all_gather | solution.py:28
  458.3 35.2 %reshape.503 = bf16[1536,7697]{1,0:T(8,128)(2,1)} reshape(bf16[128,12,7697]{2,1,0:T(8,128)(2,1)} %all-gather.11.cloned.1.call-done) | data formatting | bytes 47290368
  544.6 59.7 %custom-call.16 = f32[12,1,64,64]{2,3,1,0:T(8,128)S(1)} custom-call(f32[12,1,64,64]{3,2,1,0:T(8,128)} %get-tuple-element.1666), custom_call_target="InvertDiagBlocksLowerTriangular" | custom-call | tf_op jit(solution)/shard_map/jvp(jit(_solve_triangular))/vmap()/triangular_solve | solution.py:110
  622.2 315.8 %while.96 = (s32[]{:T(128)}, f32[12,64,128]{2,1,0:T(8,128)}, f32[12,64,128]{2,1,0:T(8,128)}, f32[12,64]{1,0:T(8,128)}, f32[12,64]{1,0:T(8,128)S(1)}, /*index=5*/...) while((s32[]{:T(128)}, f32[12,64,128]{2,1,0:T(8,128)}, ...), condition=%wide.region_9.11_spmd, body=%wide.region_6.10_spmd.sunk | while | flops 340436480 | bytes 11071861 | solution.py:225
  807.0 7.9 collective-permute-start
  850.7 7.9 collective-permute-start
  872.5 7.9 collective-permute-start
  894.3 7.9 collective-permute-start
  916.2 7.9 collective-permute-start
  938.8 60.5 %custom-call.17 = f32[12,1,64,64]{2,3,1,0:T(8,128)} custom-call(f32[12,1,64,64]{3,2,1,0:T(8,128)} %get-tuple-element.1667), custom_call_target="InvertDiagBlocksLowerTriangular" | custom-call | tf_op jit(solution)/shard_map/jvp(jit(_solve_triangular))/vmap()/triangular_solve | solution.py:110
  1019.6 339.7 %while.97 = (s32[]{:T(128)}, f32[12,64,128]{2,1,0:T(8,128)}, f32[12,64,128]{2,1,0:T(8,128)}, f32[12,64]{1,0:T(8,128)}, f32[12,64]{1,0:T(8,128)}, /*index=5*/f32[...) while((s32[]{:T(128)}, f32[12,64,128]{2,1,0:T(8,128)}, ...), condition=%wide.region_18.20_spmd, body=%wide.region_15.19_spmd.sunk | while | flops 340436480 | bytes 11071861 | solution.py:225
  1019.6 7.9 collective-permute-start.2
  1042.8 7.9 collective-permute-start.2
  1065.9 7.9 collective-permute-start.2
  1372.7 36.1 %reshape.505 = bf16[1536,8193]{1,0:T(8,128)(2,1)} reshape(bf16[128,12,8193]{2,1,0:T(8,128)(2,1)} %all-gather.13.cloned.1.call-done) | data formatting | bytes 50337792
  1418.0 10.1 fusion.290
  1428.1 8.3 fusion.84
  1436.4 8.7 multiply_reduce_fusion.7
  1452.5 10.1 fusion.293
  1462.6 8.1 fusion.82
  1472.2 8.6 multiply_reduce_fusion.6
  1494.2 535.5 %while.98 = (s32[]{:T(128)}, f32[12,64,128]{2,1,0:T(8,128)S(1)}, f32[12,64,128]{2,1,0:T(8,128)}, f32[12,64,128]{2,1,0:T(8,128)}, f32[12,64,128]{2,1,0:T(8,128)},...) while((s32[]{:T(128)}, f32[12,64,128]{2,1,0:T(8,128)S(1)}, ...), condition=%wide.region_24.26_spmd.clone, body=%wide.region_22.25_spmd.clone.sunk | while | flops 869999360 | bytes 19705300 | solution.py:293
  2045.2 520.5 %while.99 = (s32[]{:T(128)}, f32[12,64,128]{2,1,0:T(8,128)S(1)}, f32[12,64,128]{2,1,0:T(8,128)}, f32[12,64,128]{2,1,0:T(8,128)}, f32[12,64,128]{2,1,0:T(8,128)},...) while((s32[]{:T(128)}, f32[12,64,128]{2,1,0:T(8,128)S(1)}, ...), condition=%wide.region_34.37_spmd.clone, body=%wide.region_32.36_spmd.clone.sunk | while | flops 869999360 | bytes 18722232 | solution.py:293
  2630.1 11.3 concatenate.82
  2651.1 30.4 all-to-all-start
  2699.6 8.5 all-to-all-done.1
  2776.4 266.5 %all-reduce.35 = (f32[1536]{0:T(1024)S(1)}, f32[4,1536]{1,0:T(4,128)S(1)}, f32[1536]{0:T(1024)S(1)}) all-reduce(f32[1536]{0:T(1024)S(1)} %reduce_sum.418, f32[4,1536]{1,0:T(4,128)S(1)} %copy-done.148, f32[1536]{0:T(1024)S(1)} %reduce_sum.439), channel_id=2, replica_groups=mesh['dp'=8,'ctx'=16] {'dp','ctx'}, use_global_device_ids=true, to_apply=%region_42.45.clone | all-reduce | flops 9216 | bytes 73728
  3052.7 11.1 fusion.113
  3063.8 11.2 fusion.110
  3100.2 55.5 %fusion.528 = (bf16[16,1536]{1,0:T(8,128)(2,1)S(1)}, bf16[16,1536]{1,0:T(8,128)(2,1)S(1)}, bf16[16,1536]{1,0:T(8,128)(2,1)S(1)}, bf16[16,1536]{1,0:T(8,128)(2,1)...) fusion(bf16[96,1536]{1,0:T(8,128)(2,1)} %fusion.159, ...), kind=kCustom, calls=%all-reduce-scatter.8 | all-reduce-scatter fusion | flops 2033153 | bytes 3558528
  (2003 shorter events, 2040.8 us)
Async XLA Ops:
  7.2 214.4 %all-gather.7.cloned.1.call-start = ((), (), s32[]{:S(2)}) async-start(), calls=%async_computation.5 | async-start | bytes 12681216 | tf_op jit(solution)/shard_map/all_gather | solution.py:500
  7.9 450.4 %all-gather.11.cloned.1.call-start = ((), (), s32[]{:S(2)}) async-start(), calls=%async_computation.8 | async-start | bytes 32231424 | tf_op jit(solution)/shard_map/all_gather | solution.py:28
  11.3 1361.3 %all-gather.13.cloned.1.call-start = ((), (), s32[]{:S(2)}) async-start(), calls=%async_computation.9 | async-start | bytes 34344960 | tf_op jit(solution)/shard_map/all_gather | solution.py:41
  14.1 3038.6 %all-gather.9.cloned.1.call-start = ((), (), s32[]{:S(2)}) async-start(), calls=%async_computation.6 | async-start | bytes 76316672 | tf_op jit(solution)/shard_map/all_gather | solution.py:20
  1507.4 21.8 collective-permute-start.4
  1543.2 21.6 collective-permute-start.4
  1578.9 21.6 collective-permute-start.4
  1614.5 21.6 collective-permute-start.4
  1650.2 21.6 collective-permute-start.4
  1685.8 21.6 collective-permute-start.4
  1721.5 21.6 collective-permute-start.4
  1757.1 21.6 collective-permute-start.4
  1792.8 21.6 collective-permute-start.4
  1828.4 21.6 collective-permute-start.4
  1864.1 21.6 collective-permute-start.4
  1899.7 21.6 collective-permute-start.4
  1935.4 21.6 collective-permute-start.4
  1971.0 21.6 collective-permute-start.4
  2006.7 21.6 collective-permute-start.4
  2126.5 21.5 collective-permute-start.6
  2404.2 21.5 collective-permute-start.6
  2473.6 21.5 collective-permute-start.6
  2543.1 21.5 collective-permute-start.6
  2651.1 40.3 %all-to-all-start = ((bf16[128,8,16,12]{0,1,3,2:T(8,128)(2,1)}), bf16[128,8,16,12]{0,1,3,2:T(8,128)(2,1)}, u32[]{:S(2)}, u32[]{:S(2)}) async-start(bf16[128,8,16,12]{0,1,3,2:T(8,128)(2,1)} %copy.483), calls=%async_computation | async-start | bytes 786432 | tf_op jit(solution)/shard_map/all_to_all | solution.py:360
  2718.1 49.9 %all-to-all-start.2 = ((bf16[128,8,16,12]{0,1,3,2:T(8,128)(2,1)}), bf16[128,8,16,12]{0,1,3,2:T(8,128)(2,1)}, u32[]{:S(2)}, u32[]{:S(2)}) async-start(bf16[128,8,16,12]{0,1,3,2:T(8,128)(2,1)} %copy.491), calls=%async_computation.2 | async-start | bytes 786432 | tf_op jit(solution)/shard_map/all_to_all | solution.py:374
  2767.9 280.1 %all-to-all-start.3 = ((bf16[128,8,16,32]{0,3,1,2:T(8,128)(2,1)}), bf16[128,8,16,32]{0,3,1,2:T(8,128)(2,1)S(1)}, u32[]{:S(2)}, u32[]{:S(2)}) async-start(bf16[128,8,16,32]{0,3,1,2:T(8,128)(2,1)} %copy.494), calls=%async_computation.3 | async-start | bytes 2097152 | tf_op jit(solution)/shard_map/all_to_all | solution.py:381
  2775.0 449.7 %reduce-scatter.19.cloned.1.call-start = ((), (), s32[]{:S(2)}) async-start(), calls=%async_computation.7 | async-start | bytes 884736 | tf_op jit(solution)/shard_map/reduce_scatter | solution.py:443
  3155.7 39.7 %collective-permute-start.22 = (bf16[16,1536]{1,0:T(8,128)(2,1)S(1)}, bf16[16,1536]{1,0:T(8,128)(2,1)S(1)}, u32[]{:S(2)}, u32[]{:S(2)}) collective-permute-start(bf16[16,1536]{1,0:T(8,128)(2,1)S(1)} %get-tuple-element.1625), channel_id=1, source_target_pairs={{0,16},{16,32},{32,48},{48,64},{64,80},{80,96},{96,112},{1,17},{17... | collective-permute-start | bytes 147464
  3158.6 24.2 collective-permute-start.20
  3162.5 39.6 %collective-permute-start.18 = (bf16[16,1536]{1,0:T(8,128)(2,1)S(1)}, bf16[16,1536]{1,0:T(8,128)(2,1)S(1)}, u32[]{:S(2)}, u32[]{:S(2)}) collective-permute-start(bf16[16,1536]{1,0:T(8,128)(2,1)S(1)} %get-tuple-element.1623), channel_id=1, source_target_pairs={{0,16},{16,32},{32,48},{48,64},{64,80},{80,96},{96,112},{1,17},{17... | collective-permute-start | bytes 147464
  3166.7 43.2 %collective-permute-start.16 = (bf16[16,1536]{1,0:T(8,128)(2,1)S(1)}, bf16[16,1536]{1,0:T(8,128)(2,1)S(1)}, u32[]{:S(2)}, u32[]{:S(2)}) collective-permute-start(bf16[16,1536]{1,0:T(8,128)(2,1)S(1)} %get-tuple-element.1622), channel_id=1, source_target_pairs={{0,16},{16,32},{32,48},{48,64},{64,80},{80,96},{96,112},{1,17},{17... | collective-permute-start | bytes 147464
  3181.5 32.6 %collective-permute-start.14 = (bf16[16,1536]{1,0:T(8,128)(2,1)S(1)}, bf16[16,1536]{1,0:T(8,128)(2,1)S(1)}, u32[]{:S(2)}, u32[]{:S(2)}) collective-permute-start(bf16[16,1536]{1,0:T(8,128)(2,1)S(1)} %get-tuple-element.1621), channel_id=1, source_target_pairs={{0,16},{16,32},{32,48},{48,64},{64,80},{80,96},{96,112},{1,17},{17... | collective-permute-start | bytes 147464
  (329 other events, 12527.4 us)
Sparse Core Ops, SparseCore 0:
  9.7 211.8 all-gather.6
  223.9 234.3 all-gather.10
  460.0 265.5 all-gather.12
  2641.6 411.0 all-gather.8
  3177.5 30.1 reduce-scatter.18
where the time goes:
time: 3270 us; the launch traced here: 3230 us
  matrix products  1190 us (36%)
  starting transfers between devices  497 us (15%)
  waiting for transfers between devices  449 us (14%)
  local copies, waits for them, and re-layouts  401 us (12%)
  blocking collectives  322 us (10%)
  other arithmetic  311 us (10%)
  loops' own time  44.4 us (1%)
    ppermute x124, starting transfers between devices, shifted(): return lax.ppermute(block, axis, route)  397 us
    unnamed x2, blocking collectives  322 us
    all_gather x1, waiting for transfers between devices, gather_turned(): whole = lax.all_gather(both, axis, axis=0, tiled=True)  222 us
    dot_general x120, matrix products, transport(): inner_wm = jnp.einsum('hsd,hnd->hsn', vectors, moving, precision=PRECISE)  220 us
    all_gather x1, waiting for transfers between devices, per_device(): lax.all_gather(w_down, ('dp', 'ctx'), axis=0, tiled=True)  194 us
    dot_general x120, matrix products, transport(): solved = jnp.einsum('hst,htn->hsn', inverse, inner_wm, precision=PRECISE)  170 us
    another operation x6, other arithmetic, own_block(): jax.scipy.linalg.solve_triangular(system, identity, lower=True, unit_diag...  123 us
    dot_general x90, matrix products, transport(): jnp.einsum('hsn,hsd->hnd', solved, beta_vals[:, :, None] * vectors, preci...  122 us
  transfers between devices with their start and end apart: 149, of which 13 were waited for; matrix products, arithmetic and copies ran while one was open for 40% of the time, Pallas kernels for 0%

commit v1 on v0

v1 whole, which is shorter than its diff:
```python
import jax, jax.numpy as jnp
from jax import lax
from jax.experimental import pallas as pl
from jax.experimental.pallas import tpu as pltpu
from jax.sharding import Mesh, PartitionSpec as P

F32, BF16 = jnp.float32, jnp.bfloat16
SEQ, HD, BLK = 1024, 128, 128
NB = SEQ // BLK
NQC = (NB * (NB - 1) // 2) * BLK
SCALE = HD ** (-0.5)
GROUP = 4


def mm(a, b, dims=((1,), (0,))):
    return lax.dot_general(
        a.astype(BF16), b.astype(BF16), (dims, ((), ())), preferred_element_type=F32
    )


def mm_nt(a, b):
    return mm(a, b, ((1,), (1,)))


def mm_tn(a, b):
    return mm(a, b, ((0,), (0,)))


def split(a):
    high = a.astype(BF16)
    return high, (a - high.astype(F32)).astype(BF16)


def mm3(a, b):
    ah, al = split(a)
    bh, bl = split(b)
    return mm(ah, bh) + (mm(ah, bl) + mm(al, bh))


def iota2(axis):
    return lax.broadcasted_iota(jnp.int32, (BLK, BLK), axis)


BASE = 16


def unit_inverses(lowers):
    row, col = iota2(0), iota2(1)
    eye = (row == col).astype(F32)
    in_base = (row // BASE) == (col // BASE)
    narrow = [jnp.where(in_base, low, 0.0) for low in lowers]
    inv = [eye for _ in lowers]
    for u in range(BASE - 1):
        pick = (col % BASE) == u
        coef = [jnp.sum(jnp.where(pick, low, 0.0), axis=1, keepdims=True) for low in narrow]
        for n, (t, c) in enumerate(zip(inv, coef)):
            t3 = t.reshape(BLK // BASE, BASE, BLK)
            lead = jnp.broadcast_to(t3[:, u : u + 1, :], t3.shape).reshape(BLK, BLK)
            inv[n] = t - c * lead
    size = BASE
    while size < BLK:
        off = ((row // (2 * size)) == (col // (2 * size))) & ((row // size) != (col // size))
        mid = [mm3(t, jnp.where(off, low, 0.0)) for t, low in zip(inv, lowers)]
        inv = [t - mm3(m, t) for t, m in zip(inv, mid)]
        size *= 2
    return inv


def fwd_kernel(q, k, v, w, bcol, brow, dcol, drow, o, probs, qc, t_out, a_out, z_out, m_out, kp_out, s_buf, x_buf, qm_buf):
    row, col = iota2(0), iota2(1)
    strict, closed = row > col, row >= col
    eye = (row == col).astype(F32)

    def group(g, carry):
        sl = [pl.ds(pl.multiple_of((g * GROUP + n) * BLK, BLK), BLK) for n in range(GROUP)]
        qs = [q[s, :] for s in sl]
        ks = [k[s, :] for s in sl]
        ws = [w[s, :] for s in sl]
        bc = [bcol[0, s, :] for s in sl]
        br = [brow[0, :, s] for s in sl]
        low = [jnp.where(strict, mm_nt(x, x), 0.0) * b for x, b in zip(ws, br)]
        inv = unit_inverses(low)
        m1 = [jnp.where(strict, mm_nt(x, y), 0.0) for x, y in zip(ws, ks)]
        gq = [jnp.where(closed, mm_nt(x, y), 0.0) * b for x, y, b in zip(qs, ws, br)]
        a = [mm(x, t) for x, t in zip(gq, inv)]
        z = [mm_tn(t, b * x.astype(F32)) for t, b, x in zip(inv, bc, ws)]
        sd = [mm_nt(x, y) - mm(p, m) for x, y, p, m in zip(qs, ks, a, m1)]
        qm = [x.astype(F32) - mm(p, y) for x, p, y in zip(qs, a, ws)]
        kmt = [x.astype(F32).T - mm_tn(zz, m) for x, zz, m in zip(ks, z, m1)]
        pm = [eye - mm_tn(zz, x) for zz, x in zip(z, ws)]
        for n, s in enumerate(sl):
            b = g * GROUP + n
            t_out[0, s, :] = inv[n].astype(t_out.dtype)
            a_out[0, s, :] = a[n].astype(a_out.dtype)
            z_out[0, s, :] = z[n].astype(z_out.dtype)
            m_out[0, s, :] = m1[n].astype(m_out.dtype)
            kp_out[0, s, :HD] = kmt[n].astype(BF16)
            kp_out[0, s, HD:] = pm[n].astype(BF16)
            qm_buf[s, :] = qm[n]
            s_buf[s, s] = sd[n]
        return carry

    lax.fori_loop(0, NB // GROUP, group, 0)
    at = NQC
    for j in range(NB - 2, -1, -1):
        r0 = (j + 1) * BLK
        rows = SEQ - r0
        x_buf[r0 : r0 + BLK, :] = qm_buf[r0 : r0 + BLK, :]
        x = x_buf[r0:, :].astype(BF16)
        at -= rows
        qc[0, at : at + rows, :] = x
        both = mm(x, kp_out[0, j * BLK : r0, :])
        s_buf[r0:, j * BLK : r0] = both[:, :HD]
        x_buf[r0:, :] = both[:, HD:]
    for i in range(NB):
        lo, width = i * BLK, (i + 1) * BLK
        s = s_buf[lo:width, :width] * SCALE
        seen = dcol[lo:width, :] == drow[:, :width]
        seen = seen & (
            lax.broadcasted_iota(jnp.int32, (BLK, width), 0) + lo
            >= lax.broadcasted_iota(jnp.int32, (BLK, width), 1)
        )
        s = jnp.where(seen, s, -1e30)
        e = jnp.exp(s - jnp.max(s, axis=1, keepdims=True))
        p = e * (1.0 / jnp.sum(e, axis=1, keepdims=True))
        pb = p.astype(BF16)
        probs[0, lo:width, :width] = pb
        o[lo:width, :] = mm(pb, v[:width, :])


def bwd_kernel(q, k, v, w, bcol, brow, o, do, probs, qc, t_in, a_in, z_in, m_in, kp, dq, dk, dv, dw, dbc, dbr, ds_buf, x_buf, dkm_buf, dpm_buf, ):
    row, col = iota2(0), iota2(1)
    strict, closed = row > col, row >= col
    for i in range(NB):
        lo, width = i * BLK, (i + 1) * BLK
        p = probs[0, lo:width, :width].astype(F32)
        g = do[lo:width, :]
        delta = jnp.sum(g * o[lo:width, :], axis=1, keepdims=True)
        ds = p * (mm_nt(g, v[:width, :]) - delta) * SCALE
        ds_buf[lo:width, :width] = ds.astype(BF16)
    for j in range(NB):
        lo = j * BLK
        dv[lo : lo + BLK, :] = mm_tn(probs[0, lo:, lo : lo + BLK], do[lo:, :]).astype(dv.dtype)
    x_buf[...] = jnp.zeros_like(x_buf)
    dkm_buf[SEQ - BLK :, :] = jnp.zeros((BLK, HD), F32)
    dpm_buf[SEQ - BLK :, :] = jnp.zeros((BLK, HD), F32)
    at = 0
    for j in range(NB - 1):
        lo, r0 = j * BLK, (j + 1) * BLK
        rows = SEQ - r0
        x = x_buf[r0:, :].astype(BF16)
        ds = ds_buf[r0:, lo:r0]
        qcj = qc[0, at : at + rows, :]
        at += rows
        both = mm_tn(qcj, jnp.concatenate([x, ds], axis=1))
        dpm_buf[lo:r0, :] = both[:, :HD]
        dkm_buf[lo:r0, :] = both[:, HD:].T
        kpj = kp[0, lo:r0, :]
        x_buf[r0:, :] = mm_nt(jnp.concatenate([ds, x], axis=1), kpj)

    def group(g, carry):
        sl = [pl.ds(pl.multiple_of((g * GROUP + n) * BLK, BLK), BLK) for n in range(GROUP)]
        rng = range(GROUP)
        Q = [q[s, :] for s in sl]
        K = [k[s, :] for s in sl]
        W = [w[s, :] for s in sl]
        bc = [bcol[0, s, :] for s in sl]
        br = [brow[0, :, s] for s in sl]
        E = [ds_buf[s, s] for s in sl]
        T = [t_in[0, s, :] for s in sl]
        A = [a_in[0, s, :] for s in sl]
        Z = [z_in[0, s, :] for s in sl]
        M = [m_in[0, s, :] for s in sl]
        dQm = [x_buf[s, :] for s in sl]
        dKm = [dkm_buf[s, :] for s in sl]
        dPm = [dpm_buf[s, :] for s in sl]
        E = [jnp.where(closed, e, jnp.zeros_like(e)) for e in E]
        i1 = [mm_nt(W[n], W[n]) for n in rng]
        qw = [jnp.where(closed, mm_nt(Q[n], W[n]), 0.0) for n in rng]
        dA = [-(mm_nt(E[n], M[n]) + mm_nt(dQm[n], W[n])) for n in rng]
        dM = [jnp.where(strict, -(mm_tn(A[n], E[n]) + mm_nt(Z[n], dKm[n])), 0.0) for n in rng]
        dZ = [-(mm(M[n], dKm[n]) + mm_nt(W[n], dPm[n])) for n in rng]
        dW = [-(mm_tn(A[n], dQm[n]) + mm(Z[n], dPm[n])) for n in rng]
        dG = [jnp.where(closed, mm_nt(dA[n], T[n]), 0.0) for n in rng]
        bw = [bc[n] * W[n].astype(F32) for n in rng]
        dT = [mm_tn(qw[n] * br[n], dA[n]) + mm_nt(bw[n], dZ[n]) for n in rng]
        dBW = [mm(T[n], dZ[n]) for n in rng]
        dL = [mm_tn(T[n], dT[n]) for n in rng]
        dL = [jnp.where(strict, -mm_nt(dL[n], T[n]), 0.0) for n in rng]
        dI = [dL[n] * br[n] for n in rng]
        R = [dG[n] * br[n] for n in rng]
        for n, s in enumerate(sl):
            dbr[0, :, s] = jnp.sum(dL[n] * i1[n] + dG[n] * qw[n], axis=0, keepdims=True)
            dbc[0, s, :] = jnp.sum(dBW[n] * W[n].astype(F32), axis=1, keepdims=True)
            dq[s, :] = (dQm[n] + mm(E[n], K[n]) + mm(R[n], W[n])).astype(dq.dtype)
            dk[s, :] = (dKm[n] + mm_tn(E[n], Q[n]) + mm_tn(dM[n], W[n])).astype(dk.dtype)
            dw[s, :] = (
                dW[n]
                + bc[n] * dBW[n]
                + mm_tn(R[n], Q[n])
                + mm(dM[n], K[n])
                + mm(dI[n] + dI[n].T, W[n])
            )
        return carry

    lax.fori_loop(0, NB // GROUP, group, 0)


def _full(shape):
    return pl.BlockSpec(shape, lambda s: (0,) * len(shape))


def _slot(*shape):
    return pl.BlockSpec((1,) + shape, lambda s: (s,) + (0,) * len(shape))


def _cols(at):
    return pl.BlockSpec((SEQ, HD), lambda s: (0, at + s))


VM = 60 * 1024 * 1024


def attn_fwd(qkv, vec, bcol, brow, dcol, drow):
    slots = bcol.shape[0]
    sds = jax.ShapeDtypeStruct
    return pl.pallas_call(
        fwd_kernel,
        grid=(slots,),
        in_specs=[_cols(0), _cols(2), _cols(4), _cols(0), _slot(SEQ, 1), _slot(1, SEQ), _full((SEQ, 1)), _full((1, SEQ))],
        out_specs=[_cols(0), _slot(SEQ, SEQ), _slot(NQC, HD)] + [_slot(SEQ, BLK)] * 4 + [_slot(SEQ, 2 * HD)],
        out_shape=[
            sds((SEQ, slots * HD), F32),
            sds((slots, SEQ, SEQ), BF16),
            sds((slots, NQC, HD), BF16),
            sds((slots, SEQ, BLK), F32),
            sds((slots, SEQ, BLK), BF16),
            sds((slots, SEQ, BLK), BF16),
            sds((slots, SEQ, BLK), BF16),
            sds((slots, SEQ, 2 * HD), BF16),
        ],
        scratch_shapes=[pltpu.VMEM((SEQ, SEQ), F32), pltpu.VMEM((SEQ, HD), F32), pltpu.VMEM((SEQ, HD), F32)],
        compiler_params=pltpu.CompilerParams(vmem_limit_bytes=VM),
        name="attn_fwd",
    )(qkv, qkv, qkv, vec, bcol, brow, dcol, drow)


def attn_bwd(qkv, vec, bcol, brow, o, do, saved):
    slots = bcol.shape[0]
    sds = jax.ShapeDtypeStruct
    return pl.pallas_call(
        bwd_kernel,
        grid=(slots,),
        in_specs=[_cols(0), _cols(2), _cols(4), _cols(0), _slot(SEQ, 1), _slot(1, SEQ), _cols(0), _cols(0)]
        + [_slot(SEQ, SEQ), _slot(NQC, HD)] + [_slot(SEQ, BLK)] * 4 + [_slot(SEQ, 2 * HD)],
        out_specs=[_cols(0)] * 4 + [_slot(SEQ, 1), _slot(1, SEQ)],
        out_shape=[sds((SEQ, slots * HD), BF16)] * 3 + [sds((SEQ, slots * HD), F32), sds((slots, SEQ, 1), F32), sds((slots, 1, SEQ), F32)],
        scratch_shapes=[pltpu.VMEM((SEQ, SEQ), BF16)] + [pltpu.VMEM((SEQ, HD), F32)] * 3,
        compiler_params=pltpu.CompilerParams(vmem_limit_bytes=VM),
        name="attn_bwd",
    )(qkv, qkv, qkv, vec, bcol, brow, o, do, *saved)


EPS_NORM = 1e-05
EPS_UNIT = 1e-06
GROUPS = ("zl", "y", "zh")
TEAM = ("x", "c")
ALL = GROUPS + TEAM


def rms_scale(values, gain_vec):
    return (
        values * lax.rsqrt(jnp.mean(values * values, axis=-1, keepdims=True) + EPS_NORM) * gain_vec
    )


def dot_nn(a, b):
    return lax.dot_general(a, b, (((1,), (0,)), ((), ())), preferred_element_type=F32)


def dot_nt(a, b):
    return lax.dot_general(a, b, (((1,), (1,)), ((), ())), preferred_element_type=F32)


def dot_tn(a, b):
    return lax.dot_general(a, b, (((0,), (0,)), ((), ())), preferred_element_type=F32)


def gather_rows(block):
    width = block.shape[1]
    whole = lax.all_gather(block.reshape(2, -1, width), TEAM, axis=1)
    return whole.reshape(-1, width)


def scatter_rows(partial):
    width = partial.shape[1]
    parts = partial.astype(BF16).reshape(2, 8, -1, width)
    mine = lax.psum_scatter(parts, TEAM, scatter_dimension=1, tiled=False)
    return mine.reshape(-1, width).astype(F32)


def path_vectors(current, conv_w, same_doc):
    conved = conv_w[0] * current
    for tap in range(1, conv_w.shape[0]):
        earlier = jnp.pad(current, ((tap, 0), (0, 0)))[: current.shape[0]]
        conved = conved + conv_w[tap] * jnp.where(same_doc[tap][:, None], earlier, 0.0)
    heads = conved.reshape(current.shape[0], -1, HD)
    unit = heads * lax.rsqrt(jnp.sum(heads * heads, axis=-1, keepdims=True) + EPS_UNIT)
    return unit.reshape(current.shape)


def per_device(
    tokens,
    doc_start,
    gain_attn,
    w_query,
    w_key,
    w_value,
    w_path,
    conv_path,
    w_beta,
    w_out,
    gain_ffn,
    w_gate,
    w_up,
    w_down,
    grad_out,
):
    zh, chip, core = lax.axis_index("zh"), lax.axis_index("x"), lax.axis_index("c")
    dp = lax.axis_index("zl") * 4 + lax.axis_index("y")
    width = tokens.shape[2]
    share = w_query.shape[0]
    first = zh == 0
    head_a, head_b = 3 * chip + 2 * core, 3 * chip + 1

    pair = jnp.stack([tokens, grad_out])
    mine = jnp.where(first, pair[:, 0], pair[:, 1])
    other = jnp.where(first, pair[:, 1], pair[:, 0])
    got = lax.ppermute(other, "zh", [(0, 1), (1, 0)])
    halves = jnp.stack([jnp.where(first, mine, got), jnp.where(first, got, mine)], axis=1)
    x_rows = halves[0].reshape(-1, width)
    g_rows = halves[1].reshape(-1, width)
    doc_rows = jnp.cumsum(doc_start, axis=1)
    docs = jnp.where(first, doc_rows[0], doc_rows[1])

    small = jnp.concatenate(
        [gain_attn[:, None], gain_ffn[:, None], conv_path.T, w_beta], axis=1
    )
    small = lax.all_gather(small.reshape(1, -1), ALL, axis=0, tiled=True)
    small = small.reshape(width, -1)
    gain_a, gain_f = small[:, 0].astype(F32), small[:, 1].astype(F32)
    conv_full, beta_full = small[:, 2:6].T.astype(F32), small[:, 6:]
    kinds = jnp.stack([w_query, w_key, w_value, w_path], axis=1).reshape(share, 4, 4, 3, HD)
    slot_a = jnp.concatenate([kinds[:, :, :, 0:1], kinds[:, :, :, 2:3]], axis=3)
    slot_b = jnp.broadcast_to(kinds[:, :, :, 1:2], slot_a.shape)
    heads_pack = jnp.stack([slot_a, slot_b], axis=4).transpose(2, 3, 0, 1, 4, 5)
    heads_pack = heads_pack.reshape(8, share, -1)
    ffn_pack = jnp.stack([w_gate, w_up], axis=1).reshape(share, 2, 16, 8, 32)
    ffn_pack = ffn_pack.transpose(3, 0, 1, 2, 4).reshape(8, share, -1)
    packs = jnp.concatenate([heads_pack, ffn_pack], axis=2)
    packs = lax.all_to_all(packs, TEAM, split_axis=0, concat_axis=0, tiled=True)
    packs = packs.reshape(8 * share, -1)
    w_heads = lax.all_gather(packs[:, : 8 * HD], GROUPS, axis=0, tiled=True)
    w_out_full = lax.all_gather(w_out, ALL, axis=0, tiled=True)
    w_ffn = lax.all_gather(packs[:, 8 * HD :], GROUPS, axis=0, tiled=True)
    w_down_t = lax.all_gather(w_down, GROUPS, axis=0, tiled=True)
    out_a = lax.dynamic_slice_in_dim(w_out_full, head_a * HD, HD, 0)
    out_b = lax.dynamic_slice_in_dim(w_out_full, head_b * HD, HD, 0)
    out_b = jnp.where(core == 0, out_b, jnp.zeros_like(out_b))
    w_out_t = jnp.concatenate([out_a, out_b], axis=0)

    def two_heads(full, size):
        return jnp.concatenate(
            [
                lax.dynamic_slice_in_dim(full, head_a * size, size, 1),
                lax.dynamic_slice_in_dim(full, head_b * size, size, 1),
            ],
            axis=1,
        )

    def back_to_all(part, size):
        full = jnp.zeros((part.shape[0], 12 * size), F32)
        full = lax.dynamic_update_slice_in_dim(full, part[:, :size], head_a * size, 1)
        own_b = jnp.where(core == 0, part[:, size:], 0.0)
        return lax.dynamic_update_slice_in_dim(full, own_b, head_b * size, 1)

    w_beta_t = two_heads(beta_full, 1)
    conv_t = two_heads(conv_full, HD)
    same_doc = [
        jnp.concatenate([jnp.zeros((tap,), bool), docs[: SEQ - tap] == docs[tap:]])
        for tap in range(4)
    ]

    x_f = x_rows.astype(F32)
    normed = rms_scale(x_f, gain_a).astype(BF16)
    normed_all = gather_rows(normed)
    g_all = gather_rows(g_rows)
    qkvp = dot_nn(normed_all, w_heads).astype(BF16)
    beta_raw = dot_nn(normed_all, w_beta_t)
    betas = (2.0 * jax.nn.sigmoid(beta_raw)).T
    vec_f, vec_pull = jax.vjp(
        lambda cur, cw: path_vectors(cur, cw, same_doc), qkvp[:, 6 * HD :].astype(F32), conv_t
    )
    vec = vec_f.astype(BF16)
    bcol, brow = betas[:, :, None], betas[:, None, :]
    o, *saved = attn_fwd(qkvp, vec, bcol, brow, docs[:, None], docs[None, :])
    mixed = o.astype(BF16)
    hidden = x_f + scatter_rows(dot_nn(mixed, w_out_t))
    normed_ffn = rms_scale(hidden, gain_f).astype(BF16)
    ffn_all = gather_rows(normed_ffn)
    gate_up = dot_nn(ffn_all, w_ffn)

    def gated(pre):
        return jax.nn.silu(pre[:, :512]) * pre[:, 512:]

    act_f, act_pull = jax.vjp(gated, gate_up)
    act = act_f.astype(BF16)
    out_rows = (hidden + scatter_rows(dot_nn(act, w_down_t))).astype(BF16)

    (d_gate_up,) = act_pull(dot_nt(g_all, w_down_t))
    d_gate_up = d_gate_up.astype(BF16)
    d_normed_ffn = scatter_rows(dot_nt(d_gate_up, w_ffn))
    _, ffn_pull = jax.vjp(rms_scale, hidden, gain_f)
    d_hidden, d_gain_ffn = ffn_pull(d_normed_ffn)
    d_hidden = d_hidden + g_rows.astype(F32)
    branch_all = gather_rows(d_hidden.astype(BF16))
    d_mixed = dot_nt(branch_all, w_out_t)
    d_q, d_k, d_v, d_vec, d_bc, d_br = attn_bwd(qkvp, vec, bcol, brow, o, d_mixed, saved)
    d_path, d_conv = vec_pull(d_vec)
    d_betas = (d_bc[:, :, 0] + d_br[:, 0, :]) * betas * (1.0 - 0.5 * betas)
    d_beta = d_betas.T.astype(BF16)
    d_qkvp = jnp.concatenate([d_q, d_k, d_v, d_path.astype(BF16)], axis=1)
    d_normed = scatter_rows(dot_nt(d_qkvp, w_heads) + dot_nt(d_beta, w_beta_t))
    _, norm_pull = jax.vjp(rms_scale, x_f, gain_a)
    d_x, d_gain_attn = norm_pull(d_normed)
    d_rows = (d_x + d_hidden).astype(BF16)

    def sum_rows(grad):
        return lax.psum_scatter(grad.astype(BF16), GROUPS, scatter_dimension=0, tiled=True)

    d_down = sum_rows(dot_tn(act, g_all)).astype(F32)
    d_ffn = sum_rows(dot_tn(ffn_all, d_gate_up))
    d_out = lax.psum(dot_tn(mixed, branch_all).astype(BF16), GROUPS)
    d_heads = sum_rows(dot_tn(normed_all, d_qkvp))
    none = jnp.zeros((HD, width), BF16)
    own = core == 0
    chip_rows = jnp.concatenate(
        [
            jnp.where(own, d_out[:HD], none),
            jnp.where(own, d_out[HD:], none),
            jnp.where(own, none, d_out[:HD]),
        ],
        axis=0,
    )
    window = lax.dynamic_slice_in_dim(chip_rows, (dp % 2) * 192 + zh * 96, 96, 0)
    window = jnp.where(chip == dp // 2, window, jnp.zeros_like(window))
    back = jnp.concatenate([d_heads, d_ffn, window], axis=1).reshape(8, share, -1)
    back = lax.all_to_all(back, TEAM, split_axis=0, concat_axis=0, tiled=True)
    d_w_out = jnp.sum(back[:, :, 16 * HD :].astype(F32), axis=0)
    heads_back = back[:, :, : 8 * HD].reshape(4, 2, share, 4, 2, HD)
    by_head = jnp.stack(
        [heads_back[:, 0, :, :, 0], heads_back[:, 0, :, :, 1], heads_back[:, 1, :, :, 0]], axis=1
    )
    by_kind = by_head.transpose(3, 2, 0, 1, 4).reshape(4, share, width).astype(F32)
    ffn_back = back[:, :, 8 * HD : 16 * HD].reshape(8, share, 2, 16, 32)
    ffn_back = ffn_back.transpose(2, 1, 3, 0, 4).reshape(2, share, -1).astype(F32)

    d_beta_w = back_to_all(dot_tn(normed_all, d_beta), 1)
    small_back = jnp.concatenate(
        [d_gain_attn[:, None], d_gain_ffn[:, None], back_to_all(d_conv, HD).T, d_beta_w], axis=1
    )
    small_back = lax.psum_scatter(
        small_back.reshape(128, -1), ALL, scatter_dimension=0, tiled=True
    ).reshape(share, -1)

    pair = jnp.stack([out_rows, d_rows]).reshape(2, 2, -1, width)
    mine = jnp.where(first, pair[:, 0], pair[:, 1])
    other = jnp.where(first, pair[:, 1], pair[:, 0])
    got = lax.ppermute(other, "zh", [(0, 1), (1, 0)])
    rows = jnp.stack([jnp.where(first, mine, got), jnp.where(first, got, mine)], axis=1)
    return (
        rows[0],
        rows[1],
        small_back[:, 0],
        by_kind[0],
        by_kind[1],
        by_kind[2],
        by_kind[3],
        small_back[:, 2:6].T,
        small_back[:, 6:],
        d_w_out,
        small_back[:, 1],
        ffn_back[0],
        ffn_back[1],
        d_down,
    )


def solution(mesh):
    fine = Mesh(mesh.devices.reshape(2, 4, 2, 4, 2), ("zl", "y", "zh", "x", "c"))
    dp, ctx = ("zl", "y"), ("zh", "x", "c")
    rows, flat, mat, taps = P(dp, ctx, None), P(ALL), P(ALL, None), P(None, ALL)
    return jax.shard_map(
        per_device,
        mesh=fine,
        in_specs=(
            rows, P(dp, None), flat, mat, mat, mat, mat, taps, mat, mat, flat, mat, mat, mat, rows,
        ),
        out_specs=(
            rows, rows, flat, mat, mat, mat, mat, taps, mat, mat, flat, mat, mat, mat,
        ),
        check_vma=False,
    )
```

time: 3270 us -> 1460 us (0.45)
  matrix products: 1190 us -> 68.2 us
  waiting for transfers between devices: 449 us -> 1000 us
  starting transfers between devices: 497 us -> 23.7 us
  local copies, waits for them, and re-layouts: 401 us -> 64.3 us
  other arithmetic: 311 us -> 47.8 us
  blocking collectives: 322 us -> 194 us
  loops' own time: 44.4 us -> 0 us
  Pallas kernels: 0 us -> 36.4 us
    dot_general x647 -> x15, matrix products: 1180 us -> 68.2 us  [the longest x5 24.2 us: dot_nt(): lax.dot_general(a, b, (((1,), (1,)), ((), ())), preferred_element_type=F32)]
    ppermute x124 -> x2, starting transfers between devices: 397 us -> 7.43 us  [per_device(): got = lax.ppermute(other, 'zh', [(0, 1), (1, 0)])]
    unnamed x2 -> x0, blocking collectives: 322 us -> none
    reduce_scatter x1 -> x7, waiting for transfers between devices: 0.01 us -> 298 us  [the longest x3 168 us: sum_rows(): lax.psum_scatter(grad.astype(BF16), GROUPS, scatter_dimension=0, tiled=True)]
    all_gather x0 -> x1, blocking collectives: none -> 176 us  [per_device(): small = lax.all_gather(small.reshape(1, -1), ALL, axis=0, tiled=True)]
    unnamed x21 -> x18, waiting for transfers between devices: 2.58 us -> 139 us
    another operation x13 -> x7, other arithmetic: 128 us -> 3.38 us  [the longest x3 2.31 us: per_device(): jnp.stack([jnp.where(first, mine, got), jnp.where(first, got, mine)], axi...]
    dynamic_slice x122 -> x6, local copies, waits for them, and re-layouts: 120 us -> 0.81 us  [the longest x4 0.55 us: two_heads(): lax.dynamic_slice_in_dim(full, head_a * size, size, 1)]
  transfers between devices with their start and end apart: 149 -> 20, of which waited for: 13 -> 16; matrix products, arithmetic and copies ran while one was open for 40% -> 9% of each run, Pallas kernels for 0% -> 3%
where the time goes in v1:
time: 1460 us; the launch traced here: 1450 us
  waiting for transfers between devices  1000 us (68%)
  blocking collectives  194 us (13%)
  matrix products  68.2 us (5%)
  local copies, waits for them, and re-layouts  64.3 us (4%)
  other arithmetic  47.8 us (3%)
  Pallas kernels  36.4 us (2%)
  starting transfers between devices  23.7 us (2%)
  between operations  15.7 us (1%)
    all_gather x1, blocking collectives, per_device(): small = lax.all_gather(small.reshape(1, -1), ALL, axis=0, tiled=True)  176 us
    all_gather x1, waiting for transfers between devices, per_device(): w_out_full = lax.all_gather(w_out, ALL, axis=0, tiled=True)  169 us
    reduce_scatter x3, waiting for transfers between devices, sum_rows(): lax.psum_scatter(grad.astype(BF16), GROUPS, scatter_dimension=0, tiled=True)  168 us
    unnamed x18, waiting for transfers between devices  139 us
    reduce_scatter x4, waiting for transfers between devices, scatter_rows(): mine = lax.psum_scatter(parts, TEAM, scatter_dimension=1, tiled=False)  129 us
    all_gather x4, waiting for transfers between devices, gather_rows(): whole = lax.all_gather(block.reshape(2, -1, width), TEAM, axis=1)  92.4 us
    psum x1, waiting for transfers between devices, per_device(): d_out = lax.psum(dot_tn(mixed, branch_all).astype(BF16), GROUPS)  90.5 us
    all_gather x1, waiting for transfers between devices, per_device(): w_ffn = lax.all_gather(packs[:, 8 * HD:], GROUPS, axis=0, tiled=True)  77.3 us
  transfers between devices with their start and end apart: 20, of which 16 were waited for; matrix products, arithmetic and copies ran while one was open for 9% of the time, Pallas kernels for 3%

profile of v1, /device:TPU:1, one launch (start us, length us, event | category | flops | bytes accessed | tf_op | source)
XLA Modules:
  0.0 1453.0 jit_solution(1323678686546623803)
XLA Ops:
  8.5 4.5 collective-permute-start
  16.2 176.4 %all-gather.1 = bf16[128,1,216]{2,1,0:T(2,128)(2,1)S(1)} all-gather(bf16[1,1,216]{2,1,0:T(2,128)(2,1)S(1)} %reshape.558), channel_id=1, replica_groups=mesh['zl'=2,'y'=4,'zh'=2,'x'=4,'c'=2] {'zl','y','zh','x','c'}, dimensions={0}, use_global_device_ids=true | all-gather | bytes 55728 | tf_op jit(solution)/shard_map/all_gather | solution.py:349
  200.7 18.0 %all_to_all.10 = bf16[8,12,2048]{2,1,0:T(8,128)(2,1)S(1)} all-to-all(bf16[8,12,2048]{2,1,0:T(8,128)(2,1)S(1)} %copy.240), channel_id=1, replica_groups=mesh['zl'=2,'y'=4,'zh'=2,'x'=4,'c'=2] {'x','c'}, dimensions={0} | all-to-all | bytes 786432 | tf_op jit(solution)/shard_map/all_to_all | solution.py:361
  232.3 68.9 %all-gather.14.cloned.1.call-done = bf16[1536,1024]{1,0:T(8,128)(2,1)} async-done(((bf16[96,1024]{1,0:T(8,128)(2,1)}), bf16[1536,1024]{1,0:T(8,128)(2,1)}) %all-gather.14.cloned.1.call-update) | async-done | bytes 3145744 | tf_op jit(solution)/shard_map/all_gather | solution.py:363
  301.2 6.3 convolution_convert_fusion.7.q.k.v
  322.1 19.0 %attn_fwd.1 = (f32[1024,256]{1,0:T(8,128)}, bf16[2,1024,1024]{2,1,0:T(8,128)(2,1)}, bf16[2,3584,128]{2,1,0:T(8,128)(2,1)}, f32[2,1024,128]{2,1,0:T(8,128)}, bf16...) custom-call(bf16[1024,1024]{1,0:T(8,128)(2,1)} %copy-done, ...), custom_call_target="tpu_custom_call" | custom-call | tf_op jit(solution)/shard_map/attn_fwd/pallas_call | solution.py:227
  341.1 169.5 %all-gather.26.cloned.1.call-done = bf16[128,12,1536]{2,1,0:T(8,128)(2,1)} async-done(((bf16[1,12,1536]{2,1,0:T(8,128)(2,1)}), bf16[128,12,1536]{2,1,0:T(8,128)(2,1)}) %all-gather.26.cloned.1.call-update) | async-done | bytes 4718608 | tf_op jit(solution)/shard_map/all_gather | solution.py:364
  510.6 8.3 reshape.561
  523.2 31.6 %reduce-scatter.8.cloned.1.call-done = bf16[2,1,64,1536]{3,2,0,1:T(8,128)(2,1)} async-done(((bf16[2,8,64,1536]{3,2,0,1:T(8,128)(2,1)}), bf16[2,1,64,1536]{3,2,0,1:T(8,128)(2,1)}) %reduce-scatter.8.cloned.1.call-update) | async-done | bytes 393232 | tf_op jit(solution)/shard_map/reduce_scatter | solution.py:298
  560.1 27.9 %all-gather.16.cloned.1.call-done = bf16[2,8,64,1536]{3,2,0,1:T(8,128)(2,1)} async-done(((bf16[2,1,64,1536]{3,2,0,1:T(8,128)(2,1)}), bf16[2,8,64,1536]{3,2,0,1:T(8,128)(2,1)}) %all-gather.16.cloned.1.call-update) | async-done | bytes 3145744 | tf_op jit(solution)/shard_map/all_gather | solution.py:291
  591.8 77.3 %all-gather.18.cloned.1.call-done = bf16[1536,1024]{1,0:T(8,128)(2,1)} async-done(((bf16[96,1024]{1,0:T(8,128)(2,1)}), bf16[1536,1024]{1,0:T(8,128)(2,1)}) %all-gather.18.cloned.1.call-update) | async-done | bytes 3145744 | tf_op jit(solution)/shard_map/all_gather | solution.py:365
  669.1 8.2 fusion.86
  677.3 67.0 %all-gather.20.cloned.1.call-done = bf16[512,1536]{1,0:T(8,128)(2,1)} async-done(((bf16[32,1536]{1,0:T(8,128)(2,1)}), bf16[512,1536]{1,0:T(8,128)(2,1)}) %all-gather.20.cloned.1.call-update) | async-done | bytes 1572880 | tf_op jit(solution)/shard_map/all_gather | solution.py:366
  744.3 39.8 %all-gather.24.cloned.1.call-done = bf16[1,2,512,1536]{3,2,0,1:T(8,128)(2,1)} async-done(((bf16[1,2,64,1536]{3,2,0,1:T(8,128)(2,1)}), bf16[1,2,512,1536]{3,2,0,1:T(8,128)(2,1)}) %all-gather.24.cloned.1.call-update) | async-done | bytes 3145744 | tf_op jit(solution)/shard_map/all_gather | solution.py:291
  784.2 7.4 fusion.59
  802.9 26.9 %reduce-scatter.12.cloned.1.call-done = bf16[2,1,64,1536]{3,2,0,1:T(8,128)(2,1)} async-done(((bf16[2,8,64,1536]{3,2,0,1:T(8,128)(2,1)}), bf16[2,1,64,1536]{3,2,0,1:T(8,128)(2,1)}) %reduce-scatter.12.cloned.1.call-update) | async-done | bytes 393232 | tf_op jit(solution)/shard_map/reduce_scatter | solution.py:298
  829.7 36.8 %reduce-scatter.10.cloned.1.call-done = bf16[2,1,64,1536]{3,2,0,1:T(8,128)(2,1)} async-done(((bf16[2,8,64,1536]{3,2,0,1:T(8,128)(2,1)}), bf16[2,1,64,1536]{3,2,0,1:T(8,128)(2,1)}) %reduce-scatter.10.cloned.1.call-update) | async-done | bytes 393232 | tf_op jit(solution)/shard_map/reduce_scatter | solution.py:298
  871.5 5.2 convolution_convert_fusion.5
  876.8 24.7 %all-gather.22.cloned.1.call-done = bf16[2,8,64,1536]{3,2,1,0:T(8,128)(2,1)} async-done(((bf16[2,1,64,1536]{3,2,1,0:T(8,128)(2,1)}), bf16[2,8,64,1536]{3,2,1,0:T(8,128)(2,1)}) %all-gather.22.cloned.1.call-update) | async-done | bytes 3145744 | tf_op jit(solution)/shard_map/all_gather | solution.py:291
  901.5 3.9 fusion.41.do
  905.4 17.4 %attn_bwd.1 = (bf16[1024,256]{1,0:T(8,128)(2,1)}, bf16[1024,256]{1,0:T(8,128)(2,1)}, bf16[1024,256]{1,0:T(8,128)(2,1)}, f32[1024,256]{1,0:T(8,128)}, f32[2,1024,1]{2,1,0:T(8,128)}, /*index=5*/f32[2,1,1024]{2,1,0:T(1,128)}) custom-call(bf16[1024,1024]{1,0:T(8,128)(2,1)} %copy-done, bf16[1024,1024]{1,0:T(8,128)(2,1)} %copy-done, bf16[1024,1024]{1,0:T(8,128)(2,1)} %copy-done, ...), custom_call_target="tpu_custom_call" | custom-call | tf_op jit(solution)/shard_map/attn_bwd/pallas_call | solution.py:251
  930.5 3.9 multiply_reduce_fusion.3
  941.7 5.4 fusion.53
  947.4 3.9 add_convert_fusion
  955.2 7.4 convolution_convert_fusion.2
  964.5 6.4 convolution_convert_fusion.3
  978.2 90.5 %all-reduce.18.cloned.1.call-done = bf16[256,1536]{1,0:T(8,128)(2,1)} async-done(((bf16[256,1536]{1,0:T(8,128)(2,1)}), bf16[256,1536]{1,0:T(8,128)(2,1)}) %all-reduce.18.cloned.1.call-update) | async-done | bytes 786448 | tf_op jit(solution)/shard_map/psum | solution.py:443
  1070.2 34.1 %reduce-scatter.14.cloned.1.call-done = bf16[2,1,64,1536]{3,2,0,1:T(8,128)(2,1)} async-done(((bf16[2,8,64,1536]{3,2,0,1:T(8,128)(2,1)}), bf16[2,1,64,1536]{3,2,0,1:T(8,128)(2,1)}) %reduce-scatter.14.cloned.1.call-update) | async-done | bytes 393232 | tf_op jit(solution)/shard_map/reduce_scatter | solution.py:298
  1112.3 74.4 %reduce-scatter.18.cloned.1.call-done = bf16[96,1024]{1,0:T(8,128)(2,1)} async-done(((bf16[1536,1024]{1,0:T(8,128)(2,1)}), bf16[96,1024]{1,0:T(8,128)(2,1)}) %reduce-scatter.18.cloned.1.call-update) | async-done | bytes 196624 | tf_op jit(solution)/shard_map/reduce_scatter | solution.py:439
  1186.6 92.1 %reduce-scatter.16.cloned.1.call-done = bf16[96,1024]{1,0:T(8,128)(2,1)} async-done(((bf16[1536,1024]{1,0:T(8,128)(2,1)}), bf16[96,1024]{1,0:T(8,128)(2,1)}) %reduce-scatter.16.cloned.1.call-update) | async-done | bytes 196624 | tf_op jit(solution)/shard_map/reduce_scatter | solution.py:439
  1280.9 15.1 %all-to-all-start.1 = ((bf16[8,12,3584]{2,1,0:T(8,128)(2,1)}), bf16[8,12,3584]{2,1,0:T(8,128)(2,1)S(1)}, u32[]{:S(2)}, u32[]{:S(2)}) async-start(bf16[8,12,3584]{2,1,0:T(8,128)(2,1)} %reshape.545), calls=%async_computation.7 | async-start | bytes 1835008 | tf_op jit(solution)/shard_map/all_to_all | solution.py:458
  1296.0 137.3 %all-reduce.20.cloned.1.call-done = f32[128,216]{1,0:T(8,128)} async-done(((f32[128,216]{1,0:T(8,128)}), f32[128,216]{1,0:T(8,128)}) %all-reduce.20.cloned.1.call-update) | async-done | bytes 110608
  (331 shorter events, 122.2 us)
Async XLA Ops:
  7.2 219.7 %all-gather.12.cloned.1.call-start = ((), (), s32[]{:S(2)}) async-start(), calls=%async_computation.9 | async-start | bytes 3538944 | tf_op jit(solution)/shard_map/all_gather | solution.py:291
  8.5 188.7 %copy-start.21 = (bf16[12,4096]{1,0:T(8,128)(2,1)S(1)}, bf16[12,4096]{1,0:T(8,128)(2,1)}, u32[]{:S(2)}) copy-start(bf16[12,4096]{1,0:T(8,128)(2,1)} %param.27) | copy-start | bytes 294916
  8.5 185.2 %collective-permute-start = (bf16[2,64,1536]{2,1,0:T(8,128)(2,1)S(1)}, bf16[2,64,1536]{2,1,0:T(8,128)(2,1)S(1)}, u32[]{:S(2)}, u32[]{:S(2)}) collective-permute-start(bf16[2,64,1536]{2,1,0:T(8,128)(2,1)S(1)} %select_bitcast_fusion.2), channel_id=1, source_target_pairs={{0,8},{8,0},{1,9},{9,1},{2,10},{10,2},{3,11},{11,3},{4,12},{12,4},... | collective-permute-start | bytes 1179656 | tf_op jit(solution)/shard_map/ppermute | solution.py:339
  197.1 104.1 %all-gather.14.cloned.1.call-start = ((), (), s32[]{:S(2)}) async-start(), calls=%async_computation.10 | async-start | bytes 3342336 | tf_op jit(solution)/shard_map/all_gather | solution.py:363
  219.5 291.1 %all-gather.26.cloned.1.call-start = ((), (), s32[]{:S(2)}) async-start(), calls=%async_computation.24 | async-start | bytes 6340608 | tf_op jit(solution)/shard_map/all_gather | solution.py:364
  220.2 334.5 %reduce-scatter.8.cloned.1.call-start = ((), (), s32[]{:S(2)}) async-start(), calls=%async_computation.11 | async-start | bytes 3538944 | tf_op jit(solution)/shard_map/reduce_scatter | solution.py:298
  224.3 83.2 %copy-start.27 = (bf16[1536,1]{0,1:T(2,128)(2,1)}, bf16[1536,1]{0,1:T(2,128)(2,1)S(1)}, u32[]{:S(2)}) copy-start(bf16[1536,1]{0,1:T(2,128)(2,1)S(1)} %copy.246) | copy-start | bytes 9220
  341.1 179.0 %copy-start.7 = (f32[1024,256]{1,0:T(8,128)S(1)}, f32[1024,256]{1,0:T(8,128)}, u32[]{:S(2)}) copy-start(f32[1024,256]{1,0:T(8,128)} %get-tuple-element.28.o) | copy-start | bytes 3145732
  523.1 64.9 %all-gather.16.cloned.1.call-start = ((), (), s32[]{:S(2)}) async-start(), calls=%async_computation.12 | async-start | bytes 3538944 | tf_op jit(solution)/shard_map/all_gather | solution.py:291
  555.9 313.4 %copy-start.37 = (f32[2,64]{1,0:T(2,128)}, f32[2,64]{1,0:T(2,128)S(1)}, u32[]{:S(2)}) copy-start(f32[2,64]{1,0:T(2,128)S(1)} %fusion.67) | copy-start | bytes 1540
  557.9 111.2 %all-gather.18.cloned.1.call-start = ((), (), s32[]{:S(2)}) async-start(), calls=%async_computation.13 | async-start | bytes 3342336 | tf_op jit(solution)/shard_map/all_gather | solution.py:365
  558.4 185.9 %all-gather.20.cloned.1.call-start = ((), (), s32[]{:S(2)}) async-start(), calls=%async_computation.14 | async-start | bytes 1671168 | tf_op jit(solution)/shard_map/all_gather | solution.py:366
  559.2 225.0 %all-gather.24.cloned.1.call-start = ((), (), s32[]{:S(2)}) async-start(), calls=%async_computation.23 | async-start | bytes 3538944 | tf_op jit(solution)/shard_map/all_gather | solution.py:291
  560.1 269.7 %reduce-scatter.12.cloned.1.call-start = ((), (), s32[]{:S(2)}) async-start(), calls=%async_computation.16 | async-start | bytes 3538944 | tf_op jit(solution)/shard_map/reduce_scatter | solution.py:298
  797.3 69.3 %reduce-scatter.10.cloned.1.call-start = ((), (), s32[]{:S(2)}) async-start(), calls=%async_computation.15 | async-start | bytes 3538944 | tf_op jit(solution)/shard_map/reduce_scatter | solution.py:298
  802.8 98.7 %all-gather.22.cloned.1.call-start = ((), (), s32[]{:S(2)}) async-start(), calls=%async_computation.17 | async-start | bytes 3538944 | tf_op jit(solution)/shard_map/all_gather | solution.py:291
  871.5 101.4 %reduce-scatter.20.cloned.1.call-start = ((), (), s32[]{:S(2)}) async-start(), calls=%async_computation.22 | async-start | bytes 1671168 | tf_op jit(solution)/shard_map/reduce_scatter | solution.py:439
  876.8 191.9 %all-reduce.18.cloned.1.call-start = ((), (), s32[]{:S(2)}) async-start(), calls=%async_computation.21 | async-start | bytes 1572864 | tf_op jit(solution)/shard_map/psum | solution.py:443
  939.0 165.3 %reduce-scatter.14.cloned.1.call-start = ((), (), s32[]{:S(2)}) async-start(), calls=%async_computation.18 | async-start | bytes 3538944 | tf_op jit(solution)/shard_map/reduce_scatter | solution.py:298
  953.3 233.3 %reduce-scatter.18.cloned.1.call-start = ((), (), s32[]{:S(2)}) async-start(), calls=%async_computation.20 | async-start | bytes 3342336 | tf_op jit(solution)/shard_map/reduce_scatter | solution.py:439
  962.6 316.1 %reduce-scatter.16.cloned.1.call-start = ((), (), s32[]{:S(2)}) async-start(), calls=%async_computation.19 | async-start | bytes 3342336 | tf_op jit(solution)/shard_map/reduce_scatter | solution.py:439
  970.9 462.4 %all-reduce.20.cloned.1.call-start = ((), (), s32[]{:S(2)}) async-start(), calls=%async_computation.25 | async-start | bytes 262144
  977.0 127.2 %copy-start.47 = (f32[2,64]{1,0:T(2,128)S(1)}, f32[2,64]{1,0:T(2,128)}, u32[]{:S(2)}) copy-start(f32[2,64]{1,0:T(2,128)} %copy-done.46) | copy-start | bytes 1540
  977.0 128.6 %copy-start.58 = (f32[2,64]{1,0:T(2,128)S(1)}, f32[2,64]{1,0:T(2,128)}, u32[]{:S(2)}) copy-start(f32[2,64]{1,0:T(2,128)} %copy-done.57) | copy-start | bytes 1540
  977.0 128.6 %copy-start.3 = (bf16[2,1,64,1536]{3,2,0,1:T(8,128)(2,1)S(1)}, bf16[2,1,64,1536]{3,2,0,1:T(8,128)(2,1)}, u32[]{:S(2)}) copy-start(bf16[2,1,64,1536]{3,2,0,1:T(8,128)(2,1)} %reduce-scatter.8.cloned.1.call-done) | copy-start | bytes 1179652
  977.0 128.6 %copy-start.10 = (bf16[1,2,64,1536]{3,2,0,1:T(8,128)(2,1)S(1)}, bf16[1,2,64,1536]{3,2,0,1:T(8,128)(2,1)}, u32[]{:S(2)}) copy-start(bf16[1,2,64,1536]{3,2,0,1:T(8,128)(2,1)} %pad_maximum_fusion.7) | copy-start | bytes 1179652
  977.0 128.6 %copy-start.12 = (bf16[2,1,64,1536]{3,2,0,1:T(8,128)(2,1)S(1)}, bf16[2,1,64,1536]{3,2,0,1:T(8,128)(2,1)}, u32[]{:S(2)}) copy-start(bf16[2,1,64,1536]{3,2,0,1:T(8,128)(2,1)} %reduce-scatter.12.cloned.1.call-done) | copy-start | bytes 1179652
  977.0 128.6 %copy-start.38 = (f32[2,64]{1,0:T(2,128)S(1)}, f32[2,64]{1,0:T(2,128)}, u32[]{:S(2)}) copy-start(f32[2,64]{1,0:T(2,128)} %copy-done.37) | copy-start | bytes 1540
  977.1 128.6 %copy-start.56 = (f32[2,64]{1,0:T(2,128)S(1)}, f32[2,64]{1,0:T(2,128)}, u32[]{:S(2)}) copy-start(f32[2,64]{1,0:T(2,128)} %copy-done.55) | copy-start | bytes 1540
  978.2 129.0 %copy-start.11 = (bf16[1,2,64,1536]{3,2,1,0:T(8,128)(2,1)S(1)}, bf16[1,2,64,1536]{3,2,1,0:T(8,128)(2,1)}, u32[]{:S(2)}) copy-start(bf16[1,2,64,1536]{3,2,1,0:T(8,128)(2,1)} %get-tuple-element.164) | copy-start | bytes 1179652
  1108.0 328.2 %collective-permute-start.1 = (bf16[2,64,1536]{2,1,0:T(8,128)(2,1)}, bf16[2,64,1536]{2,1,0:T(8,128)(2,1)S(1)}, u32[]{:S(2)}, u32[]{:S(2)}) collective-permute-start(bf16[2,64,1536]{2,1,0:T(8,128)(2,1)} %fusion.42), channel_id=1, source_target_pairs={{0,8},{8,0},{1,9},{9,1},{2,10},{10,2},{3,11},{11,3},{4,12},{12,4},... | collective-permute-start | bytes 1179656 | tf_op jit(solution)/shard_map/ppermute | solution.py:479
  1280.9 156.4 %all-to-all-start.1 = ((bf16[8,12,3584]{2,1,0:T(8,128)(2,1)}), bf16[8,12,3584]{2,1,0:T(8,128)(2,1)S(1)}, u32[]{:S(2)}, u32[]{:S(2)}) async-start(bf16[8,12,3584]{2,1,0:T(8,128)(2,1)} %reshape.545), calls=%async_computation.7 | async-start | bytes 1835008 | tf_op jit(solution)/shard_map/all_to_all | solution.py:458
  (56 other events, 622.0 us)
Sparse Core Ops, SparseCore 0:
  197.2 26.8 all-gather.11
  226.4 74.7 all-gather.13
  302.9 207.6 all-gather.25
  523.2 31.4 reduce-scatter.7
  558.0 29.9 all-gather.15
  590.1 78.9 all-gather.17
  670.7 73.5 all-gather.19
  746.6 37.5 all-gather.23
  797.4 32.3 reduce-scatter.11
  832.0 34.5 reduce-scatter.9
  871.6 29.8 all-gather.21
  903.8 69.0 reduce-scatter.19
  976.5 92.1 all-reduce.17
  1070.9 33.2 reduce-scatter.13
  1106.5 80.0 reduce-scatter.17
  1188.9 89.7 reduce-scatter.15
  1283.9 149.3 all-reduce.19

commit v2 on v1

--- a/solution.py
+++ b/solution.py
@@ -1,10 +1,15 @@
-import jax, jax.numpy as jnp
+import functools
+
+import jax
+import jax.numpy as jnp
 from jax import lax
 from jax.experimental import pallas as pl
 from jax.experimental.pallas import tpu as pltpu
 from jax.sharding import Mesh, PartitionSpec as P
 
 F32, BF16 = jnp.float32, jnp.bfloat16
+VM = 60 * 1024 * 1024
+
 SEQ, HD, BLK = 1024, 128, 128
 NB = SEQ // BLK
 NQC = (NB * (NB - 1) // 2) * BLK
@@ -218,9 +223,6 @@
     return pl.BlockSpec((SEQ, HD), lambda s: (0, at + s))
 
 
-VM = 60 * 1024 * 1024
-
-
 def attn_fwd(qkv, vec, bcol, brow, dcol, drow):
     slots = bcol.shape[0]
     sds = jax.ShapeDtypeStruct
@@ -261,42 +263,688 @@
     )(qkv, qkv, qkv, vec, bcol, brow, o, do, *saved)
 
 
+MESH = pl.DeviceIdType.MESH
+ANY = pl.BlockSpec(memory_space=pl.ANY)
+VMEM = pl.BlockSpec(memory_space=pltpu.VMEM)
+
+
+class Place:
+    def __init__(self):
+        self.x, self.c = lax.axis_index("x"), lax.axis_index("c")
+        self.y = lax.axis_index("y")
+        self.zl, self.zh = lax.axis_index("zl"), lax.axis_index("zh")
+        self.z = self.zh * 2 + self.zl
+
+    def chip(self, d):
+        return lax.rem(self.x + d, 4)
+
+    def at_x(self, d):
+        return {"x": lax.rem(self.x + d, 4)}
+
+    def at_xc(self, d, k):
+        return {"x": lax.rem(self.x + d, 4), "c": lax.rem(self.c + k, 2)}
+
+    def sibling(self):
+        return {"c": 1 - self.c}
+
+    def at_y(self, d):
+        return {"y": lax.rem(self.y + d, 4)}
+
+    def at_z(self, d):
+        z = lax.rem(self.z + d, 4)
+        return {"zl": lax.rem(z, 2), "zh": z // 2}
+
+
+class Net:
+    def __init__(self, send_sem, recv_sem, local_sem):
+        self.place = Place()
+        self.send_sem, self.recv_sem, self.local_sem = send_sem, recv_sem, local_sem
+        self.count, self.kept, self.locals, self.sent = 0, 0, [], []
+
+    def prepare(self, src, dst, device):
+        k = self.count
+        self.count += 1
+        return pltpu.make_async_remote_copy(
+            src_ref=src,
+            dst_ref=dst,
+            send_sem=self.send_sem.at[k],
+            recv_sem=self.recv_sem.at[k],
+            device_id=device,
+            device_id_type=MESH,
+        )
+
+    def send(self, src, dst, device):
+        copy = self.prepare(src, dst, device)
+        copy.start()
+        self.sent.append(copy)
+        return copy
+
+    def local(self, src, dst):
+        self.kept += 1
+        return pltpu.make_async_copy(src, dst, self.local_sem.at[self.kept - 1])
+
+    def keep(self, src, dst):
+        copy = self.local(src, dst)
+        copy.start()
+        self.locals.append(copy)
+
+    def settle(self):
+        for copy in self.locals:
+            copy.wait()
+        self.locals = []
+
+    def finish(self):
+        for copy in self.sent:
+            copy.wait_send()
+        self.settle()
+
+
+def meet(devices):
+    barrier = pltpu.get_barrier_semaphore()
+    for device in devices:
+        pl.semaphore_signal(barrier, inc=1, device_id=device, device_id_type=MESH)
+    pl.semaphore_wait(barrier, len(devices))
+
+
+def interleave(*jobs):
+    jobs = list(jobs)
+    while jobs:
+        for job in list(jobs):
+            try:
+                next(job)
+            except StopIteration:
+                jobs.remove(job)
+
+
+def team_peers(p):
+    return [p.at_x(1), p.at_x(3), p.sibling()]
+
+
+def team_all(p):
+    return [p.at_xc(d, k) for d in range(4) for k in range(2) if d + k]
+
+
+def group_peers(p):
+    return [p.at_y(d) for d in (1, 2, 3)] + [p.at_z(d) for d in (1, 2, 3)]
+
+
+def gather_team(net, own, out):
+    p = net.place
+    me, sib = 2 * p.x + p.c, p.sibling()
+    right, left = p.at_x(1), p.at_x(3)
+    t_l, t_r, t_2 = (2 * p.chip(d) + p.c for d in (3, 1, 2))
+    to_r = net.send(own, out.at[:, me], right)
+    to_l = net.send(own, out.at[:, me], left)
+    shared = [net.send(own, out.at[:, me], sib)]
+    net.keep(own, out.at[:, me])
+    yield
+    to_r.wait_recv()
+    on_r = net.send(out.at[0, t_l], out.at[0, t_l], right)
+    shared.append(net.send(out.at[:, t_l], out.at[:, t_l], sib))
+    to_l.wait_recv()
+    on_l = net.send(out.at[1, t_r], out.at[1, t_r], left)
+    shared.append(net.send(out.at[:, t_r], out.at[:, t_r], sib))
+    yield
+    on_r.wait_recv()
+    shared.append(net.send(out.at[0, t_2], out.at[0, t_2], sib))
+    on_l.wait_recv()
+    shared.append(net.send(out.at[1, t_2], out.at[1, t_2], sib))
+    yield
+    for copy in shared:
+        copy.wait_recv()
+
+
+GATHER_TEAM = 10
+
+
+def add(a, b):
+    return (a.astype(F32) + b.astype(F32)).astype(BF16)
+
+
+def scatter_team(net, part, got, total, from_l, from_r, all_l, all_r, finish):
+    p = net.place
+    sib, right, left = p.sibling(), p.at_x(1), p.at_x(3)
+    order = (2, 1, 3, 0)
+    swaps = [
+        net.send(part.at[:, 2 * p.chip(d) + 1 - p.c], got.at[:, p.chip(d)], sib) for d in order
+    ]
+
+    def pair(n):
+        swaps[n].wait_recv()
+        at = p.chip(order[n])
+        total[:, at] = add(part[:, 2 * at + p.c], got[:, at])
+        return at
+
+    yield
+    x_2 = pair(0)
+    half_r = net.send(total.at[0, x_2], from_l, right)
+    half_l = net.send(total.at[1, x_2], from_r, left)
+    x_r = pair(1)
+    rest_r = net.send(total.at[1, x_r], all_l.at[1], right)
+    x_l = pair(2)
+    rest_l = net.send(total.at[0, x_l], all_r.at[0], left)
+    pair(3)
+    yield
+    half_r.wait_recv()
+    total[0, x_r] = add(total[0, x_r], from_l[...])
+    last_r = net.send(total.at[0, x_r], all_l.at[0], right)
+    half_l.wait_recv()
+    total[1, x_l] = add(total[1, x_l], from_r[...])
+    last_l = net.send(total.at[1, x_l], all_r.at[1], left)
+    yield
+    for copy in (rest_r, rest_l, last_r, last_l):
+        copy.wait_recv()
+    finish(total[:, p.x].astype(F32) + all_l[...].astype(F32) + all_r[...].astype(F32))
+
+
+SCATTER_TEAM = 10
+
+
+def scatter_team_scratch(n, w):
+    return [
+        pltpu.VMEM((2, 4, n, w), BF16),
+        pltpu.VMEM((2, 4, n, w), BF16),
+        pltpu.VMEM((n, w), BF16),
+        pltpu.VMEM((n, w), BF16),
+        pltpu.VMEM((2, n, w), BF16),
+        pltpu.VMEM((2, n, w), BF16),
+    ]
+
+
+def chunk_rows(y, z, rows):
+    zl, zh = (z % 2, z // 2) if isinstance(z, int) else (lax.rem(z, 2), z // 2)
+    return pl.ds(pl.multiple_of(((zl * 4 + y) * 2 + zh) * rows, rows), rows)
+
+
+def gather_groups(net, own, out, cuts):
+    p = net.place
+    rows = own.shape[0]
+    lo, mid, hi = cuts
+    first, second = pl.ds(lo, mid - lo), pl.ds(mid, hi - mid)
+    net.keep(own, out.at[chunk_rows(p.y, p.z, rows)])
+
+    def spread(cols, y, z, devices, src=None):
+        place = out.at[chunk_rows(y, z, rows), cols]
+        return [net.send(place if src is None else src.at[:, cols], place, d) for d in devices]
+
+    ys, zs = [p.at_y(d) for d in (1, 3, 2)], [p.at_z(d) for d in (1, 3, 2)]
+    y_first = spread(first, p.y, p.z, ys, own)
+    z_first = spread(second, p.y, p.z, zs, own)
+    last = spread(first, p.y, p.z, zs, own) + spread(second, p.y, p.z, ys, own)
+    yield
+    for n, d in enumerate((1, 3, 2)):
+        y_first[n].wait_recv()
+        last += spread(first, lax.rem(p.y + 4 - d, 4), p.z, zs)
+        z_first[n].wait_recv()
+        last += spread(second, p.y, lax.rem(p.z + 4 - d, 4), ys)
+        yield
+    for copy in last:
+        copy.wait_recv()
+
+
+GATHER_GROUPS = 30
+
+
+def scatter_groups(net, part, out, cuts, z_got, z_sum, z_last, y_got, y_sum, y_last):
+    p = net.place
+    lo, mid, hi = cuts
+    first, second = pl.ds(lo, mid - lo), pl.ds(mid, hi - mid)
+    rows = z_sum.shape[1]
+    flat = len(part.shape) == 2
+    order = (2, 1, 3)
+    a = []
+    b = []
+    for n, d in enumerate(order):
+        z, y = lax.rem(p.z + d, 4), lax.rem(p.y + d, 4)
+        if flat:
+            for k in range(4):
+                a.append(net.send(part.at[chunk_rows(k, z, rows), first], z_got.at[n, k], p.at_z(d)))
+                b.append(net.send(part.at[chunk_rows(y, k, rows), second], y_got.at[n, k % 2, k // 2], p.at_y(d)))
+        else:
+            a.append(net.send(part.at[lax.rem(z, 2), :, z // 2, :, first], z_got.at[n], p.at_z(d)))
+            b.append(net.send(part.at[:, y, :, :, second], y_got.at[n], p.at_y(d)))
+
+    def own(y, zl, zh, cols):
+        if flat:
+            return part[chunk_rows(y, zh * 2 + zl, rows), cols].astype(F32)
+        return part[zl, y, zh, :, cols].astype(F32)
+
+    yield
+    for copy in a:
+        copy.wait_recv()
+    for y in range(4):
+        t = own(y, p.zl, p.zh, first)
+        for n in range(3):
+            t = t + z_got[n, y].astype(F32)
+        z_sum[y] = t.astype(BF16)
+    a = [
+        net.send(z_sum.at[lax.rem(p.y + d, 4)], z_last.at[n], p.at_y(d)) for n, d in enumerate(order)
+    ]
+    yield
+    for copy in b:
+        copy.wait_recv()
+    for zl in range(2):
+        for zh in range(2):
+            t = own(p.y, zl, zh, second)
+            for n in range(3):
+                t = t + y_got[n, zl, zh].astype(F32)
+            y_sum[zl, zh] = t.astype(BF16)
+    b = []
+    for n, d in enumerate(order):
+        z = lax.rem(p.z + d, 4)
+        b.append(net.send(y_sum.at[lax.rem(z, 2), z // 2], y_last.at[n], p.at_z(d)))
+    yield
+    for copy in a:
+        copy.wait_recv()
+    t = z_sum[p.y].astype(F32)
+    for n in range(3):
+        t = t + z_last[n].astype(F32)
+    out[:, first] = t.astype(out.dtype)
+    yield
+    for copy in b:
+        copy.wait_recv()
+    t = y_sum[p.zl, p.zh].astype(F32)
+    for n in range(3):
+        t = t + y_last[n].astype(F32)
+    out[:, second] = t.astype(out.dtype)
+
+
+SCATTER_GROUPS = 12
+SCATTER_GROUPS_FLAT = 30
+
+
+def scatter_groups_scratch(r, cuts):
+    a, b = cuts[1] - cuts[0], cuts[2] - cuts[1]
+    return [
+        pltpu.VMEM((3, 4, r, a), BF16),
+        pltpu.VMEM((4, r, a), BF16),
+        pltpu.VMEM((3, r, a), BF16),
+        pltpu.VMEM((3, 2, 2, r, b), BF16),
+        pltpu.VMEM((2, 2, r, b), BF16),
+        pltpu.VMEM((3, r, b), BF16),
+    ]
+
+
+def sems(remote, local):
+    return [
+        pltpu.SemaphoreType.DMA((remote,)),
+        pltpu.SemaphoreType.DMA((remote,)),
+        pltpu.SemaphoreType.DMA((max(local, 1),)),
+    ]
+
+
+def params(collective_id):
+    return pltpu.CompilerParams(
+        collective_id=collective_id, has_side_effects=True, vmem_limit_bytes=VM
+    )
+
+
 EPS_NORM = 1e-05
 EPS_UNIT = 1e-06
-GROUPS = ("zl", "y", "zh")
-TEAM = ("x", "c")
-ALL = GROUPS + TEAM
+SHAPE = jax.ShapeDtypeStruct
+
+
+def all_to_team(net, packs, got):
+    p = net.place
+    me = 2 * p.x + p.c
+    net.keep(packs.at[me], got.at[me])
+    copies = []
+    for d in (2, 1, 3, 0):
+        for k in (1, 0):
+            if d + k:
+                to = 2 * p.chip(d) + lax.rem(p.c + k, 2)
+                copies.append(net.send(packs.at[to], got.at[me], p.at_xc(d, k)))
+    yield
+    for copy in copies:
+        copy.wait_recv()
+
+
+def start_kernel(packs, tokens, grad_out, got, x_rows, g_rows, *sem):
+    net = Net(*sem)
+    p = net.place
+    other = {"zh": 1 - p.zh}
+    meet(team_all(p) + [other])
+    swaps = []
+    for src, dst in ((tokens, x_rows), (grad_out, g_rows)):
+        net.keep(src.at[p.zh], dst.at[p.zh])
+        swaps.append(net.send(src.at[1 - p.zh], dst.at[p.zh], other))
+    interleave(all_to_team(net, packs, got))
+    for copy in swaps:
+        copy.wait_recv()
+    net.finish()
+
+
+def start(packs, tokens, grad_out):
+    rows = SHAPE(tokens.shape, BF16)
+    return pl.pallas_call(
+        start_kernel,
+        out_shape=[SHAPE(packs.shape, BF16), rows, rows],
+        in_specs=[ANY] * 3,
+        out_specs=[ANY] * 3,
+        scratch_shapes=sems(9, 3),
+        compiler_params=params(1),
+        name="start",
+    )(packs, tokens, grad_out)
+
+
+def lanes(at):
+    return pl.ds(pl.multiple_of(at * HD, HD), HD)
+
+
+OUT_AT = 8
+
+
+def trade_out(net, whole, w_out):
+    p = net.place
+    copies = []
+    for d in (2, 1, 3, 0):
+        for k in (1, 0):
+            xd, cd = p.chip(d), lax.rem(p.c + k, 2)
+            row_a, row_b = lanes(3 * xd + 2 * cd), lanes(3 * xd + 1)
+            row_c = lanes(3 * xd + jnp.where(p.c == 0, 2 * cd, 1))
+            col_a, col_b = lanes(3 * p.x + 2 * p.c), lanes(3 * p.x + 1)
+            moves = (
+                (whole.at[row_a, pl.ds(OUT_AT * HD, HD)], w_out.at[pl.ds(0, HD), col_a]),
+                (whole.at[row_b, pl.ds(OUT_AT * HD, HD)], w_out.at[pl.ds(HD, HD), col_a]),
+                (whole.at[row_c, pl.ds((OUT_AT + 1) * HD, HD)], w_out.at[lanes(p.c), col_b]),
+            )
+            for src, dst in moves:
+                if d + k:
+                    copies.append(net.send(src, dst, p.at_xc(d, k)))
+                else:
+                    net.keep(src, dst)
+    yield
+    for copy in copies:
+        copy.wait_recv()
+
+
+def gather_kernel(cuts, x_rows, g_rows, own, x_all, g_all, whole, w_out, *sem):
+    net = Net(*sem)
+    p = net.place
+    meet(team_all(p) + group_peers(p))
+    interleave(
+        gather_team(net, x_rows, x_all),
+        gather_groups(net, own, whole, cuts),
+        gather_team(net, g_rows, g_all),
+    )
+    net.settle()
+    interleave(trade_out(net, whole, w_out))
+    net.finish()
+
+
+def gather_all(x_rows, g_rows, own):
+    rows, cols = own.shape
+    two, n, width = x_rows.shape
+    every = SHAPE((two, 8, n, width), BF16)
+    return pl.pallas_call(
+        functools.partial(gather_kernel, (0, 768, cols)),
+        out_shape=[every, every, SHAPE((16 * rows, cols), BF16), SHAPE((2 * HD, width), BF16)],
+        in_specs=[ANY] * 3,
+        out_specs=[ANY] * 4,
+        scratch_shapes=sems(2 * GATHER_TEAM + GATHER_GROUPS + 21, 6),
+        compiler_params=params(2),
+        name="gather_all",
+    )(x_rows, g_rows, own)
+
+
+def ffn_in_kernel(cuts, part, x_rows, gain, own_ffn, own_down, hidden, ffn_all, w_ffn, w_down, normed, *rest):
+    net = Net(*rest[-3:])
+    p = net.place
+    meet(team_peers(p) + group_peers(p))
+
+    def finish(branch):
+        h = x_rows[...].astype(F32) + branch
+        hidden[...] = h
+        scale = lax.rsqrt(jnp.mean(h * h, axis=-1, keepdims=True) + EPS_NORM)
+        normed[...] = (h * scale * gain[...][None]).astype(BF16)
+
+    def team():
+        yield from scatter_team(net, part, *rest[:-3], finish)
+        yield from gather_team(net, normed, ffn_all)
+
+    interleave(
+        team(),
+        gather_groups(net, own_ffn, w_ffn, cuts[0]),
+        gather_groups(net, own_down, w_down, cuts[1]),
+    )
+    net.finish()
+
+
+def ffn_in(part, x_rows, gain, own_ffn, own_down):
+    two, n, width = x_rows.shape
+    cuts = [(0, a.shape[1] // 2, a.shape[1]) for a in (own_ffn, own_down)]
+    return pl.pallas_call(
+        functools.partial(ffn_in_kernel, cuts),
+        out_shape=[
+            SHAPE((two, n, width), F32),
+            SHAPE((two, 8, n, width), BF16),
+            SHAPE((16 * own_ffn.shape[0], own_ffn.shape[1]), BF16),
+            SHAPE((16 * own_down.shape[0], own_down.shape[1]), BF16),
+        ],
+        in_specs=[VMEM, VMEM, VMEM, ANY, ANY],
+        out_specs=[VMEM, ANY, ANY, ANY],
+        scratch_shapes=[pltpu.VMEM((two, n, width), BF16)]
+        + scatter_team_scratch(n, width)
+        + sems(SCATTER_TEAM + GATHER_TEAM + 2 * GATHER_GROUPS, 3),
+        compiler_params=params(3),
+        name="ffn_in",
+    )(part, x_rows, gain, own_ffn, own_down)
+
+
+def norm_back(v, gain, d_normed):
+    scale = lax.rsqrt(jnp.mean(v * v, axis=-1, keepdims=True) + EPS_NORM)
+    unit = v * scale
+    d_unit = d_normed * gain
+    d_v = scale * (d_unit - unit * jnp.mean(d_unit * unit, axis=-1, keepdims=True))
+    return d_v, d_normed * unit
+
+
+def ffn_back_kernel(cuts, part, hidden, gain, g_rows, d_ffn, d_down, d_hidden, d_gain, branch_all, ffn_sum, down_sum, branch, *rest):
+    team_scratch, ffn_scratch, down_scratch = rest[:6], rest[6:12], rest[12:18]
+    net = Net(*rest[-3:])
+    p = net.place
+    meet(team_peers(p) + group_peers(p))
+
+    def finish(d_normed):
+        d_h, d_g = norm_back(hidden[...], gain[...][None], d_normed)
+        d_h = d_h + g_rows[...].astype(F32)
+        d_hidden[...] = d_h
+        branch[...] = d_h.astype(BF16)
+        d_gain[...] = jnp.sum(jnp.sum(d_g, axis=0), axis=0, keepdims=True)
+
+    def team():
+        yield from scatter_team(net, part, *team_scratch, finish)
+        yield from gather_team(net, branch, branch_all)
+
+    interleave(
+        team(),
+        scatter_groups(net, d_ffn, ffn_sum, cuts[0], *ffn_scratch),
+        scatter_groups(net, d_down, down_sum, cuts[1], *down_scratch),
+    )
+    net.finish()
+
+
+def by_group(a):
+    return a.reshape(2, 4, 2, a.shape[0] // 16, a.shape[1])
+
+
+def ffn_back(part, hidden, gain, g_rows, d_ffn, d_down):
+    two, n, width = hidden.shape
+    d_ffn, d_down = by_group(d_ffn), by_group(d_down)
+    sizes = [a.shape[3:] for a in (d_ffn, d_down)]
+    cuts = [(0, w // 2, w) for _, w in sizes]
+    return pl.pallas_call(
+        functools.partial(ffn_back_kernel, cuts),
+        out_shape=[
+            SHAPE((two, n, width), F32),
+            SHAPE((1, width), F32),
+            SHAPE((two, 8, n, width), BF16),
+            SHAPE(sizes[0], BF16),
+            SHAPE(sizes[1], F32),
+        ],
+        in_specs=[VMEM] * 6,
+        out_specs=[VMEM, VMEM, ANY, VMEM, VMEM],
+        scratch_shapes=[pltpu.VMEM((two, n, width), BF16)]
+        + scatter_team_scratch(n, width)
+        + scatter_groups_scratch(sizes[0][0], cuts[0])
+        + scatter_groups_scratch(sizes[1][0], cuts[1])
+        + sems(SCATTER_TEAM + GATHER_TEAM + 2 * SCATTER_GROUPS, 1),
+        compiler_params=params(4),
+        name="ffn_back",
+    )(part, hidden, gain, g_rows, d_ffn, d_down)
+
+
+def trade_out_back(net, d_out, whole):
+    p = net.place
+    rows, middle, own = [], [], []
+    cases = [(d, k) for d in (2, 1, 3, 0) for k in (1, 0)]
+    for d, k in cases:
+        xd, cd = p.chip(d), lax.rem(p.c + k, 2)
+        for side, col in enumerate((lanes(3 * xd + 2 * cd), lanes(3 * xd + 1))):
+            src = d_out.at[pl.ds(0, HD), col]
+            dst = whole.at[lanes(3 * p.x + 2 * p.c), pl.ds(side * HD, HD)]
+            if d + k:
+                rows.append(net.send(src, dst, p.at_xc(d, k)))
+            else:
+                own.append(net.local(src, dst))
+                own[-1].start()
+    for d, k in cases:
+        xd, cd = p.chip(d), lax.rem(p.c + k, 2)
+        for side, col in enumerate((lanes(3 * xd + 2 * cd), lanes(3 * xd + 1))):
+            src = d_out.at[pl.ds(HD, HD), col]
+            dst = whole.at[lanes(3 * p.x + 1), pl.ds(side * HD, HD)]
+            if d + k:
+                middle.append((k, net.prepare(src, dst, p.at_xc(d, k))))
+            else:
+                middle.append((-1, net.local(src, dst)))
+
+    @pl.when(p.c == 0)
+    def _():
+        for _, copy in middle:
+            copy.start()
+
+    yield
+    for copy in rows:
+        copy.wait_recv()
+    for copy in own:
+        copy.wait()
+    for core in range(2):
+
+        @pl.when(p.c == core)
+        def _(core=core):
+            for k, copy in middle:
+                if k == core:
+                    copy.wait_recv()
+
+    @pl.when(p.c == 0)
+    def _():
+        for k, copy in middle:
+            if k < 0:
+                copy.wait()
+            else:
+                copy.wait_send()
+
+    yield
+
+
+TRADE_BACK = 28
+
+
+def last_kernel(cuts, part_n, part_o, x_rows, hidden, d_hidden, gain, d_heads, d_out, out_rows, d_rows, heads_sum, out_sum, whole, *rest):
+    n_scratch, o_scratch, h_scratch, w_scratch = rest[:6], rest[6:12], rest[12:18], rest[18:24]
+    net = Net(*rest[-3:])
+    p = net.place
+    meet(team_all(p) + group_peers(p))
+
+    def finish_n(d_normed):
+        d_x, _ = norm_back(x_rows[...].astype(F32), gain[...][None], d_normed)
+        d_rows[...] = (d_x + d_hidden[...]).astype(BF16)
+
+    def finish_o(branch):
+        out_rows[...] = (hidden[...] + branch).astype(BF16)
+
+    def out_grad():
+        yield from trade_out_back(net, d_out, whole)
+        yield from scatter_groups(net, whole, out_sum, cuts[1], *w_scratch)
+
+    interleave(
+        out_grad(),
+        scatter_groups(net, d_heads, heads_sum, cuts[0], *h_scratch),
+        scatter_team(net, part_n, *n_scratch, finish_n),
+        scatter_team(net, part_o, *o_scratch, finish_o),
+    )
+    net.finish()
+
+
+def last_sums(part_n, part_o, x_rows, hidden, d_hidden, gain, d_heads, d_out):
+    two, n, width = hidden.shape
+    d_heads = by_group(d_heads)
+    r, w = d_heads.shape[3:]
+    cuts = [(0, 640, w), (0, HD, 2 * HD)]
+    return pl.pallas_call(
+        functools.partial(last_kernel, cuts),
+        out_shape=[
+            SHAPE((two, n, width), BF16),
+            SHAPE((two, n, width), BF16),
+            SHAPE((r, w), BF16),
+            SHAPE((r, 2 * HD), BF16),
+        ],
+        in_specs=[VMEM] * 8,
+        out_specs=[VMEM] * 4,
+        scratch_shapes=[pltpu.VMEM((width, 2 * HD), BF16)]
+        + scatter_team_scratch(n, width) * 2
+        + scatter_groups_scratch(r, cuts[0])
+        + scatter_groups_scratch(r, cuts[1])
+        + sems(2 * SCATTER_TEAM + SCATTER_GROUPS + SCATTER_GROUPS_FLAT + TRADE_BACK, 4),
+        compiler_params=params(5),
+        name="last_sums",
+    )(part_n, part_o, x_rows, hidden, d_hidden, gain, d_heads, d_out)
+
+
+def end_kernel(packs, out_rows, d_rows, got, output, d_tokens, *sem):
+    net = Net(*sem)
+    p = net.place
+    other = {"zh": 1 - p.zh}
+    meet(team_all(p) + [other])
+    swaps = []
+    for src, dst in ((out_rows, output), (d_rows, d_tokens)):
+        net.keep(src.at[p.zh], dst.at[p.zh])
+        swaps.append(net.send(src.at[1 - p.zh], dst.at[p.zh], other))
+    interleave(all_to_team(net, packs, got))
+    for copy in swaps:
+        copy.wait_recv()
+    net.finish()
+
+
+def end(packs, out_rows, d_rows):
+    rows = SHAPE(out_rows.shape, BF16)
+    return pl.pallas_call(
+        end_kernel,
+        out_shape=[SHAPE(packs.shape, BF16), rows, rows],
+        in_specs=[ANY] * 3,
+        out_specs=[ANY] * 3,
+        scratch_shapes=sems(9, 3),
+        compiler_params=params(6),
+        name="end",
+    )(packs, out_rows, d_rows)
+
+
+def dot_nn(a, b):
+    return lax.dot_general(a, b, (((1,), (0,)), ((), ())), preferred_element_type=F32)
+
+
+def dot_nt(a, b):
+    return lax.dot_general(a, b, (((1,), (1,)), ((), ())), preferred_element_type=F32)
+
+
+def dot_tn(a, b):
+    return lax.dot_general(a, b, (((0,), (0,)), ((), ())), preferred_element_type=F32)
 
 
 def rms_scale(values, gain_vec):
     return (
         values * lax.rsqrt(jnp.mean(values * values, axis=-1, keepdims=True) + EPS_NORM) * gain_vec
     )
-
-
-def dot_nn(a, b):
-    return lax.dot_general(a, b, (((1,), (0,)), ((), ())), preferred_element_type=F32)
-
-
-def dot_nt(a, b):
-    return lax.dot_general(a, b, (((1,), (1,)), ((), ())), preferred_element_type=F32)
-
-
-def dot_tn(a, b):
-    return lax.dot_general(a, b, (((0,), (0,)), ((), ())), preferred_element_type=F32)
-
-
-def gather_rows(block):
-    width = block.shape[1]
-    whole = lax.all_gather(block.reshape(2, -1, width), TEAM, axis=1)
-    return whole.reshape(-1, width)
-
-
-def scatter_rows(partial):
-    width = partial.shape[1]
-    parts = partial.astype(BF16).reshape(2, 8, -1, width)
-    mine = lax.psum_scatter(parts, TEAM, scatter_dimension=1, tiled=False)
-    return mine.reshape(-1, width).astype(F32)
 
 
 def path_vectors(current, conv_w, same_doc):
@@ -307,6 +955,17 @@
     heads = conved.reshape(current.shape[0], -1, HD)
     unit = heads * lax.rsqrt(jnp.sum(heads * heads, axis=-1, keepdims=True) + EPS_UNIT)
     return unit.reshape(current.shape)
+
+
+def split_rows(partial):
+    return partial.astype(BF16).reshape(2, 8, -1, partial.shape[1])
+
+
+def pad_rows(a, rows):
+    return jnp.pad(a, ((0, 0), (0, rows - a.shape[1]), (0, 0)))
+
+
+HEADS_W, OUT_W, SMALL_W = 8 * HD, 2 * HD, HD
 
 
 def per_device(
@@ -327,47 +986,34 @@
     grad_out,
 ):
     zh, chip, core = lax.axis_index("zh"), lax.axis_index("x"), lax.axis_index("c")
-    dp = lax.axis_index("zl") * 4 + lax.axis_index("y")
     width = tokens.shape[2]
     share = w_query.shape[0]
-    first = zh == 0
     head_a, head_b = 3 * chip + 2 * core, 3 * chip + 1
-
-    pair = jnp.stack([tokens, grad_out])
-    mine = jnp.where(first, pair[:, 0], pair[:, 1])
-    other = jnp.where(first, pair[:, 1], pair[:, 0])
-    got = lax.ppermute(other, "zh", [(0, 1), (1, 0)])
-    halves = jnp.stack([jnp.where(first, mine, got), jnp.where(first, got, mine)], axis=1)
-    x_rows = halves[0].reshape(-1, width)
-    g_rows = halves[1].reshape(-1, width)
-    doc_rows = jnp.cumsum(doc_start, axis=1)
-    docs = jnp.where(first, doc_rows[0], doc_rows[1])
-
-    small = jnp.concatenate(
-        [gain_attn[:, None], gain_ffn[:, None], conv_path.T, w_beta], axis=1
-    )
-    small = lax.all_gather(small.reshape(1, -1), ALL, axis=0, tiled=True)
-    small = small.reshape(width, -1)
-    gain_a, gain_f = small[:, 0].astype(F32), small[:, 1].astype(F32)
-    conv_full, beta_full = small[:, 2:6].T.astype(F32), small[:, 6:]
-    kinds = jnp.stack([w_query, w_key, w_value, w_path], axis=1).reshape(share, 4, 4, 3, HD)
+    owns_b = core == 0
+
+    small = jnp.concatenate([gain_attn[:, None], gain_ffn[:, None], conv_path.T, w_beta], axis=1)
+    small = jnp.pad(small, ((0, 0), (0, SMALL_W - small.shape[1])))
+    small = jnp.broadcast_to(small[None], (8, share, SMALL_W))
+    kinds = jnp.stack([w_query, w_key, w_value, w_path, w_out], axis=1).reshape(share, 5, 4, 3, HD)
     slot_a = jnp.concatenate([kinds[:, :, :, 0:1], kinds[:, :, :, 2:3]], axis=3)
     slot_b = jnp.broadcast_to(kinds[:, :, :, 1:2], slot_a.shape)
     heads_pack = jnp.stack([slot_a, slot_b], axis=4).transpose(2, 3, 0, 1, 4, 5)
     heads_pack = heads_pack.reshape(8, share, -1)
     ffn_pack = jnp.stack([w_gate, w_up], axis=1).reshape(share, 2, 16, 8, 32)
     ffn_pack = ffn_pack.transpose(3, 0, 1, 2, 4).reshape(8, share, -1)
-    packs = jnp.concatenate([heads_pack, ffn_pack], axis=2)
-    packs = lax.all_to_all(packs, TEAM, split_axis=0, concat_axis=0, tiled=True)
-    packs = packs.reshape(8 * share, -1)
-    w_heads = lax.all_gather(packs[:, : 8 * HD], GROUPS, axis=0, tiled=True)
-    w_out_full = lax.all_gather(w_out, ALL, axis=0, tiled=True)
-    w_ffn = lax.all_gather(packs[:, 8 * HD :], GROUPS, axis=0, tiled=True)
-    w_down_t = lax.all_gather(w_down, GROUPS, axis=0, tiled=True)
-    out_a = lax.dynamic_slice_in_dim(w_out_full, head_a * HD, HD, 0)
-    out_b = lax.dynamic_slice_in_dim(w_out_full, head_b * HD, HD, 0)
-    out_b = jnp.where(core == 0, out_b, jnp.zeros_like(out_b))
-    w_out_t = jnp.concatenate([out_a, out_b], axis=0)
+    packs = pad_rows(jnp.concatenate([heads_pack, small, ffn_pack], axis=2), 16)
+    packs, x_rows, g_rows = start(packs, tokens, grad_out)
+    packs = packs[:, :share].reshape(8 * share, -1)
+    first_w = HEADS_W + OUT_W + SMALL_W
+    x_all, g_all, whole, w_out_t = gather_all(x_rows, g_rows, packs[:, :first_w])
+    w_heads = whole[:, :HEADS_W]
+    small = whole[:, HEADS_W + OUT_W :]
+    gain_a, gain_f = small[:, 0].astype(F32), small[:, 1].astype(F32)
+    conv_full, beta_full = small[:, 2:6].T.astype(F32), small[:, 6:18]
+    x_all = x_all.reshape(SEQ, width)
+    g_all = g_all.reshape(SEQ, width)
+    doc_rows = jnp.cumsum(doc_start, axis=1)
+    docs = jnp.where(zh == 0, doc_rows[0], doc_rows[1])
 
     def two_heads(full, size):
         return jnp.concatenate(
@@ -381,8 +1027,11 @@
     def back_to_all(part, size):
         full = jnp.zeros((part.shape[0], 12 * size), F32)
         full = lax.dynamic_update_slice_in_dim(full, part[:, :size], head_a * size, 1)
-        own_b = jnp.where(core == 0, part[:, size:], 0.0)
+        own_b = jnp.where(owns_b, part[:, size:], 0.0)
         return lax.dynamic_update_slice_in_dim(full, own_b, head_b * size, 1)
+
+    def own_heads(v):
+        return jnp.where((jnp.arange(2 * HD) < HD) | owns_b, v, 0.0)
 
     w_beta_t = two_heads(beta_full, 1)
     conv_t = two_heads(conv_full, HD)
@@ -391,10 +1040,7 @@
         for tap in range(4)
     ]
 
-    x_f = x_rows.astype(F32)
-    normed = rms_scale(x_f, gain_a).astype(BF16)
-    normed_all = gather_rows(normed)
-    g_all = gather_rows(g_rows)
+    normed_all = rms_scale(x_all.astype(F32), gain_a).astype(BF16)
     qkvp = dot_nn(normed_all, w_heads).astype(BF16)
     beta_raw = dot_nn(normed_all, w_beta_t)
     betas = (2.0 * jax.nn.sigmoid(beta_raw)).T
@@ -404,102 +1050,98 @@
     vec = vec_f.astype(BF16)
     bcol, brow = betas[:, :, None], betas[:, None, :]
     o, *saved = attn_fwd(qkvp, vec, bcol, brow, docs[:, None], docs[None, :])
-    mixed = o.astype(BF16)
-    hidden = x_f + scatter_rows(dot_nn(mixed, w_out_t))
-    normed_ffn = rms_scale(hidden, gain_f).astype(BF16)
-    ffn_all = gather_rows(normed_ffn)
+    mixed = own_heads(o).astype(BF16)
+    hidden, ffn_all, w_ffn, w_down_t = ffn_in(
+        split_rows(dot_nn(mixed, w_out_t)), x_rows, gain_f[None], packs[:, first_w:], w_down
+    )
+    ffn_all = ffn_all.reshape(SEQ, width)
     gate_up = dot_nn(ffn_all, w_ffn)
+    half = gate_up.shape[1] // 2
 
     def gated(pre):
-        return jax.nn.silu(pre[:, :512]) * pre[:, 512:]
+        return jax.nn.silu(pre[:, :half]) * pre[:, half:]
 
     act_f, act_pull = jax.vjp(gated, gate_up)
     act = act_f.astype(BF16)
-    out_rows = (hidden + scatter_rows(dot_nn(act, w_down_t))).astype(BF16)
+    out_part = split_rows(dot_nn(act, w_down_t))
 
     (d_gate_up,) = act_pull(dot_nt(g_all, w_down_t))
     d_gate_up = d_gate_up.astype(BF16)
-    d_normed_ffn = scatter_rows(dot_nt(d_gate_up, w_ffn))
-    _, ffn_pull = jax.vjp(rms_scale, hidden, gain_f)
-    d_hidden, d_gain_ffn = ffn_pull(d_normed_ffn)
-    d_hidden = d_hidden + g_rows.astype(F32)
-    branch_all = gather_rows(d_hidden.astype(BF16))
-    d_mixed = dot_nt(branch_all, w_out_t)
+    d_hidden, d_gain_ffn, branch_all, d_ffn, d_down = ffn_back(
+        split_rows(dot_nt(d_gate_up, w_ffn)),
+        hidden,
+        gain_f[None],
+        g_rows,
+        dot_tn(ffn_all, d_gate_up).astype(BF16),
+        dot_tn(act, g_all).astype(BF16),
+    )
+    branch_all = branch_all.reshape(SEQ, width)
+    d_mixed = own_heads(dot_nt(branch_all, w_out_t))
     d_q, d_k, d_v, d_vec, d_bc, d_br = attn_bwd(qkvp, vec, bcol, brow, o, d_mixed, saved)
     d_path, d_conv = vec_pull(d_vec)
     d_betas = (d_bc[:, :, 0] + d_br[:, 0, :]) * betas * (1.0 - 0.5 * betas)
     d_beta = d_betas.T.astype(BF16)
     d_qkvp = jnp.concatenate([d_q, d_k, d_v, d_path.astype(BF16)], axis=1)
-    d_normed = scatter_rows(dot_nt(d_qkvp, w_heads) + dot_nt(d_beta, w_beta_t))
-    _, norm_pull = jax.vjp(rms_scale, x_f, gain_a)
-    d_x, d_gain_attn = norm_pull(d_normed)
-    d_rows = (d_x + d_hidden).astype(BF16)
-
-    def sum_rows(grad):
-        return lax.psum_scatter(grad.astype(BF16), GROUPS, scatter_dimension=0, tiled=True)
-
-    d_down = sum_rows(dot_tn(act, g_all)).astype(F32)
-    d_ffn = sum_rows(dot_tn(ffn_all, d_gate_up))
-    d_out = lax.psum(dot_tn(mixed, branch_all).astype(BF16), GROUPS)
-    d_heads = sum_rows(dot_tn(normed_all, d_qkvp))
-    none = jnp.zeros((HD, width), BF16)
-    own = core == 0
-    chip_rows = jnp.concatenate(
+    norm_part = (dot_nt(d_qkvp, w_heads) + dot_nt(d_beta, w_beta_t)).astype(BF16)
+    d_gain_attn = jnp.sum(norm_part.astype(F32) * normed_all.astype(F32), axis=0) / gain_a
+
+    small_back = jnp.concatenate(
         [
-            jnp.where(own, d_out[:HD], none),
-            jnp.where(own, d_out[HD:], none),
-            jnp.where(own, none, d_out[:HD]),
+            d_gain_attn[:, None],
+            d_gain_ffn.T,
+            back_to_all(d_conv, HD).T,
+            back_to_all(dot_tn(normed_all, d_beta), 1),
         ],
-        axis=0,
-    )
-    window = lax.dynamic_slice_in_dim(chip_rows, (dp % 2) * 192 + zh * 96, 96, 0)
-    window = jnp.where(chip == dp // 2, window, jnp.zeros_like(window))
-    back = jnp.concatenate([d_heads, d_ffn, window], axis=1).reshape(8, share, -1)
-    back = lax.all_to_all(back, TEAM, split_axis=0, concat_axis=0, tiled=True)
-    d_w_out = jnp.sum(back[:, :, 16 * HD :].astype(F32), axis=0)
-    heads_back = back[:, :, : 8 * HD].reshape(4, 2, share, 4, 2, HD)
+        axis=1,
+    ).astype(BF16)
+    small_back = jnp.pad(small_back, ((0, 0), (0, SMALL_W - small_back.shape[1])))
+    d_heads = dot_tn(normed_all, d_qkvp).astype(BF16)
+    out_rows, d_rows, heads_sum, out_sum = last_sums(
+        split_rows(norm_part),
+        out_part,
+        x_rows,
+        hidden,
+        d_hidden,
+        gain_a[None],
+        jnp.concatenate([d_heads, small_back], axis=1),
+        dot_tn(mixed, branch_all).astype(BF16),
+    )
+    packs = jnp.concatenate([heads_sum, out_sum, d_ffn], axis=1).reshape(8, share, -1)
+    packs, output, d_tokens = end(pad_rows(packs, 16), out_rows, d_rows)
+    packs = packs[:, :share]
+    small = jnp.sum(packs[:, :, HEADS_W : HEADS_W + SMALL_W].astype(F32), axis=0)
+    at = HEADS_W + SMALL_W
+    heads_back = jnp.concatenate([packs[:, :, :HEADS_W], packs[:, :, at : at + OUT_W]], axis=2)
+    heads_back = heads_back.reshape(4, 2, share, 5, 2, HD)
     by_head = jnp.stack(
         [heads_back[:, 0, :, :, 0], heads_back[:, 0, :, :, 1], heads_back[:, 1, :, :, 0]], axis=1
     )
-    by_kind = by_head.transpose(3, 2, 0, 1, 4).reshape(4, share, width).astype(F32)
-    ffn_back = back[:, :, 8 * HD : 16 * HD].reshape(8, share, 2, 16, 32)
-    ffn_back = ffn_back.transpose(2, 1, 3, 0, 4).reshape(2, share, -1).astype(F32)
-
-    d_beta_w = back_to_all(dot_tn(normed_all, d_beta), 1)
-    small_back = jnp.concatenate(
-        [d_gain_attn[:, None], d_gain_ffn[:, None], back_to_all(d_conv, HD).T, d_beta_w], axis=1
-    )
-    small_back = lax.psum_scatter(
-        small_back.reshape(128, -1), ALL, scatter_dimension=0, tiled=True
-    ).reshape(share, -1)
-
-    pair = jnp.stack([out_rows, d_rows]).reshape(2, 2, -1, width)
-    mine = jnp.where(first, pair[:, 0], pair[:, 1])
-    other = jnp.where(first, pair[:, 1], pair[:, 0])
-    got = lax.ppermute(other, "zh", [(0, 1), (1, 0)])
-    rows = jnp.stack([jnp.where(first, mine, got), jnp.where(first, got, mine)], axis=1)
+    by_kind = by_head.transpose(3, 2, 0, 1, 4).reshape(5, share, width).astype(F32)
+    ffn_sum = packs[:, :, at + OUT_W :].reshape(8, share, 2, 16, 32)
+    ffn_sum = ffn_sum.transpose(2, 1, 3, 0, 4).reshape(2, share, -1).astype(F32)
     return (
-        rows[0],
-        rows[1],
-        small_back[:, 0],
+        output,
+        d_tokens,
+        small[:, 0],
         by_kind[0],
         by_kind[1],
         by_kind[2],
         by_kind[3],
-        small_back[:, 2:6].T,
-        small_back[:, 6:],
-        d_w_out,
-        small_back[:, 1],
-        ffn_back[0],
-        ffn_back[1],
+        small[:, 2:6].T,
+        small[:, 6:18],
+        by_kind[4],
+        small[:, 1],
+        ffn_sum[0],
+        ffn_sum[1],
         d_down,
     )
 
 
 def solution(mesh):
-    fine = Mesh(mesh.devices.reshape(2, 4, 2, 4, 2), ("zl", "y", "zh", "x", "c"))
-    dp, ctx = ("zl", "y"), ("zh", "x", "c")
-    rows, flat, mat, taps = P(dp, ctx, None), P(ALL), P(ALL, None), P(None, ALL)
+    names = ("zl", "y", "zh", "x", "c")
+    fine = Mesh(mesh.devices.reshape(2, 4, 2, 4, 2), names)
+    dp, ctx = names[:2], names[2:]
+    rows, flat, mat, taps = P(dp, ctx, None), P(names), P(names, None), P(None, names)
     return jax.shard_map(
         per_device,
         mesh=fine,

time: 1460 us -> 463 us (0.32)
  waiting for transfers between devices: 1000 us -> 0 us
  Pallas kernels: 36.4 us -> 298 us
  blocking collectives: 194 us -> 0 us
  starting transfers between devices: 23.7 us -> 0 us
    all_gather x8 -> x0, waiting for transfers between devices: 475 us -> none  [the longest x1 169 us: per_device(): w_out_full = lax.all_gather(w_out, ALL, axis=0, tiled=True)]
    reduce_scatter x7 -> x0, waiting for transfers between devices: 298 us -> none  [the longest x3 168 us: sum_rows(): lax.psum_scatter(grad.astype(BF16), GROUPS, scatter_dimension=0, tiled=True)]
    pallas_call x0 -> x6, Pallas kernels: none -> 262 us  [the longest x1 63.2 us: last_sums(): pl.pallas_call(functools.partial(last_kernel, cuts), out_shape=[SHAPE((tw...]
    all_gather x1 -> x0, blocking collectives: 176 us -> none  [per_device(): small = lax.all_gather(small.reshape(1, -1), ALL, axis=0, tiled=True)]
    unnamed x18 -> x0, waiting for transfers between devices: 139 us -> none
    psum x1 -> x0, waiting for transfers between devices: 90.5 us -> none  [per_device(): d_out = lax.psum(dot_tn(mixed, branch_all).astype(BF16), GROUPS)]
    all_to_all x1 -> x0, blocking collectives: 18 us -> none  [per_device(): packs = lax.all_to_all(packs, TEAM, split_axis=0, concat_axis=0, tiled=True)]
    all_to_all x1 -> x0, starting transfers between devices: 15.1 us -> none  [per_device(): back = lax.all_to_all(back, TEAM, split_axis=0, concat_axis=0, tiled=True)]
  transfers between devices with their start and end apart: 20 -> 0, of which waited for: 16 -> 0; matrix products, arithmetic and copies ran while one was open for 9% -> 0% of each run, Pallas kernels for 3% -> 0%
where the time goes in v2:
time: 463 us; the launch traced here: 456 us
  Pallas kernels  298 us (64%)
  matrix products  60.6 us (13%)
  local copies, waits for them, and re-layouts  56.1 us (12%)
  other arithmetic  39.1 us (8%)
    pallas_call x1, Pallas kernels, last_sums(): pl.pallas_call(functools.partial(last_kernel, cuts), out_shape=[SHAPE((tw...  63.2 us
    pallas_call x1, Pallas kernels, ffn_back(): pl.pallas_call(functools.partial(ffn_back_kernel, cuts), out_shape=[SHAPE...  61.6 us
    pallas_call x1, Pallas kernels, gather_all(): pl.pallas_call(functools.partial(gather_kernel, (0, 768, cols)), out_shap...  52.5 us
    pallas_call x1, Pallas kernels, ffn_in(): pl.pallas_call(functools.partial(ffn_in_kernel, cuts), out_shape=[SHAPE((...  45.8 us
    dot_general x5, matrix products, dot_nt(): lax.dot_general(a, b, (((1,), (1,)), ((), ())), preferred_element_type=F32)  21 us
    dot_general x5, matrix products, dot_nn(): lax.dot_general(a, b, (((1,), (0,)), ((), ())), preferred_element_type=F32)  20.8 us
    pallas_call x1, Pallas kernels, start(): pl.pallas_call(start_kernel, out_shape=[SHAPE(packs.shape, BF16), rows, r...  20 us
    pallas_call x1, Pallas kernels, attn_fwd(): pl.pallas_call(fwd_kernel, grid=(slots,), in_specs=[_cols(0), _cols(2), _...  19.2 us

profile of v2, /device:TPU:1, one launch (start us, length us, event | category | flops | bytes accessed | tf_op | source)
XLA Modules:
  0.0 455.9 jit_solution(8934296265807640800)
XLA Ops:
  9.6 20.0 %start.1 = (bf16[8,16,2432]{2,1,0:T(8,128)(2,1)}, bf16[2,64,1536]{2,1,0:T(8,128)(2,1)}, bf16[2,64,1536]{2,1,0:T(8,128)(2,1)}) custom-call(bf16[8,16,2432]{2,1,0:T(8,128)(2,1)} %fusion.32.packs, bf16[2,64,1536]{2,1,0:T(8,128)(2,1)} %tokens.1, bf16[2,64,1536]{2,1,0:T(8,128)(2,1)} %grad_out.1), custom_call_target="tpu_custom_call" | custom-call | tf_op jit(solution)/shard_map/start/pallas_call | solution.py:619
  31.7 52.5 %gather_all.1 = (bf16[2,8,64,1536]{3,2,1,0:T(8,128)(2,1)}, bf16[2,8,64,1536]{3,2,1,0:T(8,128)(2,1)}, bf16[1536,1408]{1,0:T(8,128)(2,1)}, bf16[256,1536]{1,0:T(8,128)(2,1)}) custom-call(bf16[2,64,1536]{2,1,0:T(8,128)(2,1)} %get-tuple-element.51.x_rows, bf16[2,64,1536]{2,1,0:T(8,128)(2,1)} %get-tuple-element.52.g_rows, bf16[96,1408]{1,0:T(8,128)(2,1)} %slice.240.own), custom_call_target="tpu_custom_call" | custom-call | tf_op jit(solution)/shard_map/gather_all/pallas_call | solution.py:679
  84.2 2.2 slice_convert_fusion.1
  87.5 2.3 convert_reduce_fusion.1
  89.8 2.6 multiply_reduce_fusion.1
  94.7 4.1 fusion.9.q.k.v
  102.7 2.7 mul.226
  105.5 3.2 reduce_sum.84
  112.5 2.4 fusion.25.w
  123.6 19.2 %attn_fwd.1 = (f32[1024,256]{1,0:T(8,128)}, bf16[2,1024,1024]{2,1,0:T(8,128)(2,1)}, bf16[2,3584,128]{2,1,0:T(8,128)(2,1)}, f32[2,1024,128]{2,1,0:T(8,128)}, bf16...) custom-call(bf16[1024,1024]{1,0:T(8,128)(2,1)} %copy-done, ...), custom_call_target="tpu_custom_call" | custom-call | tf_op jit(solution)/shard_map/attn_fwd/pallas_call | solution.py:229
  142.8 4.1 convolution_convert_fusion
  149.1 45.8 %ffn_in.1 = (f32[2,64,1536]{2,1,0:T(8,128)}, bf16[2,8,64,1536]{3,2,1,0:T(8,128)(2,1)}, bf16[1536,1024]{1,0:T(8,128)(2,1)}, bf16[512,1536]{1,0:T(8,128)(2,1)}) custom-call(bf16[2,8,64,1536]{3,2,1,0:T(8,128)(2,1)} %bitcast.122, bf16[2,64,1536]{2,1,0:T(8,128)(2,1)} %get-tuple-element.51.x_rows, f32[1,1536]{1,0:T(1,128)} %reshape.281.gain, ...), custom_call_target="tpu_custom_call" | custom-call | tf_op jit(solution)/shard_map/ffn_in/pallas_call | solution.py:716
  194.9 6.4 %fusion.66 = f32[1024,1024]{1,0:T(8,128)S(1)} fusion(bf16[1024,1536]{1,0:T(8,128)(2,1)} %bitcast.161, bf16[1536,1024]{1,0:T(8,128)(2,1)} %get-tuple-element.59), kind=kOutput, calls=%fused_computation.161 | convolution fusion | flops 3221225472 | bytes 10485760 | tf_op jit(solution)/shard_map/dot_general | solution.py:933
  201.4 2.7 fusion.36
  204.1 3.0 convolution_convert_fusion.5
  207.1 4.9 %convolution_convert_fusion.3 = bf16[1536,1024]{1,0:T(8,128)(2,1)} fusion(bf16[1024,1536]{1,0:T(8,128)(2,1)S(1)} %bitcast.162, f32[1024,512]{1,0:T(8,128)S(1)} %get-tuple-element.198, f32[1024,512]{1,0:T(8,128)S(1)} %get-tuple-element.197), kind=kOutput, calls=%fused_computation.10 | convolution fusion | flops 3224895488 | bytes 10485760 | tf_op jit(solution)/shard_map/dot_general | solution.py:941
  212.1 5.1 %convolution_convert_fusion.4 = bf16[1024,1536]{1,0:T(8,128)(2,1)} fusion(bf16[1536,1024]{1,0:T(8,128)(2,1)S(1)} %copy-done.44, f32[1024,512]{1,0:T(8,128)S(1)} %get-tuple-element.198, f32[1024,512]{1,0:T(8,128)S(1)} %get-tuple-element.197), kind=kOutput, calls=%fused_computation.11 | convolution fusion | flops 3224895488 | bytes 10485760 | tf_op jit(solution)/shard_map/dot_general | solution.py:937
  217.2 61.6 %ffn_back.1 = (f32[2,64,1536]{2,1,0:T(8,128)}, f32[1,1536]{1,0:T(1,128)}, bf16[2,8,64,1536]{3,2,1,0:T(8,128)(2,1)}, bf16[96,1024]{1,0:T(8,128)(2,1)}, f32[32,1536]{1,0:T(8,128)}) custom-call(bf16[2,8,64,1536]{3,2,1,0:T(8,128)(2,1)} %bitcast.130, f32[2,64,1536]{2,1,0:T(8,128)} %get-tuple-element.62.hidden, f32[1,1536]{1,0:T(1,128)} %reshape.281.gain, ...), custom_call_target="tpu_custom_call" | custom-call | tf_op jit(solution)/shard_map/ffn_back/pallas_call | solution.py:776
  278.8 4.2 convolution_convert_fusion.6.d_out
  285.0 17.2 %attn_bwd.1 = (bf16[1024,256]{1,0:T(8,128)(2,1)}, bf16[1024,256]{1,0:T(8,128)(2,1)}, bf16[1024,256]{1,0:T(8,128)(2,1)}, f32[1024,256]{1,0:T(8,128)}, f32[2,1024,1]{2,1,0:T(8,128)}, /*index=5*/f32[2,1,1024]{2,1,0:T(1,128)}) custom-call(bf16[1024,1024]{1,0:T(8,128)(2,1)} %copy-done, bf16[1024,1024]{1,0:T(8,128)(2,1)} %copy-done, bf16[1024,1024]{1,0:T(8,128)(2,1)} %copy-done, ...), custom_call_target="tpu_custom_call" | custom-call | tf_op jit(solution)/shard_map/attn_bwd/pallas_call | solution.py:253
  302.2 2.7 mul.241
  304.9 2.8 mul.242
  307.7 3.2 reduce_sum.85
  313.2 2.2 broadcast_in_dim.99
  315.5 4.5 multiply_reduce_fusion.5
  322.2 5.4 %convolution_convert_fusion.2 = bf16[1536,1024]{0,1:T(8,128)(2,1)} fusion(bf16[1024,1536]{1,0:T(8,128)(2,1)S(1)} %copy-done.2, bf16[1024,256]{1,0:T(8,128)(2,1)S(1)} %fusion.24, bf16[1024,256]{1,0:T(8,128)(2,1)S(1)} %copy-done.50, bf16[1024,256]{1,0:T(8,128)(2,1)S(1)} %copy-done.49, bf16[1024,256]{1,0:T(8,128)(2,1)S(1)} %copy-done.48), kind=kOutput, calls=%fused_computation.9 | convolution fusion | flops 3231186944 | bytes 8388608 | tf_op jit(solution)/shard_map/dot_general | solution.py:941
  327.6 5.4 %fusion.2 = f32[1024,1536]{1,0:T(8,128)} fusion(bf16[1536,1408]{1,0:T(8,128)(2,1)S(1)} %bitcast.134, bf16[1024,256]{1,0:T(8,128)(2,1)S(1)} %fusion.24, bf16[1024,256]{1,0:T(8,128)(2,1)S(1)} %copy-done.50, bf16[1024,256]{1,0:T(8,128)(2,1)S(1)} %copy-done.49, bf16[1024,256]{1,0:T(8,128)(2,1)S(1)} %copy-done.48), kind=kOutput, calls=%fused_computation.15 | convolution fusion | flops 3229614080 | bytes 11534336 | tf_op jit(solution)/shard_map/dot_general | solution.py:937
  334.6 5.8 %multiply_reduce_fusion = (f32[1536]{0:T(1024)S(1)}, bf16[1024,1536]{1,0:T(8,128)(2,1)}) fusion(bf16[1024,1536]{1,0:T(8,128)(2,1)S(1)} %copy-done.2, f32[1024,1536]{1,0:T(8,128)} %fusion.2, bf16[1536,1]{0,1:T(2,128)(2,1)S(1)} %copy.222, bf16[1536,1]{0,1:T(2,128)(2,1)S(1)} %copy.221, f32[2,1024]{1,0:T(2,128)S(1)} %reduce.4, f32[2,1,1024]{2,1,0:T(1,128)S(1)} %copy-done.20, ...), kind=kOutput, calls=%fused_computation.3 | convolution fusion | flops 15751680 | bytes 12619776 | tf_op jit(solution)/shard_map/dot_general | solution.py:937
  347.0 3.8 copy.230
  350.8 5.2 %convolution_convert_fusion.1 = bf16[1024,1536]{1,0:T(8,128)(2,1)} fusion(bf16[1024,512]{1,0:T(8,128)(2,1)} %copy-done.51, bf16[512,1536]{1,0:T(8,128)(2,1)} %get-tuple-element.61), kind=kOutput, calls=%fused_computation.8 | convolution fusion | flops 1612185600 | bytes 5767168 | tf_op jit(solution)/shard_map/dot_general | solution.py:933
  356.6 63.2 %last_sums.1 = (bf16[2,64,1536]{2,1,0:T(8,128)(2,1)}, bf16[2,64,1536]{2,1,0:T(8,128)(2,1)}, bf16[96,1152]{1,0:T(8,128)(2,1)}, bf16[96,256]{1,0:T(8,128)(2,1)}) custom-call(bf16[2,8,64,1536]{3,2,1,0:T(8,128)(2,1)} %bitcast.124, bf16[2,8,64,1536]{3,2,1,0:T(8,128)(2,1)} %bitcast.131, bf16[2,64,1536]{2,1,0:T(8,128)(2,1)} %get-tuple-element.51.x_rows, ...), custom_call_target="tpu_custom_call" | custom-call | tf_op jit(solution)/shard_map/last_sums/pallas_call | solution.py:884
  421.8 18.8 %end.1 = (bf16[8,16,2432]{2,1,0:T(8,128)(2,1)}, bf16[2,64,1536]{2,1,0:T(8,128)(2,1)}, bf16[2,64,1536]{2,1,0:T(8,128)(2,1)}) custom-call(bf16[8,16,2432]{2,1,0:T(8,128)(2,1)} %pad.89.packs, bf16[2,64,1536]{2,1,0:T(8,128)(2,1)} %get-tuple-element.82.out_rows, bf16[2,64,1536]{2,1,0:T(8,128)(2,1)} %get-tuple-element.83.d_rows), custom_call_target="tpu_custom_call" | custom-call | tf_op jit(solution)/shard_map/end/pallas_call | solution.py:921
  (238 shorter events, 64.7 us)
Async XLA Ops:
  0.6 5.8 %copy-start.13 = (bf16[12,4096]{1,0:T(8,128)(2,1)S(1)}, bf16[12,4096]{1,0:T(8,128)(2,1)}, u32[]{:S(2)}) copy-start(bf16[12,4096]{1,0:T(8,128)(2,1)} %param.26) | copy-start | bytes 294916
  0.7 6.1 %copy-start.14 = (bf16[12,4096]{1,0:T(8,128)(2,1)S(1)}, bf16[12,4096]{1,0:T(8,128)(2,1)}, u32[]{:S(2)}) copy-start(bf16[12,4096]{1,0:T(8,128)(2,1)} %param.27) | copy-start | bytes 294916
  84.2 8.3 %copy-start.3 = (bf16[2,8,64,1536]{3,2,1,0:T(8,128)(2,1)S(1)}, bf16[2,8,64,1536]{3,2,1,0:T(8,128)(2,1)}, u32[]{:S(2)}) copy-start(bf16[2,8,64,1536]{3,2,1,0:T(8,128)(2,1)} %get-tuple-element.54) | copy-start | bytes 9437188
  87.4 13.1 %copy-start.29 = (f32[1,256]{1,0:T(1,128)}, f32[1,256]{1,0:T(1,128)S(1)}, u32[]{:S(2)}) copy-start(f32[1,256]{1,0:T(1,128)S(1)} %get-tuple-element.226) | copy-start | bytes 3076
  87.4 13.1 %copy-start.31 = (f32[1,256]{1,0:T(1,128)}, f32[1,256]{1,0:T(1,128)S(1)}, u32[]{:S(2)}) copy-start(f32[1,256]{1,0:T(1,128)S(1)} %get-tuple-element.227) | copy-start | bytes 3076
  87.4 13.1 %copy-start.33 = (f32[1,256]{1,0:T(1,128)}, f32[1,256]{1,0:T(1,128)S(1)}, u32[]{:S(2)}) copy-start(f32[1,256]{1,0:T(1,128)S(1)} %get-tuple-element.228) | copy-start | bytes 3076
  87.5 13.1 %copy-start.35 = (f32[1,256]{1,0:T(1,128)}, f32[1,256]{1,0:T(1,128)S(1)}, u32[]{:S(2)}) copy-start(f32[1,256]{1,0:T(1,128)S(1)} %get-tuple-element.229) | copy-start | bytes 3076
  98.8 6.6 %copy-start = (bf16[1024,1024]{1,0:T(8,128)(2,1)}, bf16[1024,1024]{1,0:T(8,128)(2,1)S(1)}, u32[]{:S(2)}) copy-start(bf16[1024,1024]{1,0:T(8,128)(2,1)S(1)} %fusion.9.q.k.v) | copy-start | bytes 6291460
  98.9 9.8 %copy-start.4 = (f32[1024,256]{1,0:T(8,128)}, f32[1024,256]{1,0:T(8,128)S(1)}, u32[]{:S(2)}) copy-start(f32[1024,256]{1,0:T(8,128)S(1)} %slice_convert_fusion) | copy-start | bytes 3145732
  100.0 8.7 %copy-start.17 = (s32[2,8,128]{2,1,0:T(8,128)}, s32[2,8,128]{2,1,0:T(8,128)S(1)}, u32[]{:S(2)}) copy-start(s32[2,8,128]{2,1,0:T(8,128)S(1)} %broadcast_add_fusion) | copy-start | bytes 24580
  111.4 8.1 %copy-start.2 = (bf16[1024,1536]{1,0:T(8,128)(2,1)S(1)}, bf16[1024,1536]{1,0:T(8,128)(2,1)}, u32[]{:S(2)}) copy-start(bf16[1024,1536]{1,0:T(8,128)(2,1)} %copy-done.1) | copy-start | bytes 9437188
  117.2 5.3 %copy-start.18 = (s32[2,8,128]{2,1,0:T(8,128)S(1)}, s32[2,8,128]{2,1,0:T(8,128)}, u32[]{:S(2)}) copy-start(s32[2,8,128]{2,1,0:T(8,128)} %copy-done.17) | copy-start | bytes 24580
  194.9 6.4 %copy-start.43 = (bf16[2,8,64,1536]{3,2,1,0:T(8,128)(2,1)S(1)}, bf16[2,8,64,1536]{3,2,1,0:T(8,128)(2,1)}, u32[]{:S(2)}) copy-start(bf16[2,8,64,1536]{3,2,1,0:T(8,128)(2,1)} %get-tuple-element.60) | copy-start | bytes 9437188
  194.9 6.4 %copy-start.47 = (bf16[512,1536]{1,0:T(8,128)(2,1)S(1)}, bf16[512,1536]{1,0:T(8,128)(2,1)}, u32[]{:S(2)}) copy-start(bf16[512,1536]{1,0:T(8,128)(2,1)} %get-tuple-element.61) | copy-start | bytes 4718596
  204.1 8.0 %copy-start.51 = (bf16[1024,512]{1,0:T(8,128)(2,1)}, bf16[1024,512]{1,0:T(8,128)(2,1)S(1)}, u32[]{:S(2)}) copy-start(bf16[1024,512]{1,0:T(8,128)(2,1)S(1)} %get-tuple-element.199) | copy-start | bytes 3145732
  207.1 4.9 %copy-start.44 = (bf16[1536,1024]{1,0:T(8,128)(2,1)S(1)}, bf16[1536,1024]{1,0:T(8,128)(2,1)}, u32[]{:S(2)}) copy-start(bf16[1536,1024]{1,0:T(8,128)(2,1)} %get-tuple-element.59) | copy-start | bytes 9437188
  278.8 4.3 copy-start.8
  278.8 4.3 copy-start.46
  304.9 10.5 %copy-start.24 = (pred[1024]{0:T(1024)(128)(4,1)S(1)}, pred[1024]{0:T(1024)(128)(4,1)}, u32[]{:S(2)}) copy-start(pred[1024]{0:T(1024)(128)(4,1)} %copy-done.23) | copy-start | bytes 3076
  304.9 10.5 %copy-start.26 = (pred[1024]{0:T(1024)(128)(4,1)S(1)}, pred[1024]{0:T(1024)(128)(4,1)}, u32[]{:S(2)}) copy-start(pred[1024]{0:T(1024)(128)(4,1)} %copy-done.25) | copy-start | bytes 3076
  304.9 10.5 %copy-start.28 = (pred[1024]{0:T(1024)(128)(4,1)S(1)}, pred[1024]{0:T(1024)(128)(4,1)}, u32[]{:S(2)}) copy-start(pred[1024]{0:T(1024)(128)(4,1)} %copy-done.27) | copy-start | bytes 3076
  315.4 4.5 copy-start.32
  315.5 4.5 copy-start.34
  315.5 4.5 copy-start.36
  320.9 6.8 %slice-start = ((s8[4325376]{0:T(1024)(128)(4,1)}), s8[4194304]{0:T(1024)(128)(4,1)S(1)}, s32[]{:S(2)}) async-start(s8[4325376]{0:T(1024)(128)(4,1)} %bitcast.133), calls=%async_computation | async-start | bytes 8388608
  322.2 5.4 %slice-start.1 = ((s8[4325376]{0:T(1024)(128)(4,1)}), s8[131072]{0:T(1024)(128)(4,1)S(1)}, s32[]{:S(2)}) async-start(s8[4325376]{0:T(1024)(128)(4,1)} %bitcast.133), calls=%async_computation.1 | async-start | bytes 262144
  327.6 6.9 %copy-start.20 = (f32[2,1,1024]{2,1,0:T(1,128)S(1)}, f32[2,1,1024]{2,1,0:T(1,128)}, u32[]{:S(2)}) copy-start(f32[2,1,1024]{2,1,0:T(1,128)} %get-tuple-element.76) | copy-start | bytes 24580
  350.8 5.2 %copy-start.16 = (f32[1536]{0:T(1024)S(1)}, f32[1536]{0:T(1024)}, u32[]{:S(2)}) copy-start(f32[1536]{0:T(1024)} %copy-done.15) | copy-start | bytes 18436
  356.6 63.2 %copy-start.11 = (bf16[96,1024]{1,0:T(8,128)(2,1)S(1)}, bf16[96,1024]{1,0:T(8,128)(2,1)}, u32[]{:S(2)}) copy-start(bf16[96,1024]{1,0:T(8,128)(2,1)} %get-tuple-element.81) | copy-start | bytes 589828
  445.4 8.1 %copy-start.10 = (bf16[2,64,1536]{2,1,0:T(8,128)(2,1)S(1)}, bf16[2,64,1536]{2,1,0:T(8,128)(2,1)}, u32[]{:S(2)}) copy-start(bf16[2,64,1536]{2,1,0:T(8,128)(2,1)} %get-tuple-element.248) | copy-start | bytes 1179652
  446.3 8.0 %copy-start.9 = (bf16[2,64,1536]{2,1,0:T(8,128)(2,1)S(1)}, bf16[2,64,1536]{2,1,0:T(8,128)(2,1)}, u32[]{:S(2)}) copy-start(bf16[2,64,1536]{2,1,0:T(8,128)(2,1)} %get-tuple-element.249) | copy-start | bytes 1179652
  446.4 8.6 %copy-start.12 = (f32[32,1536]{1,0:T(8,128)S(1)}, f32[32,1536]{1,0:T(8,128)}, u32[]{:S(2)}) copy-start(f32[32,1536]{1,0:T(8,128)} %get-tuple-element.261) | copy-start | bytes 589828
  (22 other events, 46.6 us)

commit v3 on v2

--- a/solution.py
+++ b/solution.py
@@ -71,18 +71,43 @@
     return inv
 
 
-def fwd_kernel(q, k, v, w, bcol, brow, dcol, drow, o, probs, qc, t_out, a_out, z_out, m_out, kp_out, s_buf, x_buf, qm_buf):
+def betas_of(raw, head):
+    lane = lax.broadcasted_iota(jnp.int32, raw.shape, 1)
+    return 2.0 * jax.nn.sigmoid(
+        jnp.sum(jnp.where(lane == head + BETA_AT, raw, 0.0), axis=1, keepdims=True)
+    )
+
+
+BETA_AT = 6
+CONV_AT = 2
+TAPS = 4
+
+
+def conv_weights(small, head):
+    part = small[pl.ds(pl.multiple_of(head * HD, HD), HD), :].astype(F32)
+    return part.T[CONV_AT : CONV_AT + TAPS, :]
+
+
+def convolve(path, taps, marks):
+    total = taps[0:1, :] * path
+    for m in range(1, TAPS):
+        total = total + taps[m : m + 1, :] * (pltpu.roll(path, m, 0) * marks[:, m : m + 1])
+    return total
+
+
+def own_blocks(s, q, k, w, bcol, stores):
+    t_out, a_out, z_out, m_out, kp_out, qm_buf, s_buf = stores
     row, col = iota2(0), iota2(1)
     strict, closed = row > col, row >= col
     eye = (row == col).astype(F32)
 
     def group(g, carry):
         sl = [pl.ds(pl.multiple_of((g * GROUP + n) * BLK, BLK), BLK) for n in range(GROUP)]
-        qs = [q[s, :] for s in sl]
-        ks = [k[s, :] for s in sl]
-        ws = [w[s, :] for s in sl]
-        bc = [bcol[0, s, :] for s in sl]
-        br = [brow[0, :, s] for s in sl]
+        qs = [q[r, :] for r in sl]
+        ks = [k[r, :] for r in sl]
+        ws = [w[r, :] for r in sl]
+        bc = [jnp.broadcast_to(bcol[r, :], (BLK, BLK)) for r in sl]
+        br = [b.T for b in bc]
         low = [jnp.where(strict, mm_nt(x, x), 0.0) * b for x, b in zip(ws, br)]
         inv = unit_inverses(low)
         m1 = [jnp.where(strict, mm_nt(x, y), 0.0) for x, y in zip(ws, ks)]
@@ -93,19 +118,21 @@
         qm = [x.astype(F32) - mm(p, y) for x, p, y in zip(qs, a, ws)]
         kmt = [x.astype(F32).T - mm_tn(zz, m) for x, zz, m in zip(ks, z, m1)]
         pm = [eye - mm_tn(zz, x) for zz, x in zip(z, ws)]
-        for n, s in enumerate(sl):
-            b = g * GROUP + n
-            t_out[0, s, :] = inv[n].astype(t_out.dtype)
-            a_out[0, s, :] = a[n].astype(a_out.dtype)
-            z_out[0, s, :] = z[n].astype(z_out.dtype)
-            m_out[0, s, :] = m1[n].astype(m_out.dtype)
-            kp_out[0, s, :HD] = kmt[n].astype(BF16)
-            kp_out[0, s, HD:] = pm[n].astype(BF16)
-            qm_buf[s, :] = qm[n]
-            s_buf[s, s] = sd[n]
+        for n, r in enumerate(sl):
+            t_out[s, r, :] = inv[n].astype(t_out.dtype)
+            a_out[s, r, :] = a[n].astype(a_out.dtype)
+            z_out[s, r, :] = z[n].astype(z_out.dtype)
+            m_out[s, r, :] = m1[n].astype(m_out.dtype)
+            kp_out[s, r, :HD] = kmt[n].astype(BF16)
+            kp_out[s, r, HD:] = pm[n].astype(BF16)
+            qm_buf[r, :] = qm[n]
+            s_buf[r, r] = sd[n]
         return carry
 
     lax.fori_loop(0, NB // GROUP, group, 0)
+
+
+def sweep(s, qc, kp, qm_buf, x_buf, s_buf):
     at = NQC
     for j in range(NB - 2, -1, -1):
         r0 = (j + 1) * BLK
@@ -113,39 +140,83 @@
         x_buf[r0 : r0 + BLK, :] = qm_buf[r0 : r0 + BLK, :]
         x = x_buf[r0:, :].astype(BF16)
         at -= rows
-        qc[0, at : at + rows, :] = x
-        both = mm(x, kp_out[0, j * BLK : r0, :])
+        qc[s, at : at + rows, :] = x
+        both = mm(x, kp[s, j * BLK : r0, :])
         s_buf[r0:, j * BLK : r0] = both[:, :HD]
         x_buf[r0:, :] = both[:, HD:]
+
+
+def weigh(s, v, dcol, drow, s_buf, probs, o):
     for i in range(NB):
         lo, width = i * BLK, (i + 1) * BLK
-        s = s_buf[lo:width, :width] * SCALE
-        seen = dcol[lo:width, :] == drow[:, :width]
+        t = s_buf[lo:width, :width] * SCALE
+        seen = dcol[lo:width, 0:1] == drow[0:1, :width]
         seen = seen & (
             lax.broadcasted_iota(jnp.int32, (BLK, width), 0) + lo
             >= lax.broadcasted_iota(jnp.int32, (BLK, width), 1)
         )
-        s = jnp.where(seen, s, -1e30)
-        e = jnp.exp(s - jnp.max(s, axis=1, keepdims=True))
-        p = e * (1.0 / jnp.sum(e, axis=1, keepdims=True))
-        pb = p.astype(BF16)
-        probs[0, lo:width, :width] = pb
-        o[lo:width, :] = mm(pb, v[:width, :])
-
-
-def bwd_kernel(q, k, v, w, bcol, brow, o, do, probs, qc, t_in, a_in, z_in, m_in, kp, dq, dk, dv, dw, dbc, dbr, ds_buf, x_buf, dkm_buf, dpm_buf, ):
-    row, col = iota2(0), iota2(1)
-    strict, closed = row > col, row >= col
+        t = jnp.where(seen, t, -1e30)
+        e = jnp.exp(t - jnp.max(t, axis=1, keepdims=True))
+        p = (e * (1.0 / jnp.sum(e, axis=1, keepdims=True))).astype(BF16)
+        probs[s, lo:width, :width] = p
+        o[lo:width, :] = mm(p, v[:width, :])
+
+
+def project(x_all, whole, normed, qkvp, raw):
+    rows = 256
+    gain = whole[:, 8 * HD : 9 * HD].astype(F32)
+    gain = jnp.concatenate(
+        [gain[n * HD : (n + 1) * HD, :].T[0:1, :] for n in range(gain.shape[0] // HD)], axis=1
+    )
+
+    def block(i, carry):
+        at = pl.ds(pl.multiple_of(i * rows, rows), rows)
+        x = x_all[at, :].astype(F32)
+        scale = lax.rsqrt(jnp.mean(x * x, axis=1, keepdims=True) + 1e-05)
+        n = (x * scale * gain).astype(BF16)
+        normed[at, :] = n
+        y = mm(n, whole[:, : 9 * HD])
+        qkvp[at, :] = y[:, : 8 * HD].astype(BF16)
+        raw[at, :] = y[:, 8 * HD :]
+        return carry
+
+    lax.fori_loop(0, SEQ // rows, block, 0)
+
+
+def fwd_steps(poke, x_all, whole, marks, drow, normed, qkvp, raw, vec, o, probs, qc, t_out, a_out, z_out, m_out, kp_out, s_buf, x_buf, qm_buf, b_buf):
+    chip, core = lax.axis_index("x"), lax.axis_index("c")
+    project(x_all, whole, normed, qkvp, raw)
+    poke()
+    for s, head in enumerate((3 * chip + 2 * core, 3 * chip + 1)):
+        cols = slice(s * HD, (s + 1) * HD)
+        q, k, v, path = (qkvp.at[:, (2 * n + s) * HD : (2 * n + s + 1) * HD] for n in range(4))
+        taps = conv_weights(whole.at[:, 8 * HD : 9 * HD], head)
+        conved = convolve(path[...].astype(F32), taps, marks[...])
+        unit = conved * lax.rsqrt(jnp.sum(conved * conved, axis=1, keepdims=True) + 1e-06)
+        vec[:, cols] = unit.astype(BF16)
+        b_buf[...] = betas_of(raw[...], head)
+        own_blocks(s, q, k, vec.at[:, cols], b_buf, (t_out, a_out, z_out, m_out, kp_out, qm_buf, s_buf))
+        poke()
+        sweep(s, qc, kp_out, qm_buf, x_buf, s_buf)
+        poke()
+        weigh(s, v, marks, drow, s_buf, probs, o.at[:, cols])
+        poke()
+
+
+def score_grads(s, v, o, do, probs, ds_buf, dv):
     for i in range(NB):
         lo, width = i * BLK, (i + 1) * BLK
-        p = probs[0, lo:width, :width].astype(F32)
+        p = probs[s, lo:width, :width].astype(F32)
         g = do[lo:width, :]
         delta = jnp.sum(g * o[lo:width, :], axis=1, keepdims=True)
         ds = p * (mm_nt(g, v[:width, :]) - delta) * SCALE
         ds_buf[lo:width, :width] = ds.astype(BF16)
     for j in range(NB):
         lo = j * BLK
-        dv[lo : lo + BLK, :] = mm_tn(probs[0, lo:, lo : lo + BLK], do[lo:, :]).astype(dv.dtype)
+        dv[lo : lo + BLK, :] = mm_tn(probs[s, lo:, lo : lo + BLK], do[lo:, :]).astype(dv.dtype)
+
+
+def sweep_back(s, qc, kp, ds_buf, x_buf, dkm_buf, dpm_buf):
     x_buf[...] = jnp.zeros_like(x_buf)
     dkm_buf[SEQ - BLK :, :] = jnp.zeros((BLK, HD), F32)
     dpm_buf[SEQ - BLK :, :] = jnp.zeros((BLK, HD), F32)
@@ -155,31 +226,36 @@
         rows = SEQ - r0
         x = x_buf[r0:, :].astype(BF16)
         ds = ds_buf[r0:, lo:r0]
-        qcj = qc[0, at : at + rows, :]
+        qcj = qc[s, at : at + rows, :]
         at += rows
         both = mm_tn(qcj, jnp.concatenate([x, ds], axis=1))
         dpm_buf[lo:r0, :] = both[:, :HD]
         dkm_buf[lo:r0, :] = both[:, HD:].T
-        kpj = kp[0, lo:r0, :]
-        x_buf[r0:, :] = mm_nt(jnp.concatenate([ds, x], axis=1), kpj)
+        x_buf[r0:, :] = mm_nt(jnp.concatenate([ds, x], axis=1), kp[s, lo:r0, :])
+
+
+def own_blocks_back(s, q, k, w, bcol, saved, bufs, dq, dk, dw, db):
+    t_in, a_in, z_in, m_in = saved
+    ds_buf, x_buf, dkm_buf, dpm_buf = bufs
+    row, col = iota2(0), iota2(1)
+    strict, closed = row > col, row >= col
 
     def group(g, carry):
         sl = [pl.ds(pl.multiple_of((g * GROUP + n) * BLK, BLK), BLK) for n in range(GROUP)]
         rng = range(GROUP)
-        Q = [q[s, :] for s in sl]
-        K = [k[s, :] for s in sl]
-        W = [w[s, :] for s in sl]
-        bc = [bcol[0, s, :] for s in sl]
-        br = [brow[0, :, s] for s in sl]
-        E = [ds_buf[s, s] for s in sl]
-        T = [t_in[0, s, :] for s in sl]
-        A = [a_in[0, s, :] for s in sl]
-        Z = [z_in[0, s, :] for s in sl]
-        M = [m_in[0, s, :] for s in sl]
-        dQm = [x_buf[s, :] for s in sl]
-        dKm = [dkm_buf[s, :] for s in sl]
-        dPm = [dpm_buf[s, :] for s in sl]
-        E = [jnp.where(closed, e, jnp.zeros_like(e)) for e in E]
+        Q = [q[r, :] for r in sl]
+        K = [k[r, :] for r in sl]
+        W = [w[r, :] for r in sl]
+        bc = [jnp.broadcast_to(bcol[r, :], (BLK, BLK)) for r in sl]
+        br = [b.T for b in bc]
+        E = [ds_buf[r, r] for r in sl]
+        T = [t_in[s, r, :] for r in sl]
+        A = [a_in[s, r, :] for r in sl]
+        Z = [z_in[s, r, :] for r in sl]
+        M = [m_in[s, r, :] for r in sl]
+        dQm = [x_buf[r, :] for r in sl]
+        dKm = [dkm_buf[r, :] for r in sl]
+        dPm = [dpm_buf[r, :] for r in sl]
         i1 = [mm_nt(W[n], W[n]) for n in rng]
         qw = [jnp.where(closed, mm_nt(Q[n], W[n]), 0.0) for n in rng]
         dA = [-(mm_nt(E[n], M[n]) + mm_nt(dQm[n], W[n])) for n in rng]
@@ -194,12 +270,13 @@
         dL = [jnp.where(strict, -mm_nt(dL[n], T[n]), 0.0) for n in rng]
         dI = [dL[n] * br[n] for n in rng]
         R = [dG[n] * br[n] for n in rng]
-        for n, s in enumerate(sl):
-            dbr[0, :, s] = jnp.sum(dL[n] * i1[n] + dG[n] * qw[n], axis=0, keepdims=True)
-            dbc[0, s, :] = jnp.sum(dBW[n] * W[n].astype(F32), axis=1, keepdims=True)
-            dq[s, :] = (dQm[n] + mm(E[n], K[n]) + mm(R[n], W[n])).astype(dq.dtype)
-            dk[s, :] = (dKm[n] + mm_tn(E[n], Q[n]) + mm_tn(dM[n], W[n])).astype(dk.dtype)
-            dw[s, :] = (
+        for n, r in enumerate(sl):
+            db[r, :] = jnp.sum(
+                (dL[n] * i1[n] + dG[n] * qw[n]).T + dBW[n] * W[n].astype(F32), axis=1, keepdims=True
+            )
+            dq[r, :] = (dQm[n] + mm(E[n], K[n]) + mm(R[n], W[n])).astype(dq.dtype)
+            dk[r, :] = (dKm[n] + mm_tn(E[n], Q[n]) + mm_tn(dM[n], W[n])).astype(dk.dtype)
+            dw[r, :] = (
                 dW[n]
                 + bc[n] * dBW[n]
                 + mm_tn(R[n], Q[n])
@@ -211,56 +288,86 @@
     lax.fori_loop(0, NB // GROUP, group, 0)
 
 
-def _full(shape):
-    return pl.BlockSpec(shape, lambda s: (0,) * len(shape))
-
-
-def _slot(*shape):
-    return pl.BlockSpec((1,) + shape, lambda s: (s,) + (0,) * len(shape))
-
-
-def _cols(at):
-    return pl.BlockSpec((SEQ, HD), lambda s: (0, at + s))
-
-
-def attn_fwd(qkv, vec, bcol, brow, dcol, drow):
-    slots = bcol.shape[0]
+def bwd_steps(poke, qkvp, raw, small, marks, vec, o, do, probs, qc, t_in, a_in, z_in, m_in, kp, d_ext, d_conv, ds_buf, x_buf, dkm_buf, dpm_buf, b_buf, db_buf, dw_buf):
+    chip, core = lax.axis_index("x"), lax.axis_index("c")
+    lane = lax.broadcasted_iota(jnp.int32, (SEQ, HD), 1)
+    d_raw = jnp.zeros((SEQ, HD), F32)
+    d_conv[...] = jnp.zeros_like(d_conv)
+    for s, head in enumerate((3 * chip + 2 * core, 3 * chip + 1)):
+        cols = slice(s * HD, (s + 1) * HD)
+        q, k, v, path = (qkvp.at[:, (2 * n + s) * HD : (2 * n + s + 1) * HD] for n in range(4))
+        dq, dk, dv, dpath = (d_ext.at[:, (2 * n + s) * HD : (2 * n + s + 1) * HD] for n in range(4))
+        beta = betas_of(raw[...], head)
+        b_buf[...] = beta
+        score_grads(s, v, o.at[:, cols], do.at[:, cols], probs, ds_buf, dv)
+        poke()
+        sweep_back(s, qc, kp, ds_buf, x_buf, dkm_buf, dpm_buf)
+        poke()
+        own_blocks_back(
+            s, q, k, vec.at[:, cols], b_buf, (t_in, a_in, z_in, m_in), (ds_buf, x_buf, dkm_buf, dpm_buf), dq, dk, dw_buf, db_buf
+        )
+        poke()
+        d_raw = d_raw + jnp.where(
+            lane == head + BETA_AT, db_buf[...] * beta * (1.0 - 0.5 * beta), 0.0
+        )
+        taps = conv_weights(small, head)
+        raw_path = path[...].astype(F32)
+        conved = convolve(raw_path, taps, marks[...])
+        scale = lax.rsqrt(jnp.sum(conved * conved, axis=1, keepdims=True) + 1e-06)
+        unit = conved * scale
+        dw = dw_buf[...]
+        d_conved = scale * (dw - unit * jnp.sum(dw * unit, axis=1, keepdims=True))
+        total = taps[0:1, :] * d_conved
+        d_conv[s, 0:1, :] = jnp.sum(d_conved * raw_path, axis=0, keepdims=True)
+        for m in range(1, TAPS):
+            marked = d_conved * marks[:, m : m + 1]
+            d_conv[s, m : m + 1, :] = jnp.sum(
+                marked * pltpu.roll(raw_path, m, 0), axis=0, keepdims=True
+            )
+            total = total + taps[m : m + 1, :] * pltpu.roll(marked, SEQ - m, 0)
+        dpath[...] = total.astype(dpath.dtype)
+    d_ext[:, 8 * HD :] = d_raw.astype(d_ext.dtype)
+
+
+def fwd_shapes(width):
     sds = jax.ShapeDtypeStruct
-    return pl.pallas_call(
-        fwd_kernel,
-        grid=(slots,),
-        in_specs=[_cols(0), _cols(2), _cols(4), _cols(0), _slot(SEQ, 1), _slot(1, SEQ), _full((SEQ, 1)), _full((1, SEQ))],
-        out_specs=[_cols(0), _slot(SEQ, SEQ), _slot(NQC, HD)] + [_slot(SEQ, BLK)] * 4 + [_slot(SEQ, 2 * HD)],
-        out_shape=[
-            sds((SEQ, slots * HD), F32),
-            sds((slots, SEQ, SEQ), BF16),
-            sds((slots, NQC, HD), BF16),
-            sds((slots, SEQ, BLK), F32),
-            sds((slots, SEQ, BLK), BF16),
-            sds((slots, SEQ, BLK), BF16),
-            sds((slots, SEQ, BLK), BF16),
-            sds((slots, SEQ, 2 * HD), BF16),
-        ],
-        scratch_shapes=[pltpu.VMEM((SEQ, SEQ), F32), pltpu.VMEM((SEQ, HD), F32), pltpu.VMEM((SEQ, HD), F32)],
-        compiler_params=pltpu.CompilerParams(vmem_limit_bytes=VM),
-        name="attn_fwd",
-    )(qkv, qkv, qkv, vec, bcol, brow, dcol, drow)
-
-
-def attn_bwd(qkv, vec, bcol, brow, o, do, saved):
-    slots = bcol.shape[0]
+    return [
+        sds((SEQ, width), BF16),
+        sds((SEQ, 8 * HD), BF16),
+        sds((SEQ, HD), F32),
+        sds((SEQ, 2 * HD), BF16),
+        sds((SEQ, 2 * HD), F32),
+        sds((2, SEQ, SEQ), BF16),
+        sds((2, NQC, HD), BF16),
+        sds((2, SEQ, BLK), F32),
+        sds((2, SEQ, BLK), BF16),
+        sds((2, SEQ, BLK), BF16),
+        sds((2, SEQ, BLK), BF16),
+        sds((2, SEQ, 2 * HD), BF16),
+    ]
+
+
+def fwd_scratch():
+    return [
+        pltpu.VMEM((SEQ, SEQ), F32),
+        pltpu.VMEM((SEQ, HD), F32),
+        pltpu.VMEM((SEQ, HD), F32),
+        pltpu.VMEM((SEQ, 1), F32),
+    ]
+
+
+def bwd_shapes():
     sds = jax.ShapeDtypeStruct
-    return pl.pallas_call(
-        bwd_kernel,
-        grid=(slots,),
-        in_specs=[_cols(0), _cols(2), _cols(4), _cols(0), _slot(SEQ, 1), _slot(1, SEQ), _cols(0), _cols(0)]
-        + [_slot(SEQ, SEQ), _slot(NQC, HD)] + [_slot(SEQ, BLK)] * 4 + [_slot(SEQ, 2 * HD)],
-        out_specs=[_cols(0)] * 4 + [_slot(SEQ, 1), _slot(1, SEQ)],
-        out_shape=[sds((SEQ, slots * HD), BF16)] * 3 + [sds((SEQ, slots * HD), F32), sds((slots, SEQ, 1), F32), sds((slots, 1, SEQ), F32)],
-        scratch_shapes=[pltpu.VMEM((SEQ, SEQ), BF16)] + [pltpu.VMEM((SEQ, HD), F32)] * 3,
-        compiler_params=pltpu.CompilerParams(vmem_limit_bytes=VM),
-        name="attn_bwd",
-    )(qkv, qkv, qkv, vec, bcol, brow, o, do, *saved)
+    return [sds((SEQ, 9 * HD), BF16), sds((2, 8, HD), F32)]
+
+
+def bwd_scratch():
+    return (
+        [pltpu.VMEM((SEQ, SEQ), BF16)]
+        + [pltpu.VMEM((SEQ, HD), F32)] * 3
+        + [pltpu.VMEM((SEQ, 1), F32)] * 2
+        + [pltpu.VMEM((SEQ, HD), F32)]
+    )
 
 
 MESH = pl.DeviceIdType.MESH
@@ -346,14 +453,24 @@
     pl.semaphore_wait(barrier, len(devices))
 
 
-def interleave(*jobs):
-    jobs = list(jobs)
-    while jobs:
-        for job in list(jobs):
+class Jobs:
+    def __init__(self, *jobs):
+        self.jobs = list(jobs)
+
+    def poke(self):
+        for job in list(self.jobs):
             try:
                 next(job)
             except StopIteration:
-                jobs.remove(job)
+                self.jobs.remove(job)
+
+    def drain(self):
+        while self.jobs:
+            self.poke()
+
+
+def interleave(*jobs):
+    Jobs(*jobs).drain()
 
 
 def team_peers(p):
@@ -490,6 +607,7 @@
     lo, mid, hi = cuts
     first, second = pl.ds(lo, mid - lo), pl.ds(mid, hi - mid)
     rows = z_sum.shape[1]
+    both = hi > mid
     flat = len(part.shape) == 2
     order = (2, 1, 3)
     a = []
@@ -502,7 +620,8 @@
                 b.append(net.send(part.at[chunk_rows(y, k, rows), second], y_got.at[n, k % 2, k // 2], p.at_y(d)))
         else:
             a.append(net.send(part.at[lax.rem(z, 2), :, z // 2, :, first], z_got.at[n], p.at_z(d)))
-            b.append(net.send(part.at[:, y, :, :, second], y_got.at[n], p.at_y(d)))
+            if both:
+                b.append(net.send(part.at[:, y, :, :, second], y_got.at[n], p.at_y(d)))
 
     def own(y, zl, zh, cols):
         if flat:
@@ -520,19 +639,20 @@
     a = [
         net.send(z_sum.at[lax.rem(p.y + d, 4)], z_last.at[n], p.at_y(d)) for n, d in enumerate(order)
     ]
-    yield
-    for copy in b:
-        copy.wait_recv()
-    for zl in range(2):
-        for zh in range(2):
-            t = own(p.y, zl, zh, second)
-            for n in range(3):
-                t = t + y_got[n, zl, zh].astype(F32)
-            y_sum[zl, zh] = t.astype(BF16)
-    b = []
-    for n, d in enumerate(order):
-        z = lax.rem(p.z + d, 4)
-        b.append(net.send(y_sum.at[lax.rem(z, 2), z // 2], y_last.at[n], p.at_z(d)))
+    if both:
+        yield
+        for copy in b:
+            copy.wait_recv()
+        for zl in range(2):
+            for zh in range(2):
+                t = own(p.y, zl, zh, second)
+                for n in range(3):
+                    t = t + y_got[n, zl, zh].astype(F32)
+                y_sum[zl, zh] = t.astype(BF16)
+        b = []
+        for n, d in enumerate(order):
+            z = lax.rem(p.z + d, 4)
+            b.append(net.send(y_sum.at[lax.rem(z, 2), z // 2], y_last.at[n], p.at_z(d)))
     yield
     for copy in a:
         copy.wait_recv()
@@ -540,13 +660,14 @@
     for n in range(3):
         t = t + z_last[n].astype(F32)
     out[:, first] = t.astype(out.dtype)
-    yield
-    for copy in b:
-        copy.wait_recv()
-    t = y_sum[p.zl, p.zh].astype(F32)
-    for n in range(3):
-        t = t + y_last[n].astype(F32)
-    out[:, second] = t.astype(out.dtype)
+    if both:
+        yield
+        for copy in b:
+            copy.wait_recv()
+        t = y_sum[p.zl, p.zh].astype(F32)
+        for n in range(3):
+            t = t + y_last[n].astype(F32)
+        out[:, second] = t.astype(out.dtype)
 
 
 SCATTER_GROUPS = 12
@@ -554,7 +675,7 @@
 
 
 def scatter_groups_scratch(r, cuts):
-    a, b = cuts[1] - cuts[0], cuts[2] - cuts[1]
+    a, b = cuts[1] - cuts[0], max(cuts[2] - cuts[1], HD)
     return [
         pltpu.VMEM((3, 4, r, a), BF16),
         pltpu.VMEM((4, r, a), BF16),
@@ -631,7 +752,7 @@
     return pl.ds(pl.multiple_of(at * HD, HD), HD)
 
 
-OUT_AT = 8
+OUT_AT = 9
 
 
 def trade_out(net, whole, w_out):
@@ -658,36 +779,62 @@
         copy.wait_recv()
 
 
-def gather_kernel(cuts, x_rows, g_rows, own, x_all, g_all, whole, w_out, *sem):
+def gather_kernel(cuts, x_rows, own, x_all, whole, *sem):
     net = Net(*sem)
     p = net.place
-    meet(team_all(p) + group_peers(p))
-    interleave(
-        gather_team(net, x_rows, x_all),
-        gather_groups(net, own, whole, cuts),
-        gather_team(net, g_rows, g_all),
-    )
-    net.settle()
-    interleave(trade_out(net, whole, w_out))
+    meet(team_peers(p) + group_peers(p))
+    interleave(gather_team(net, x_rows, x_all), gather_groups(net, own, whole, cuts))
     net.finish()
 
 
-def gather_all(x_rows, g_rows, own):
+def gather_all(x_rows, own):
     rows, cols = own.shape
     two, n, width = x_rows.shape
-    every = SHAPE((two, 8, n, width), BF16)
     return pl.pallas_call(
         functools.partial(gather_kernel, (0, 768, cols)),
-        out_shape=[every, every, SHAPE((16 * rows, cols), BF16), SHAPE((2 * HD, width), BF16)],
-        in_specs=[ANY] * 3,
-        out_specs=[ANY] * 4,
-        scratch_shapes=sems(2 * GATHER_TEAM + GATHER_GROUPS + 21, 6),
+        out_shape=[SHAPE((two, 8, n, width), BF16), SHAPE((16 * rows, cols), BF16)],
+        in_specs=[ANY] * 2,
+        out_specs=[ANY] * 2,
+        scratch_shapes=sems(GATHER_TEAM + GATHER_GROUPS, 2),
         compiler_params=params(2),
         name="gather_all",
-    )(x_rows, g_rows, own)
-
-
-def ffn_in_kernel(cuts, part, x_rows, gain, own_ffn, own_down, hidden, ffn_all, w_ffn, w_down, normed, *rest):
+    )(x_rows, own)
+
+
+def attn_fwd_kernel(cuts, x_all, whole, marks, drow, own_ffn, g_rows, *rest):
+    kept, rest = rest[:12], rest[12:]
+    w_ffn, g_all, w_out, rest = rest[0], rest[1], rest[2], rest[3:]
+    net = Net(*rest[-3:])
+    p = net.place
+    meet(team_all(p) + group_peers(p))
+    jobs = Jobs(
+        gather_groups(net, own_ffn, w_ffn, cuts),
+        trade_out(net, whole, w_out),
+        gather_team(net, g_rows, g_all),
+    )
+    jobs.poke()
+    fwd_steps(jobs.poke, x_all, whole, marks, drow, *kept, *rest[:-3])
+    jobs.drain()
+    net.finish()
+
+
+def attn_fwd(x_all, whole, marks, drow, own_ffn, g_rows):
+    rows, cols = own_ffn.shape
+    two, n, width = g_rows.shape
+    kept = fwd_shapes(width)
+    return pl.pallas_call(
+        functools.partial(attn_fwd_kernel, (0, cols // 2, cols)),
+        out_shape=kept
+        + [SHAPE((16 * rows, cols), BF16), SHAPE((two, 8, n, width), BF16), SHAPE((2 * HD, width), BF16)],
+        in_specs=[VMEM] * 4 + [ANY] * 2,
+        out_specs=[VMEM] * len(kept) + [ANY] * 3,
+        scratch_shapes=fwd_scratch() + sems(GATHER_TEAM + GATHER_GROUPS + 21, 5),
+        compiler_params=params(7),
+        name="attn_fwd",
+    )(x_all, whole, marks, drow, own_ffn, g_rows)
+
+
+def ffn_in_kernel(cuts, part, x_rows, gain, own_down, hidden, ffn_all, w_down, normed, *rest):
     net = Net(*rest[-3:])
     p = net.place
     meet(team_peers(p) + group_peers(p))
@@ -702,33 +849,27 @@
         yield from scatter_team(net, part, *rest[:-3], finish)
         yield from gather_team(net, normed, ffn_all)
 
-    interleave(
-        team(),
-        gather_groups(net, own_ffn, w_ffn, cuts[0]),
-        gather_groups(net, own_down, w_down, cuts[1]),
-    )
+    interleave(team(), gather_groups(net, own_down, w_down, cuts))
     net.finish()
 
 
-def ffn_in(part, x_rows, gain, own_ffn, own_down):
+def ffn_in(part, x_rows, gain, own_down):
     two, n, width = x_rows.shape
-    cuts = [(0, a.shape[1] // 2, a.shape[1]) for a in (own_ffn, own_down)]
     return pl.pallas_call(
-        functools.partial(ffn_in_kernel, cuts),
+        functools.partial(ffn_in_kernel, (0, width // 2, width)),
         out_shape=[
             SHAPE((two, n, width), F32),
             SHAPE((two, 8, n, width), BF16),
-            SHAPE((16 * own_ffn.shape[0], own_ffn.shape[1]), BF16),
-            SHAPE((16 * own_down.shape[0], own_down.shape[1]), BF16),
+            SHAPE((16 * own_down.shape[0], width), BF16),
         ],
-        in_specs=[VMEM, VMEM, VMEM, ANY, ANY],
-        out_specs=[VMEM, ANY, ANY, ANY],
+        in_specs=[VMEM, VMEM, VMEM, ANY],
+        out_specs=[VMEM, ANY, ANY],
         scratch_shapes=[pltpu.VMEM((two, n, width), BF16)]
         + scatter_team_scratch(n, width)
-        + sems(SCATTER_TEAM + GATHER_TEAM + 2 * GATHER_GROUPS, 3),
+        + sems(SCATTER_TEAM + GATHER_TEAM + GATHER_GROUPS, 2),
         compiler_params=params(3),
         name="ffn_in",
-    )(part, x_rows, gain, own_ffn, own_down)
+    )(part, x_rows, gain, own_down)
 
 
 def norm_back(v, gain, d_normed):
@@ -739,8 +880,8 @@
     return d_v, d_normed * unit
 
 
-def ffn_back_kernel(cuts, part, hidden, gain, g_rows, d_ffn, d_down, d_hidden, d_gain, branch_all, ffn_sum, down_sum, branch, *rest):
-    team_scratch, ffn_scratch, down_scratch = rest[:6], rest[6:12], rest[12:18]
+def ffn_back_kernel(cuts, part, hidden, gain, g_rows, d_down, d_hidden, d_gain, branch_all, down_sum, branch, *rest):
+    team_scratch, down_scratch = rest[:6], rest[6:12]
     net = Net(*rest[-3:])
     p = net.place
     meet(team_peers(p) + group_peers(p))
@@ -756,11 +897,7 @@
         yield from scatter_team(net, part, *team_scratch, finish)
         yield from gather_team(net, branch, branch_all)
 
-    interleave(
-        team(),
-        scatter_groups(net, d_ffn, ffn_sum, cuts[0], *ffn_scratch),
-        scatter_groups(net, d_down, down_sum, cuts[1], *down_scratch),
-    )
+    interleave(team(), scatter_groups(net, d_down, down_sum, cuts, *down_scratch))
     net.finish()
 
 
@@ -768,30 +905,28 @@
     return a.reshape(2, 4, 2, a.shape[0] // 16, a.shape[1])
 
 
-def ffn_back(part, hidden, gain, g_rows, d_ffn, d_down):
+def ffn_back(part, hidden, gain, g_rows, d_down):
     two, n, width = hidden.shape
-    d_ffn, d_down = by_group(d_ffn), by_group(d_down)
-    sizes = [a.shape[3:] for a in (d_ffn, d_down)]
-    cuts = [(0, w // 2, w) for _, w in sizes]
+    d_down = by_group(d_down)
+    rows = d_down.shape[3]
+    cuts = (0, width // 2, width)
     return pl.pallas_call(
         functools.partial(ffn_back_kernel, cuts),
         out_shape=[
             SHAPE((two, n, width), F32),
             SHAPE((1, width), F32),
             SHAPE((two, 8, n, width), BF16),
-            SHAPE(sizes[0], BF16),
-            SHAPE(sizes[1], F32),
+            SHAPE((rows, width), F32),
         ],
-        in_specs=[VMEM] * 6,
-        out_specs=[VMEM, VMEM, ANY, VMEM, VMEM],
+        in_specs=[VMEM] * 5,
+        out_specs=[VMEM, VMEM, ANY, VMEM],
         scratch_shapes=[pltpu.VMEM((two, n, width), BF16)]
         + scatter_team_scratch(n, width)
-        + scatter_groups_scratch(sizes[0][0], cuts[0])
-        + scatter_groups_scratch(sizes[1][0], cuts[1])
-        + sems(SCATTER_TEAM + GATHER_TEAM + 2 * SCATTER_GROUPS, 1),
+        + scatter_groups_scratch(rows, cuts)
+        + sems(SCATTER_TEAM + GATHER_TEAM + SCATTER_GROUPS, 1),
         compiler_params=params(4),
         name="ffn_back",
-    )(part, hidden, gain, g_rows, d_ffn, d_down)
+    )(part, hidden, gain, g_rows, d_down)
 
 
 def trade_out_back(net, d_out, whole):
@@ -850,55 +985,92 @@
 TRADE_BACK = 28
 
 
-def last_kernel(cuts, part_n, part_o, x_rows, hidden, d_hidden, gain, d_heads, d_out, out_rows, d_rows, heads_sum, out_sum, whole, *rest):
-    n_scratch, o_scratch, h_scratch, w_scratch = rest[:6], rest[6:12], rest[12:18], rest[18:24]
-    net = Net(*rest[-3:])
+def attn_bwd_kernel(cuts, *refs):
+    given, refs = refs[:14], refs[14:]
+    d_ffn, part_o, hidden, d_out, refs = *refs[:4], refs[4:]
+    results, refs = refs[:2], refs[2:]
+    out_rows, ffn_sum, out_sum, whole, refs = *refs[:4], refs[4:]
+    bufs, o_scratch, f_scratch, w_scratch = refs[:7], refs[7:13], refs[13:19], refs[19:25]
+    net = Net(*refs[-3:])
     p = net.place
     meet(team_all(p) + group_peers(p))
 
-    def finish_n(d_normed):
-        d_x, _ = norm_back(x_rows[...].astype(F32), gain[...][None], d_normed)
-        d_rows[...] = (d_x + d_hidden[...]).astype(BF16)
-
-    def finish_o(branch):
+    def finish(branch):
         out_rows[...] = (hidden[...] + branch).astype(BF16)
 
     def out_grad():
         yield from trade_out_back(net, d_out, whole)
         yield from scatter_groups(net, whole, out_sum, cuts[1], *w_scratch)
 
+    jobs = Jobs(
+        scatter_groups(net, d_ffn, ffn_sum, cuts[0], *f_scratch),
+        scatter_team(net, part_o, *o_scratch, finish),
+        out_grad(),
+    )
+    jobs.poke()
+    bwd_steps(jobs.poke, *given, *results, *bufs)
+    jobs.drain()
+    net.finish()
+
+
+def attn_bwd(given, d_ffn, part_o, hidden, d_out):
+    two, n, width = hidden.shape
+    d_ffn = by_group(d_ffn)
+    r, w = d_ffn.shape[3:]
+    cuts = [(0, w // 2, w), (0, HD, 2 * HD)]
+    results = bwd_shapes()
+    return pl.pallas_call(
+        functools.partial(attn_bwd_kernel, cuts),
+        out_shape=results
+        + [SHAPE((two, n, width), BF16), SHAPE((r, w), BF16), SHAPE((r, 2 * HD), BF16)],
+        in_specs=[VMEM] * (len(given) + 4),
+        out_specs=[VMEM] * (len(results) + 3),
+        scratch_shapes=[pltpu.VMEM((width, 2 * HD), BF16)]
+        + bwd_scratch()
+        + scatter_team_scratch(n, width)
+        + scatter_groups_scratch(r, cuts[0])
+        + scatter_groups_scratch(r, cuts[1])
+        + sems(SCATTER_TEAM + SCATTER_GROUPS + SCATTER_GROUPS_FLAT + TRADE_BACK, 4),
+        compiler_params=params(8),
+        name="attn_bwd",
+    )(*given, d_ffn, part_o, hidden, d_out)
+
+
+def last_kernel(cuts, part_n, x_rows, d_hidden, gain, d_heads, d_small, d_rows, heads_sum, small_sum, *rest):
+    n_scratch, h_scratch, s_scratch = rest[:6], rest[6:12], rest[12:18]
+    net = Net(*rest[-3:])
+    p = net.place
+    meet(team_peers(p) + group_peers(p))
+
+    def finish(d_normed):
+        d_x, _ = norm_back(x_rows[...].astype(F32), gain[...][None], d_normed)
+        d_rows[...] = (d_x + d_hidden[...]).astype(BF16)
+
     interleave(
-        out_grad(),
         scatter_groups(net, d_heads, heads_sum, cuts[0], *h_scratch),
-        scatter_team(net, part_n, *n_scratch, finish_n),
-        scatter_team(net, part_o, *o_scratch, finish_o),
+        scatter_groups(net, d_small, small_sum, cuts[1], *s_scratch),
+        scatter_team(net, part_n, *n_scratch, finish),
     )
     net.finish()
 
 
-def last_sums(part_n, part_o, x_rows, hidden, d_hidden, gain, d_heads, d_out):
-    two, n, width = hidden.shape
-    d_heads = by_group(d_heads)
+def last_sums(part_n, x_rows, d_hidden, gain, d_heads, d_small):
+    two, n, width = d_hidden.shape
+    d_heads, d_small = by_group(d_heads), by_group(d_small)
     r, w = d_heads.shape[3:]
-    cuts = [(0, 640, w), (0, HD, 2 * HD)]
+    cuts = [(0, w // 2, w), (0, HD, HD)]
     return pl.pallas_call(
         functools.partial(last_kernel, cuts),
-        out_shape=[
-            SHAPE((two, n, width), BF16),
-            SHAPE((two, n, width), BF16),
-            SHAPE((r, w), BF16),
-            SHAPE((r, 2 * HD), BF16),
-        ],
-        in_specs=[VMEM] * 8,
-        out_specs=[VMEM] * 4,
-        scratch_shapes=[pltpu.VMEM((width, 2 * HD), BF16)]
-        + scatter_team_scratch(n, width) * 2
+        out_shape=[SHAPE((two, n, width), BF16), SHAPE((r, w), BF16), SHAPE((r, HD), BF16)],
+        in_specs=[VMEM] * 6,
+        out_specs=[VMEM] * 3,
+        scratch_shapes=scatter_team_scratch(n, width)
         + scatter_groups_scratch(r, cuts[0])
         + scatter_groups_scratch(r, cuts[1])
-        + sems(2 * SCATTER_TEAM + SCATTER_GROUPS + SCATTER_GROUPS_FLAT + TRADE_BACK, 4),
+        + sems(SCATTER_TEAM + 2 * SCATTER_GROUPS, 0),
         compiler_params=params(5),
         name="last_sums",
-    )(part_n, part_o, x_rows, hidden, d_hidden, gain, d_heads, d_out)
+    )(part_n, x_rows, d_hidden, gain, d_heads, d_small)
 
 
 def end_kernel(packs, out_rows, d_rows, got, output, d_tokens, *sem):
@@ -939,22 +1111,6 @@
 
 def dot_tn(a, b):
     return lax.dot_general(a, b, (((0,), (0,)), ((), ())), preferred_element_type=F32)
-
-
-def rms_scale(values, gain_vec):
-    return (
-        values * lax.rsqrt(jnp.mean(values * values, axis=-1, keepdims=True) + EPS_NORM) * gain_vec
-    )
-
-
-def path_vectors(current, conv_w, same_doc):
-    conved = conv_w[0] * current
-    for tap in range(1, conv_w.shape[0]):
-        earlier = jnp.pad(current, ((tap, 0), (0, 0)))[: current.shape[0]]
-        conved = conved + conv_w[tap] * jnp.where(same_doc[tap][:, None], earlier, 0.0)
-    heads = conved.reshape(current.shape[0], -1, HD)
-    unit = heads * lax.rsqrt(jnp.sum(heads * heads, axis=-1, keepdims=True) + EPS_UNIT)
-    return unit.reshape(current.shape)
 
 
 def split_rows(partial):
@@ -1001,58 +1157,34 @@
     heads_pack = heads_pack.reshape(8, share, -1)
     ffn_pack = jnp.stack([w_gate, w_up], axis=1).reshape(share, 2, 16, 8, 32)
     ffn_pack = ffn_pack.transpose(3, 0, 1, 2, 4).reshape(8, share, -1)
-    packs = pad_rows(jnp.concatenate([heads_pack, small, ffn_pack], axis=2), 16)
+    packs = pad_rows(
+        jnp.concatenate([heads_pack[:, :, :HEADS_W], small, heads_pack[:, :, HEADS_W:], ffn_pack], axis=2), 16
+    )
     packs, x_rows, g_rows = start(packs, tokens, grad_out)
     packs = packs[:, :share].reshape(8 * share, -1)
     first_w = HEADS_W + OUT_W + SMALL_W
-    x_all, g_all, whole, w_out_t = gather_all(x_rows, g_rows, packs[:, :first_w])
-    w_heads = whole[:, :HEADS_W]
-    small = whole[:, HEADS_W + OUT_W :]
-    gain_a, gain_f = small[:, 0].astype(F32), small[:, 1].astype(F32)
-    conv_full, beta_full = small[:, 2:6].T.astype(F32), small[:, 6:18]
-    x_all = x_all.reshape(SEQ, width)
-    g_all = g_all.reshape(SEQ, width)
+    x_all, whole = gather_all(x_rows, packs[:, :first_w])
+    w_ext = whole[:, : HEADS_W + SMALL_W]
+    gain_a, gain_f = (whole[:, HEADS_W + n].astype(F32) for n in range(2))
     doc_rows = jnp.cumsum(doc_start, axis=1)
-    docs = jnp.where(zh == 0, doc_rows[0], doc_rows[1])
-
-    def two_heads(full, size):
-        return jnp.concatenate(
-            [
-                lax.dynamic_slice_in_dim(full, head_a * size, size, 1),
-                lax.dynamic_slice_in_dim(full, head_b * size, size, 1),
-            ],
-            axis=1,
-        )
-
-    def back_to_all(part, size):
-        full = jnp.zeros((part.shape[0], 12 * size), F32)
-        full = lax.dynamic_update_slice_in_dim(full, part[:, :size], head_a * size, 1)
-        own_b = jnp.where(owns_b, part[:, size:], 0.0)
-        return lax.dynamic_update_slice_in_dim(full, own_b, head_b * size, 1)
+    docs = jnp.where(zh == 0, doc_rows[0], doc_rows[1]).astype(F32)
+    marks = [docs]
+    for tap in range(1, TAPS):
+        same = docs[: SEQ - tap] == docs[tap:]
+        marks.append(jnp.concatenate([jnp.zeros((tap,), F32), same.astype(F32)]))
+    drow = jnp.stack(marks + marks)
+    marks = drow.T
 
     def own_heads(v):
         return jnp.where((jnp.arange(2 * HD) < HD) | owns_b, v, 0.0)
 
-    w_beta_t = two_heads(beta_full, 1)
-    conv_t = two_heads(conv_full, HD)
-    same_doc = [
-        jnp.concatenate([jnp.zeros((tap,), bool), docs[: SEQ - tap] == docs[tap:]])
-        for tap in range(4)
-    ]
-
-    normed_all = rms_scale(x_all.astype(F32), gain_a).astype(BF16)
-    qkvp = dot_nn(normed_all, w_heads).astype(BF16)
-    beta_raw = dot_nn(normed_all, w_beta_t)
-    betas = (2.0 * jax.nn.sigmoid(beta_raw)).T
-    vec_f, vec_pull = jax.vjp(
-        lambda cur, cw: path_vectors(cur, cw, same_doc), qkvp[:, 6 * HD :].astype(F32), conv_t
-    )
-    vec = vec_f.astype(BF16)
-    bcol, brow = betas[:, :, None], betas[:, None, :]
-    o, *saved = attn_fwd(qkvp, vec, bcol, brow, docs[:, None], docs[None, :])
+    normed_all, qkvp, raw, vec, o, *saved, w_ffn, g_all, w_out_t = attn_fwd(
+        x_all.reshape(SEQ, width), whole, marks, drow, packs[:, first_w:], g_rows
+    )
+    g_all = g_all.reshape(SEQ, width)
     mixed = own_heads(o).astype(BF16)
-    hidden, ffn_all, w_ffn, w_down_t = ffn_in(
-        split_rows(dot_nn(mixed, w_out_t)), x_rows, gain_f[None], packs[:, first_w:], w_down
+    hidden, ffn_all, w_down_t = ffn_in(
+        split_rows(dot_nn(mixed, w_out_t)), x_rows, gain_f[None], w_down
     )
     ffn_all = ffn_all.reshape(SEQ, width)
     gate_up = dot_nn(ffn_all, w_ffn)
@@ -1067,58 +1199,46 @@
 
     (d_gate_up,) = act_pull(dot_nt(g_all, w_down_t))
     d_gate_up = d_gate_up.astype(BF16)
-    d_hidden, d_gain_ffn, branch_all, d_ffn, d_down = ffn_back(
+    d_hidden, d_gain_ffn, branch_all, d_down = ffn_back(
         split_rows(dot_nt(d_gate_up, w_ffn)),
         hidden,
         gain_f[None],
         g_rows,
-        dot_tn(ffn_all, d_gate_up).astype(BF16),
         dot_tn(act, g_all).astype(BF16),
     )
+    d_ffn = dot_tn(ffn_all, d_gate_up).astype(BF16)
     branch_all = branch_all.reshape(SEQ, width)
     d_mixed = own_heads(dot_nt(branch_all, w_out_t))
-    d_q, d_k, d_v, d_vec, d_bc, d_br = attn_bwd(qkvp, vec, bcol, brow, o, d_mixed, saved)
-    d_path, d_conv = vec_pull(d_vec)
-    d_betas = (d_bc[:, :, 0] + d_br[:, 0, :]) * betas * (1.0 - 0.5 * betas)
-    d_beta = d_betas.T.astype(BF16)
-    d_qkvp = jnp.concatenate([d_q, d_k, d_v, d_path.astype(BF16)], axis=1)
-    norm_part = (dot_nt(d_qkvp, w_heads) + dot_nt(d_beta, w_beta_t)).astype(BF16)
+    d_out = dot_tn(mixed, branch_all).astype(BF16)
+    d_ext, d_conv, out_rows, ffn_sum, out_sum = attn_bwd(
+        (qkvp, raw, w_ext[:, HEADS_W:], marks, vec, o, d_mixed, *saved), d_ffn, out_part, hidden, d_out
+    )
+    norm_part = dot_nt(d_ext, w_ext).astype(BF16)
     d_gain_attn = jnp.sum(norm_part.astype(F32) * normed_all.astype(F32), axis=0) / gain_a
 
-    small_back = jnp.concatenate(
-        [
-            d_gain_attn[:, None],
-            d_gain_ffn.T,
-            back_to_all(d_conv, HD).T,
-            back_to_all(dot_tn(normed_all, d_beta), 1),
-        ],
-        axis=1,
-    ).astype(BF16)
+    d_heads = dot_tn(normed_all, d_ext[:, :HEADS_W]).astype(BF16)
+    conv_rows = jnp.zeros((width, TAPS), F32)
+    conv_rows = lax.dynamic_update_slice_in_dim(conv_rows, d_conv[1, :TAPS].T, head_b * HD, 0)
+    conv_rows = lax.dynamic_update_slice_in_dim(conv_rows, d_conv[0, :TAPS].T, head_a * HD, 0)
+    small_back = jnp.concatenate([d_gain_attn[:, None], d_gain_ffn.T, conv_rows], axis=1)
     small_back = jnp.pad(small_back, ((0, 0), (0, SMALL_W - small_back.shape[1])))
-    d_heads = dot_tn(normed_all, d_qkvp).astype(BF16)
-    out_rows, d_rows, heads_sum, out_sum = last_sums(
-        split_rows(norm_part),
-        out_part,
-        x_rows,
-        hidden,
-        d_hidden,
-        gain_a[None],
-        jnp.concatenate([d_heads, small_back], axis=1),
-        dot_tn(mixed, branch_all).astype(BF16),
-    )
-    packs = jnp.concatenate([heads_sum, out_sum, d_ffn], axis=1).reshape(8, share, -1)
+    d_small = (dot_tn(normed_all, d_ext[:, HEADS_W:]) + small_back).astype(BF16)
+    d_rows, heads_sum, small_sum = last_sums(
+        split_rows(norm_part), x_rows, d_hidden, gain_a[None], d_heads, d_small
+    )
+    packs = jnp.concatenate([heads_sum, small_sum, out_sum, ffn_sum], axis=1).reshape(8, share, -1)
     packs, output, d_tokens = end(pad_rows(packs, 16), out_rows, d_rows)
     packs = packs[:, :share]
-    small = jnp.sum(packs[:, :, HEADS_W : HEADS_W + SMALL_W].astype(F32), axis=0)
     at = HEADS_W + SMALL_W
+    small = jnp.sum(packs[:, :, HEADS_W:at].astype(F32), axis=0)
     heads_back = jnp.concatenate([packs[:, :, :HEADS_W], packs[:, :, at : at + OUT_W]], axis=2)
     heads_back = heads_back.reshape(4, 2, share, 5, 2, HD)
     by_head = jnp.stack(
         [heads_back[:, 0, :, :, 0], heads_back[:, 0, :, :, 1], heads_back[:, 1, :, :, 0]], axis=1
     )
     by_kind = by_head.transpose(3, 2, 0, 1, 4).reshape(5, share, width).astype(F32)
-    ffn_sum = packs[:, :, at + OUT_W :].reshape(8, share, 2, 16, 32)
-    ffn_sum = ffn_sum.transpose(2, 1, 3, 0, 4).reshape(2, share, -1).astype(F32)
+    ffn_back_w = packs[:, :, at + OUT_W :].reshape(8, share, 2, 16, 32)
+    ffn_back_w = ffn_back_w.transpose(2, 1, 3, 0, 4).reshape(2, share, -1).astype(F32)
     return (
         output,
         d_tokens,
@@ -1131,8 +1251,8 @@
         small[:, 6:18],
         by_kind[4],
         small[:, 1],
-        ffn_sum[0],
-        ffn_sum[1],
+        ffn_back_w[0],
+        ffn_back_w[1],
         d_down,
     )
 

time: 463 us -> 420 us (0.907)
  other arithmetic: 39.1 us -> 9.39 us
  local copies, waits for them, and re-layouts: 56.1 us -> 28.9 us
  Pallas kernels: 298 us -> 322 us
  matrix products: 60.6 us -> 52.6 us
    pallas_call x3, Pallas kernels: 82.1 us -> 157 us  [the longest x1 58.7 us: attn_fwd(): pl.pallas_call(functools.partial(attn_fwd_kernel, (0, cols // 2, cols)),...]
    pallas_call x1, Pallas kernels: 63.2 us -> 44.5 us  [last_sums(): pl.pallas_call(functools.partial(last_kernel, cuts), out_shape=[SHAPE((tw...]
    pallas_call x1, Pallas kernels: 61.6 us -> 43.2 us  [ffn_back(): pl.pallas_call(functools.partial(ffn_back_kernel, cuts), out_shape=[SHAPE...]
    pallas_call x1, Pallas kernels: 52.5 us -> 38.5 us  [gather_all(): pl.pallas_call(functools.partial(gather_kernel, (0, 768, cols)), out_shap...]
    reduce_sum x5 -> x1, other arithmetic: 14.3 us -> 0.77 us  [per_device(): small = jnp.sum(packs[:, :, HEADS_W:at].astype(F32), axis=0)]
    mul x4 -> x0, local copies, waits for them, and re-layouts: 7.79 us -> none  [the longest x2 4.01 us: path_vectors(): heads * lax.rsqrt(jnp.sum(heads * heads, axis=-1, keepdims=True) + EPS_UNIT)]
    dot_general x5 -> x3, matrix products: 20.8 us -> 13 us  [dot_nn(): lax.dot_general(a, b, (((1,), (0,)), ((), ())), preferred_element_type=F32)]
    convert_element_type x7 -> x4, other arithmetic: 9.31 us -> 2.8 us  [the longest x1 1.69 us: per_device(): gain_a, gain_f = (whole[:, HEADS_W + n].astype(F32) for n in range(2))]
where the time goes in v3:
time: 420 us; the launch traced here: 415 us
  Pallas kernels  322 us (77%)
  matrix products  52.6 us (13%)
  local copies, waits for them, and re-layouts  28.9 us (7%)
  other arithmetic  9.39 us (2%)
    pallas_call x1, Pallas kernels, attn_fwd(): pl.pallas_call(functools.partial(attn_fwd_kernel, (0, cols // 2, cols)),...  58.7 us
    pallas_call x1, Pallas kernels, attn_bwd(): pl.pallas_call(functools.partial(attn_bwd_kernel, cuts), out_shape=result...  57.1 us
    pallas_call x1, Pallas kernels, last_sums(): pl.pallas_call(functools.partial(last_kernel, cuts), out_shape=[SHAPE((tw...  44.5 us
    pallas_call x1, Pallas kernels, ffn_back(): pl.pallas_call(functools.partial(ffn_back_kernel, cuts), out_shape=[SHAPE...  43.2 us
    pallas_call x1, Pallas kernels, ffn_in(): pl.pallas_call(functools.partial(ffn_in_kernel, (0, width // 2, width)),...  41.5 us
    pallas_call x1, Pallas kernels, gather_all(): pl.pallas_call(functools.partial(gather_kernel, (0, 768, cols)), out_shap...  38.5 us
    dot_general x5, matrix products, dot_tn(): lax.dot_general(a, b, (((0,), (0,)), ((), ())), preferred_element_type=F32)  21.2 us
    pallas_call x1, Pallas kernels, start(): pl.pallas_call(start_kernel, out_shape=[SHAPE(packs.shape, BF16), rows, r...  20 us

profile of v3, /device:TPU:1, one launch (start us, length us, event | category | flops | bytes accessed | tf_op | source)
XLA Modules:
  0.0 415.0 jit_solution(9160564224954394794)
XLA Ops:
  8.7 1.0 fusion.12.packs
  9.7 20.0 %start.1 = (bf16[8,16,2432]{2,1,0:T(8,128)(2,1)}, bf16[2,64,1536]{2,1,0:T(8,128)(2,1)}, bf16[2,64,1536]{2,1,0:T(8,128)(2,1)}) custom-call(bf16[8,16,2432]{2,1,0:T(8,128)(2,1)} %fusion.12.packs, bf16[2,64,1536]{2,1,0:T(8,128)(2,1)} %tokens.1, bf16[2,64,1536]{2,1,0:T(8,128)(2,1)} %grad_out.1), custom_call_target="tpu_custom_call" | custom-call | tf_op jit(solution)/shard_map/start/pallas_call | solution.py:740
  29.7 1.2 reshape.184
  31.6 38.5 %gather_all.1 = (bf16[2,8,64,1536]{3,2,1,0:T(8,128)(2,1)}, bf16[1536,1408]{1,0:T(8,128)(2,1)}) custom-call(bf16[2,64,1536]{2,1,0:T(8,128)(2,1)} %get-tuple-element.52.x_rows, bf16[96,1408]{1,0:T(8,128)(2,1)} %slice.207.own), custom_call_target="tpu_custom_call" | custom-call | tf_op jit(solution)/shard_map/gather_all/pallas_call | solution.py:793
  72.0 1.0 copy.230
  73.7 58.7 %attn_fwd.1 = (bf16[1024,1536]{1,0:T(8,128)(2,1)}, bf16[1024,1024]{1,0:T(8,128)(2,1)}, f32[1024,128]{1,0:T(8,128)}, bf16[1024,256]{1,0:T(8,128)(2,1)}, f32[1024,...) custom-call(bf16[1024,1536]{1,0:T(8,128)(2,1)} %bitcast.89, ...), custom_call_target="tpu_custom_call" | custom-call | tf_op jit(solution)/shard_map/attn_fwd/pallas_call | solution.py:825
  132.5 4.1 convolution_convert_fusion
  136.6 1.7 convert_reduce_fusion
  138.9 41.5 %ffn_in.1 = (f32[2,64,1536]{2,1,0:T(8,128)}, bf16[2,8,64,1536]{3,2,1,0:T(8,128)(2,1)}, bf16[512,1536]{1,0:T(8,128)(2,1)}) custom-call(bf16[2,8,64,1536]{3,2,1,0:T(8,128)(2,1)} %bitcast.85, bf16[2,64,1536]{2,1,0:T(8,128)(2,1)} %get-tuple-element.52.x_rows, f32[1,1536]{1,0:T(1,128)} %reshape.204.gain, bf16[32,1536]{1,0:T(8,128)(2,1)} %own_down.1), custom_call_target="tpu_custom_call" | custom-call | tf_op jit(solution)/shard_map/ffn_in/pallas_call | solution.py:858
  180.4 5.4 %fusion.31 = f32[1024,1024]{1,0:T(8,128)S(1)} fusion(bf16[1024,1536]{1,0:T(8,128)(2,1)} %bitcast.117, bf16[1536,1024]{1,0:T(8,128)(2,1)S(1)} %copy-done.19), kind=kOutput, calls=%fused_computation.91 | convolution fusion | flops 3221225472 | bytes 10485760 | tf_op jit(solution)/shard_map/dot_general | solution.py:1105
  185.9 2.6 fusion.14
  188.5 3.0 convolution_convert_fusion.6
  191.5 5.1 %convolution_convert_fusion.4 = bf16[1024,1536]{1,0:T(8,128)(2,1)} fusion(bf16[1536,1024]{1,0:T(8,128)(2,1)S(1)} %copy-done.19, f32[1024,512]{1,0:T(8,128)S(1)} %get-tuple-element.193, f32[1024,512]{1,0:T(8,128)S(1)} %get-tuple-element.192), kind=kOutput, calls=%fused_computation.6 | convolution fusion | flops 3224895488 | bytes 10485760 | tf_op jit(solution)/shard_map/dot_general | solution.py:1109
  196.7 43.2 %ffn_back.1 = (f32[2,64,1536]{2,1,0:T(8,128)}, f32[1,1536]{1,0:T(1,128)}, bf16[2,8,64,1536]{3,2,1,0:T(8,128)(2,1)}, f32[32,1536]{1,0:T(8,128)}) custom-call(bf16[2,8,64,1536]{3,2,1,0:T(8,128)(2,1)} %bitcast.90, f32[2,64,1536]{2,1,0:T(8,128)} %get-tuple-element.66.hidden.refs_16_, f32[1,1536]{1,0:T(1,128)} %reshape.204.gain, ...), custom_call_target="tpu_custom_call" | custom-call | tf_op jit(solution)/shard_map/ffn_back/pallas_call | solution.py:913
  239.9 3.9 convolution_convert_fusion.7.refs_17_
  243.9 3.5 convolution_convert_fusion.1
  247.9 5.0 %convolution_convert_fusion.3 = bf16[1536,1024]{1,0:T(8,128)(2,1)} fusion(bf16[1024,1536]{1,0:T(8,128)(2,1)S(1)} %bitcast.118, f32[1024,512]{1,0:T(8,128)S(1)} %copy-done.31, f32[1024,512]{1,0:T(8,128)S(1)} %copy-done.29), kind=kOutput, calls=%fused_computation.5 | convolution fusion | flops 3224895488 | bytes 10485760 | tf_op jit(solution)/shard_map/dot_general | solution.py:1113
  252.9 2.0 convolution_select_fusion.refs_6_
  254.9 1.8 slice.174.refs_2_
  256.6 57.1 %attn_bwd.1 = (bf16[1024,1152]{1,0:T(8,128)(2,1)}, f32[2,8,128]{2,1,0:T(8,128)}, bf16[2,64,1536]{2,1,0:T(8,128)(2,1)}, bf16[96,1024]{1,0:T(8,128)(2,1)}, bf16[96,256]{1,0:T(8,128)(2,1)}) custom-call(bf16[1024,1024]{1,0:T(8,128)(2,1)} %get-tuple-element.57.refs_0_, f32[1024,128]{1,0:T(8,128)} %get-tuple-element.58.refs_1_, bf16[1536,128]{1,0:T(8,128)(2,1)} %slice.174.refs_2_, ...), custom_call_target="tpu_custom_call" | custom-call | tf_op jit(solution)/shard_map/attn_bwd/pallas_call | solution.py:1022
  313.8 8.6 %multiply_reduce_fusion = (f32[1536]{0:T(1024)S(1)}, bf16[1024,1536]{1,0:T(8,128)(2,1)}) fusion(bf16[1024,1536]{1,0:T(8,128)(2,1)S(1)} %copy-done.17, bf16[1024,1152]{1,0:T(8,128)(2,1)} %get-tuple-element.75, bf16[1536,1408]{1,0:T(8,128)(2,1)} %get-tuple-element.55.whole), kind=kOutput, calls=%fused_computation | convolution fusion | flops 3631741440 | bytes 12195840 | tf_op jit(solution)/shard_map/dot_general | solution.py:1109
  322.4 1.3 convert_divide_fusion
  324.4 4.1 fusion.1
  328.5 5.2 %convolution_convert_fusion.2 = bf16[1536,1024]{1,0:T(8,128)(2,1)} fusion(bf16[1024,1536]{1,0:T(8,128)(2,1)S(1)} %copy-done.18, bf16[1024,1152]{1,0:T(8,128)(2,1)S(1)} %copy-done.23), kind=kOutput, calls=%fused_computation.4 | convolution fusion | flops 3222798336 | bytes 8388608 | tf_op jit(solution)/shard_map/dot_general | solution.py:1113
  334.3 44.5 %last_sums.1 = (bf16[2,64,1536]{2,1,0:T(8,128)(2,1)}, bf16[96,1024]{1,0:T(8,128)(2,1)}, bf16[96,128]{1,0:T(8,128)(2,1)}) custom-call(bf16[2,8,64,1536]{3,2,1,0:T(8,128)(2,1)} %bitcast.91, bf16[2,64,1536]{2,1,0:T(8,128)(2,1)} %get-tuple-element.52.x_rows, f32[2,64,1536]{2,1,0:T(8,128)} %get-tuple-element.76.d_hidden, f32[1,1536]{1,0:T(1,128)} %reshape.205.gain, ...), custom_call_target="tpu_custom_call" | custom-call | tf_op jit(solution)/shard_map/last_sums/pallas_call | solution.py:1062
  378.9 1.0 pad_maximum_fusion
  380.0 0.9 pad.30.packs
  380.9 18.5 %end.1 = (bf16[8,16,2432]{2,1,0:T(8,128)(2,1)}, bf16[2,64,1536]{2,1,0:T(8,128)(2,1)}, bf16[2,64,1536]{2,1,0:T(8,128)(2,1)}) custom-call(bf16[8,16,2432]{2,1,0:T(8,128)(2,1)} %pad.30.packs, bf16[2,64,1536]{2,1,0:T(8,128)(2,1)} %get-tuple-element.84.out_rows, bf16[2,64,1536]{2,1,0:T(8,128)(2,1)} %get-tuple-element.85.d_rows), custom_call_target="tpu_custom_call" | custom-call | tf_op jit(solution)/shard_map/end/pallas_call | solution.py:1093
  399.4 1.1 slice_convert_fusion
  401.7 1.1 squeeze.46
  403.1 1.1 squeeze.47
  404.1 0.9 slice.187
  (152 shorter events, 24.4 us)
Async XLA Ops:
  0.6 5.8 %copy-start.7 = (bf16[12,4096]{1,0:T(8,128)(2,1)S(1)}, bf16[12,4096]{1,0:T(8,128)(2,1)}, u32[]{:S(2)}) copy-start(bf16[12,4096]{1,0:T(8,128)(2,1)} %param.26) | copy-start | bytes 294916
  0.7 6.2 %copy-start.8 = (bf16[12,4096]{1,0:T(8,128)(2,1)S(1)}, bf16[12,4096]{1,0:T(8,128)(2,1)}, u32[]{:S(2)}) copy-start(bf16[12,4096]{1,0:T(8,128)(2,1)} %param.27) | copy-start | bytes 294916
  6.4 1.9 copy-start.14
  6.4 2.0 copy-start.15
  6.4 2.1 copy-start.16
  6.4 2.2 copy-start.12
  7.3 62.8 %copy-start.10 = (s32[2,1024]{1,0:T(2,128)S(1)}, s32[2,1024]{1,0:T(2,128)}, u32[]{:S(2)}) copy-start(s32[2,1024]{1,0:T(2,128)} %param.16) | copy-start | bytes 24580
  72.0 1.7 copy-start.4
  136.6 43.8 %copy-start.19 = (bf16[1536,1024]{1,0:T(8,128)(2,1)S(1)}, bf16[1536,1024]{1,0:T(8,128)(2,1)}, u32[]{:S(2)}) copy-start(bf16[1536,1024]{1,0:T(8,128)(2,1)} %get-tuple-element.63) | copy-start | bytes 9437188
  180.4 5.5 %copy-start.20 = (bf16[2,8,64,1536]{3,2,1,0:T(8,128)(2,1)S(1)}, bf16[2,8,64,1536]{3,2,1,0:T(8,128)(2,1)}, u32[]{:S(2)}) copy-start(bf16[2,8,64,1536]{3,2,1,0:T(8,128)(2,1)} %get-tuple-element.64) | copy-start | bytes 9437188
  180.4 5.5 %copy-start.24 = (bf16[512,1536]{1,0:T(8,128)(2,1)S(1)}, bf16[512,1536]{1,0:T(8,128)(2,1)}, u32[]{:S(2)}) copy-start(bf16[512,1536]{1,0:T(8,128)(2,1)} %get-tuple-element.65) | copy-start | bytes 4718596
  188.5 3.0 copy-start.26
  188.5 8.1 %copy-start.28 = (f32[1024,512]{1,0:T(8,128)}, f32[1024,512]{1,0:T(8,128)S(1)}, u32[]{:S(2)}) copy-start(f32[1024,512]{1,0:T(8,128)S(1)} %get-tuple-element.192) | copy-start | bytes 6291460
  188.5 8.1 %copy-start.30 = (f32[1024,512]{1,0:T(8,128)}, f32[1024,512]{1,0:T(8,128)S(1)}, u32[]{:S(2)}) copy-start(f32[1024,512]{1,0:T(8,128)S(1)} %get-tuple-element.193) | copy-start | bytes 6291460
  196.7 43.3 %copy-start = (f32[1024,256]{1,0:T(8,128)S(1)}, f32[1024,256]{1,0:T(8,128)}, u32[]{:S(2)}) copy-start(f32[1024,256]{1,0:T(8,128)} %get-tuple-element.60.refs_5_) | copy-start | bytes 3145732
  239.9 4.0 copy-start.25
  239.9 4.0 copy-start.27
  243.9 3.5 copy-start.21
  243.9 3.5 copy-start.29
  243.9 4.0 copy-start.31
  247.9 5.0 %copy-start.1 = (bf16[256,1536]{1,0:T(8,128)(2,1)S(1)}, bf16[256,1536]{1,0:T(8,128)(2,1)}, u32[]{:S(2)}) copy-start(bf16[256,1536]{1,0:T(8,128)(2,1)} %get-tuple-element.61) | copy-start | bytes 2359300
  247.9 5.0 %copy-start.22 = (bf16[2,8,64,1536]{3,2,1,0:T(8,128)(2,1)S(1)}, bf16[2,8,64,1536]{3,2,1,0:T(8,128)(2,1)}, u32[]{:S(2)}) copy-start(bf16[2,8,64,1536]{3,2,1,0:T(8,128)(2,1)} %get-tuple-element.67) | copy-start | bytes 9437188
  256.6 57.1 %copy-start.17 = (bf16[1024,1536]{1,0:T(8,128)(2,1)S(1)}, bf16[1024,1536]{1,0:T(8,128)(2,1)}, u32[]{:S(2)}) copy-start(bf16[1024,1536]{1,0:T(8,128)(2,1)} %get-tuple-element.77) | copy-start | bytes 9437188
  313.8 9.9 %copy-start.13 = (f32[2,8,128]{2,1,0:T(8,128)S(1)}, f32[2,8,128]{2,1,0:T(8,128)}, u32[]{:S(2)}) copy-start(f32[2,8,128]{2,1,0:T(8,128)} %get-tuple-element.79) | copy-start | bytes 24580
  313.8 10.3 %copy-start.11 = (f32[1,1536]{1,0:T(1,128)S(1)}, f32[1,1536]{1,0:T(1,128)}, u32[]{:S(2)}) copy-start(f32[1,1536]{1,0:T(1,128)} %get-tuple-element.78) | copy-start | bytes 18436
  324.3 4.2 %copy-start.18 = (bf16[1024,1536]{1,0:T(8,128)(2,1)S(1)}, bf16[1024,1536]{1,0:T(8,128)(2,1)}, u32[]{:S(2)}) copy-start(bf16[1024,1536]{1,0:T(8,128)(2,1)} %get-tuple-element.77) | copy-start | bytes 9437188
  324.4 4.1 copy-start.23
  334.3 44.6 %copy-start.5 = (bf16[96,1024]{1,0:T(8,128)(2,1)S(1)}, bf16[96,1024]{1,0:T(8,128)(2,1)}, u32[]{:S(2)}) copy-start(bf16[96,1024]{1,0:T(8,128)(2,1)} %get-tuple-element.83) | copy-start | bytes 589828
  334.3 44.6 %copy-start.9 = (bf16[96,256]{1,0:T(8,128)(2,1)S(1)}, bf16[96,256]{1,0:T(8,128)(2,1)}, u32[]{:S(2)}) copy-start(bf16[96,256]{1,0:T(8,128)(2,1)} %get-tuple-element.82) | copy-start | bytes 147460
  404.1 8.1 %copy-start.3 = (bf16[2,64,1536]{2,1,0:T(8,128)(2,1)S(1)}, bf16[2,64,1536]{2,1,0:T(8,128)(2,1)}, u32[]{:S(2)}) copy-start(bf16[2,64,1536]{2,1,0:T(8,128)(2,1)} %get-tuple-element.230) | copy-start | bytes 1179652
  405.0 8.0 %copy-start.2 = (bf16[2,64,1536]{2,1,0:T(8,128)(2,1)S(1)}, bf16[2,64,1536]{2,1,0:T(8,128)(2,1)}, u32[]{:S(2)}) copy-start(bf16[2,64,1536]{2,1,0:T(8,128)(2,1)} %get-tuple-element.231) | copy-start | bytes 1179652
  405.2 8.6 %copy-start.6 = (f32[32,1536]{1,0:T(8,128)S(1)}, f32[32,1536]{1,0:T(8,128)}, u32[]{:S(2)}) copy-start(f32[32,1536]{1,0:T(8,128)} %get-tuple-element.243) | copy-start | bytes 589828
